TPU v7x, 768 devices: a whole 4x8x12 slice. The times are simulated.
768 devices in a mesh: ab: 48 (over z_lo, x, core), cd: 16 (over y, z_hi).
Axes of the slice: x: 4, y: 8, z: 12 (z_hi: 2, z_lo: 6; z = z_hi * 6 + z_lo), core: 2. Of those that a mesh axis runs over, the one named last changes fastest.
Arguments:
- integrals: bfloat16 [73728, 20480], P('ab', 'cd'), may hold values from -0.3125 to 0.3125
- tile_mask: int32 [288, 80], P('ab', 'cd'), may hold values 0 or 1
- virt_irrep: int32 [1000], replicated, may hold values from 0 to 7
- occ_pairs: int32 [2, 288], replicated, may hold values from 0 to 99
- virt_energy: float32 [1000], replicated, may hold values from 0.3 to 3
- occ_energy: float32 [100], replicated, may hold values from -2 to -0.5
- amp_ab: bfloat16 [288, 73728], P('cd', 'ab'), may hold values from -8 to 8
- amp_cd: bfloat16 [288, 20480], P('ab', 'cd'), may hold values from -8 to 8
Outputs:
- update_ab: float32 [288, 73728], P('cd', 'ab')
- update_cd: float32 [288, 20480], P('ab', 'cd')
All inputs are finite; a program needn't handle non-finite values. No bound on the sum of `tile_mask` on one device may be relied on, other than what follows from the above.
Results may differ from a plain program's by a relative error of at most 0.0003.
Values may be sent and summed in bfloat16 or wider, within the bound.
No kernel may reach another device: no remote copies, remote signals or barrier semaphores. Data moves between devices by JAX's collectives and lax.ppermute only.
A program may use at most 32 MiB of HBM per device.

v0:
```python
import jax
import jax.numpy as jnp
from jax import lax
from jax.sharding import PartitionSpec as P

NV = 1000
TILE = 256


def lookup(index, table):
    equal = index[:, None] == jnp.arange(table.shape[0], dtype=jnp.int32)[None, :]
    return jnp.sum(jnp.where(equal, table[None, :], jnp.zeros_like(table)[None, :]), axis=1)


def pair_data(first, count, virt_irrep, virt_energy):
    index = first + jnp.arange(count, dtype=jnp.int32)
    left = index // NV
    right = index % NV
    irreps = jnp.bitwise_xor(lookup(left, virt_irrep), lookup(right, virt_irrep))
    energy = lookup(left, virt_energy) + lookup(right, virt_energy)
    return (irreps, energy)


def occ_sums(occ_pairs, occ_energy, first, count):
    left = lax.dynamic_slice_in_dim(occ_pairs[0], first, count, 0)
    right = lax.dynamic_slice_in_dim(occ_pairs[1], first, count, 0)
    return lookup(left, occ_energy) + lookup(right, occ_energy)


def local(integrals, tile_mask, virt_irrep, occ_pairs, virt_energy, occ_energy, amp_ab, amp_cd):
    rows_dev = integrals.shape[0]
    cols_dev = integrals.shape[1]
    row_group = lax.axis_index("ab")
    col_group = lax.axis_index("cd")
    nab = rows_dev * lax.axis_size("ab")
    row_first = row_group * rows_dev
    col_first = nab + col_group * cols_dev
    row_irrep, row_energy = pair_data(row_first, rows_dev, virt_irrep, virt_energy)
    col_irrep, col_energy = pair_data(col_first, cols_dev, virt_irrep, virt_energy)
    tiles = jnp.repeat(jnp.repeat(tile_mask, TILE, axis=0), TILE, axis=1)
    keep = (tiles == 1) & (row_irrep[:, None] == col_irrep[None, :])
    masked = jnp.where(keep, integrals, jnp.zeros_like(integrals))
    partial_ab = lax.dot_general(
        lax.all_gather(amp_cd, "ab", axis=0, tiled=True),
        masked,
        (((1,), (1,)), ((), ())),
        preferred_element_type=jnp.float32,
    )
    partial_cd = jnp.dot(
        lax.all_gather(amp_ab, "cd", axis=0, tiled=True), masked, preferred_element_type=jnp.float32
    )
    ladder_ab = lax.psum_scatter(partial_ab, "cd", scatter_dimension=0, tiled=True)
    ladder_cd = lax.psum_scatter(partial_cd, "ab", scatter_dimension=0, tiled=True)
    ab_count = ladder_ab.shape[0]
    cd_count = ladder_cd.shape[0]
    occ_ab = occ_sums(occ_pairs, occ_energy, col_group * ab_count, ab_count)
    occ_cd = occ_sums(occ_pairs, occ_energy, row_group * cd_count, cd_count)
    update_ab = ladder_ab / (row_energy[None, :] - occ_ab[:, None])
    update_cd = ladder_cd / (col_energy[None, :] - occ_cd[:, None])
    return (update_ab, update_cd)


def solution(mesh):
    return jax.shard_map(
        local,
        mesh=mesh,
        in_specs=(P("ab", "cd"), P("ab", "cd"), P(), P(), P(), P(), P("cd", "ab"), P("ab", "cd")),
        out_specs=(P("cd", "ab"), P("ab", "cd")),
        check_vma=False,
    )
```

profile of v0, /device:TPU:1, one launch (start us, length us, event | category | flops | bytes accessed | tf_op | source)
XLA Modules:
  0.0 594.6 jit_solution(1599873670296923960)
XLA Ops:
  0.7 6.3 %copy.15 = bf16[1536,1280]{0,1:T(8,128)(2,1)} copy(bf16[1536,1280]{1,0:T(8,128)(2,1)} %param.8) | data formatting | bytes 7864320 | tf_op args[0]
  7.0 0.1 copy.14
  7.1 0.1 broadcast_bitcast_fusion
  7.2 115.8 %all-gather.1 = bf16[16,18,1536]{2,1,0:T(8,128)(2,1)S(1)} all-gather(bf16[1,18,1536]{2,1,0:T(8,128)(2,1)S(1)} %bitcast.33), channel_id=1, replica_groups=mesh['ab'=48,'cd'=16] {'cd'}, dimensions={0}, use_global_device_ids=true | all-gather | bytes 940032 | tf_op jit(solution)/shard_map/all_gather | solution.py:50
  123.1 0.3 reshape.94
  123.4 2.1 select_reduce_fusion.2
  125.5 1.2 select_reduce_fusion.6
  126.7 3.8 fusion.2
  130.6 1.9 copy-done
  132.5 1.3 convolution_bitcast_fusion.1
  133.8 164.7 %fusion.1 = f32[8,1280]{1,0:T(8,128)S(1)} fusion(f32[288,1280]{1,0:T(8,128)S(1)} %convolution_bitcast_fusion.1), kind=kCustom, calls=%all-reduce-scatter.1 | all-reduce-scatter fusion | flops 491521 | bytes 1519616
  298.5 1.3 collective-permute-start.14
  299.8 1.3 collective-permute-start.13
  301.1 1.3 collective-permute-start.12
  302.4 1.3 collective-permute-start.11
  303.7 1.3 collective-permute-start.15
  305.0 2.2 select_reduce_fusion
  307.2 1.7 select_reduce_fusion.4
  308.9 83.1 %all-gather = bf16[48,6,1280]{2,1,0:T(8,128)(2,1)S(1)} all-gather(bf16[1,6,1280]{2,1,0:T(8,128)(2,1)S(1)} %bitcast.35), channel_id=1, replica_groups=mesh['ab'=48,'cd'=16] {'ab'}, dimensions={0}, use_global_device_ids=true | all-gather | bytes 752640 | tf_op jit(solution)/shard_map/all_gather | solution.py:44
  392.0 0.2 reshape.92
  392.2 0.0 copy-start.6
  392.2 0.0 copy-start.7
  392.2 3.4 convolution_bitcast_fusion
  395.7 152.5 %fusion = f32[24,1536]{1,0:T(8,128)S(1)} fusion(f32[288,1536]{1,0:T(8,128)S(1)} %convolution_bitcast_fusion), kind=kCustom, calls=%all-reduce-scatter | all-reduce-scatter fusion | flops 589825 | bytes 1921024
  548.1 0.1 fusion.15
  548.2 0.2 select_reduce_fusion.8
  548.4 1.3 collective-permute-start.10
  549.7 0.0 collective-permute-done.14
  549.7 1.3 collective-permute-start.9
  551.0 0.1 fusion.13
  551.1 1.6 collective-permute-start.8
  552.7 3.7 collective-permute-start.7
  556.4 4.4 collective-permute-start.6
  560.9 1.3 collective-permute-start.5
  562.2 2.5 collective-permute-start.4
  564.7 0.2 select_reduce_fusion.10
  564.9 1.3 dynamic-slice.10
  566.2 1.3 dynamic-slice.14
  568.8 8.1 %collective-permute-start.2 = (f32[24,1536]{1,0:T(8,128)S(1)}, f32[24,1536]{1,0:T(8,128)S(1)}, u32[]{:S(2)}, u32[]{:S(2)}) collective-permute-start(f32[24,1536]{1,0:T(8,128)S(1)} %fusion), channel_id=1, source_target_pairs={{0,3},{1,4},{2,5},{3,6},{4,7},{5,8},{6,9},{7,10},{8,11},{9,12},{10... | collective-permute-start | bytes 442376
  577.0 1.8 collective-permute-start.1
  578.7 5.3 collective-permute-start
  584.0 3.3 collective-permute-start.3
  587.3 1.4 concatenate.1
  588.7 0.7 dynamic-slice_divide_fusion.1
  589.4 3.2 collective-permute-done.3
  592.7 0.4 collective-permute-done
  593.1 0.7 concatenate
  593.8 0.8 dynamic-slice_divide_fusion
  (39 shorter events, 0.2 us)
Async XLA Ops:
  0.6 6.4 %copy-start.5 = (s32[6,5]{1,0:T(8,128)S(1)}, s32[6,5]{1,0:T(8,128)}, u32[]{:S(2)}) copy-start(s32[6,5]{1,0:T(8,128)} %param.9) | copy-start | bytes 364
  0.6 6.6 %copy-start.1 = (bf16[18,1536]{1,0:T(8,128)(2,1)S(1)}, bf16[18,1536]{1,0:T(8,128)(2,1)}, u32[]{:S(2)}) copy-start(bf16[18,1536]{1,0:T(8,128)(2,1)} %param.14) | copy-start | bytes 165892
  0.7 122.7 %copy-start.3 = (s32[1000]{0:T(1024)S(1)}, s32[1000]{0:T(1024)}, u32[]{:S(2)}) copy-start(s32[1000]{0:T(1024)} %param.10) | copy-start | bytes 12004
  130.6 1.9 copy-start
  132.5 172.6 %copy-start.4 = (f32[1000]{0:T(1024)S(1)}, f32[1000]{0:T(1024)}, u32[]{:S(2)}) copy-start(f32[1000]{0:T(1024)} %param.12) | copy-start | bytes 12004
  132.5 176.4 %copy-start.2 = (bf16[6,1280]{1,0:T(8,128)(2,1)S(1)}, bf16[6,1280]{1,0:T(8,128)(2,1)}, u32[]{:S(2)}) copy-start(bf16[6,1280]{1,0:T(8,128)(2,1)} %param.15) | copy-start | bytes 46084
  298.5 251.2 %collective-permute-start.14 = (f32[8,1280]{1,0:T(8,128)S(1)}, f32[8,1280]{1,0:T(8,128)S(1)}, u32[]{:S(2)}, u32[]{:S(2)}) collective-permute-start(f32[8,1280]{1,0:T(8,128)S(1)} %fusion.1), channel_id=1, source_target_pairs={{0,176},{16,192},{32,208},{48,224},{64,240},{80,256},{96,272},{112... | collective-permute-start | bytes 122888
  299.8 251.3 %collective-permute-start.13 = (f32[8,1280]{1,0:T(8,128)S(1)}, f32[8,1280]{1,0:T(8,128)S(1)}, u32[]{:S(2)}, u32[]{:S(2)}) collective-permute-start(f32[8,1280]{1,0:T(8,128)S(1)} %fusion.1), channel_id=1, source_target_pairs={{0,160},{16,176},{32,192},{48,208},{64,224},{80,240},{96,256},{112... | collective-permute-start | bytes 122888
  301.1 251.6 %collective-permute-start.12 = (f32[8,1280]{1,0:T(8,128)S(1)}, f32[8,1280]{1,0:T(8,128)S(1)}, u32[]{:S(2)}, u32[]{:S(2)}) collective-permute-start(f32[8,1280]{1,0:T(8,128)S(1)} %fusion.1), channel_id=1, source_target_pairs={{0,144},{16,160},{32,176},{48,192},{64,208},{80,224},{96,240},{112... | collective-permute-start | bytes 122888
  302.4 254.0 %collective-permute-start.11 = (f32[8,1280]{1,0:T(8,128)S(1)}, f32[8,1280]{1,0:T(8,128)S(1)}, u32[]{:S(2)}, u32[]{:S(2)}) collective-permute-start(f32[8,1280]{1,0:T(8,128)S(1)} %fusion.1), channel_id=1, source_target_pairs={{0,128},{16,144},{32,160},{48,176},{64,192},{80,208},{96,224},{112... | collective-permute-start | bytes 122888
  303.7 244.7 %collective-permute-start.15 = (f32[6,1280]{1,0:T(8,128)S(1)}, f32[6,1280]{1,0:T(8,128)S(1)}, u32[]{:S(2)}, u32[]{:S(2)}) collective-permute-start(f32[6,1280]{1,0:T(8,128)S(1)} %slice.11), channel_id=1, source_target_pairs={{0,192},{16,208},{32,224},{48,240},{64,256},{80,272},{96,288},{112... | collective-permute-start | bytes 92168
  392.2 155.9 %copy-start.6 = (s32[2,288]{1,0:T(2,128)S(1)}, s32[2,288]{1,0:T(2,128)}, u32[]{:S(2)}) copy-start(s32[2,288]{1,0:T(2,128)} %param.11) | copy-start | bytes 6916
  392.2 156.0 %copy-start.7 = (f32[100]{0:T(128)S(1)}, f32[100]{0:T(128)}, u32[]{:S(2)}) copy-start(f32[100]{0:T(128)} %param.13) | copy-start | bytes 1204
  548.4 12.4 %collective-permute-start.10 = (f32[8,1280]{1,0:T(8,128)S(1)}, f32[8,1280]{1,0:T(8,128)S(1)}, u32[]{:S(2)}, u32[]{:S(2)}) collective-permute-start(f32[8,1280]{1,0:T(8,128)S(1)} %fusion.1), channel_id=1, source_target_pairs={{0,112},{16,128},{32,144},{48,160},{64,176},{80,192},{96,208},{112... | collective-permute-start | bytes 122888
  549.7 12.4 %collective-permute-start.9 = (f32[8,1280]{1,0:T(8,128)S(1)}, f32[8,1280]{1,0:T(8,128)S(1)}, u32[]{:S(2)}, u32[]{:S(2)}) collective-permute-start(f32[8,1280]{1,0:T(8,128)S(1)} %fusion.1), channel_id=1, source_target_pairs={{0,96},{16,112},{32,128},{48,144},{64,160},{80,176},{96,192},{112,... | collective-permute-start | bytes 122888
  551.1 17.7 %collective-permute-start.8 = (f32[8,1280]{1,0:T(8,128)S(1)}, f32[8,1280]{1,0:T(8,128)S(1)}, u32[]{:S(2)}, u32[]{:S(2)}) collective-permute-start(f32[8,1280]{1,0:T(8,128)S(1)} %fusion.1), channel_id=1, source_target_pairs={{0,80},{16,96},{32,112},{48,128},{64,144},{80,160},{96,176},{112,1... | collective-permute-start | bytes 122888
  552.7 24.2 %collective-permute-start.7 = (f32[8,1280]{1,0:T(8,128)S(1)}, f32[8,1280]{1,0:T(8,128)S(1)}, u32[]{:S(2)}, u32[]{:S(2)}) collective-permute-start(f32[8,1280]{1,0:T(8,128)S(1)} %fusion.1), channel_id=1, source_target_pairs={{0,64},{16,80},{32,96},{48,112},{64,128},{80,144},{96,160},{112,17... | collective-permute-start | bytes 122888
  556.4 22.3 %collective-permute-start.6 = (f32[8,1280]{1,0:T(8,128)S(1)}, f32[8,1280]{1,0:T(8,128)S(1)}, u32[]{:S(2)}, u32[]{:S(2)}) collective-permute-start(f32[8,1280]{1,0:T(8,128)S(1)} %fusion.1), channel_id=1, source_target_pairs={{0,48},{16,64},{32,80},{48,96},{64,112},{80,128},{96,144},{112,160... | collective-permute-start | bytes 122888
  560.9 23.2 %collective-permute-start.5 = (f32[8,1280]{1,0:T(8,128)S(1)}, f32[8,1280]{1,0:T(8,128)S(1)}, u32[]{:S(2)}, u32[]{:S(2)}) collective-permute-start(f32[8,1280]{1,0:T(8,128)S(1)} %fusion.1), channel_id=1, source_target_pairs={{0,32},{16,48},{32,64},{48,80},{64,96},{80,112},{96,128},{112,144}... | collective-permute-start | bytes 122888
  562.2 25.2 %collective-permute-start.4 = (f32[8,1280]{1,0:T(8,128)S(1)}, f32[8,1280]{1,0:T(8,128)S(1)}, u32[]{:S(2)}, u32[]{:S(2)}) collective-permute-start(f32[8,1280]{1,0:T(8,128)S(1)} %fusion.1), channel_id=1, source_target_pairs={{0,16},{16,32},{32,48},{48,64},{64,80},{80,96},{96,112},{112,128},... | collective-permute-start | bytes 122888
  568.8 23.8 %collective-permute-start.2 = (f32[24,1536]{1,0:T(8,128)S(1)}, f32[24,1536]{1,0:T(8,128)S(1)}, u32[]{:S(2)}, u32[]{:S(2)}) collective-permute-start(f32[24,1536]{1,0:T(8,128)S(1)} %fusion), channel_id=1, source_target_pairs={{0,3},{1,4},{2,5},{3,6},{4,7},{5,8},{6,9},{7,10},{8,11},{9,12},{10... | collective-permute-start | bytes 442376
  577.0 15.7 %collective-permute-start.1 = (f32[24,1536]{1,0:T(8,128)S(1)}, f32[24,1536]{1,0:T(8,128)S(1)}, u32[]{:S(2)}, u32[]{:S(2)}) collective-permute-start(f32[24,1536]{1,0:T(8,128)S(1)} %fusion), channel_id=1, source_target_pairs={{0,2},{1,3},{2,4},{3,5},{4,6},{5,7},{6,8},{7,9},{8,10},{9,11},{10,... | collective-permute-start | bytes 442376
  578.7 14.3 %collective-permute-start = (f32[24,1536]{1,0:T(8,128)S(1)}, f32[24,1536]{1,0:T(8,128)S(1)}, u32[]{:S(2)}, u32[]{:S(2)}) collective-permute-start(f32[24,1536]{1,0:T(8,128)S(1)} %fusion), channel_id=1, source_target_pairs={{0,1},{1,2},{2,3},{3,4},{4,5},{5,6},{6,7},{7,8},{8,9},{9,10},{10,1... | collective-permute-start | bytes 442376
  584.0 8.6 %collective-permute-start.3 = (f32[18,1536]{1,0:T(8,128)S(1)}, f32[18,1536]{1,0:T(8,128)S(1)}, u32[]{:S(2)}, u32[]{:S(2)}) collective-permute-start(f32[18,1536]{1,0:T(8,128)S(1)} %slice.10), channel_id=1, source_target_pairs={{0,4},{1,5},{2,6},{3,7},{4,8},{5,9},{6,10},{7,11},{8,12},{9,13},{1... | collective-permute-start | bytes 331784
where the time goes:
time: 603 us; the launch traced here: 595 us
  blocking collectives  516 us (86%)
  starting transfers between devices  41 us (7%)
  local copies, waits for them, and re-layouts  13.7 us (2%)
  other arithmetic  12.9 us (2%)
    unnamed x2, blocking collectives  317 us
    all_gather x1, blocking collectives, local(): lax.all_gather(amp_ab, 'cd', axis=0, tiled=True)  116 us
    all_gather x1, blocking collectives, local(): lax.all_gather(amp_cd, 'ab', axis=0, tiled=True)  83.1 us
    unnamed x16, starting transfers between devices  41 us
    unnamed x27, local copies, waits for them, and re-layouts  13.5 us
  transfers between devices with their start and end apart: 16, of which 2 were waited for; matrix products, arithmetic and copies ran while one was open for 28% of the time, Pallas kernels for 0%

commit v1 on v0

v1 whole, which is shorter than its diff:
```python
import jax
import jax.numpy as jnp
from jax import lax
from jax.sharding import Mesh
from jax.sharding import PartitionSpec as P

NV = 1000
TILE = 256
AB = ("zl", "x", "core")
CD = ("y", "zh")


def lookup(index, table):
    equal = index[:, None] == jnp.arange(table.shape[0], dtype=jnp.int32)[None, :]
    return jnp.sum(jnp.where(equal, table[None, :], jnp.zeros_like(table)[None, :]), axis=1)


def pair_data(first, count, virt_irrep, virt_energy):
    index = first + jnp.arange(count, dtype=jnp.int32)
    left = index // NV
    right = index % NV
    irreps = jnp.bitwise_xor(lookup(left, virt_irrep), lookup(right, virt_irrep))
    energy = lookup(left, virt_energy) + lookup(right, virt_energy)
    return (irreps, energy)


def occ_sums(occ_pairs, occ_energy, first, count):
    left = lax.dynamic_slice_in_dim(occ_pairs[0], first, count, 0)
    right = lax.dynamic_slice_in_dim(occ_pairs[1], first, count, 0)
    return lookup(left, occ_energy) + lookup(right, occ_energy)


def send(block, axis, size, shift):
    return lax.ppermute(block, axis, [(i, (i + shift) % size) for i in range(size)])


def pick(source, rows):
    chosen = (rows[:, None] == jnp.arange(source.shape[0], dtype=jnp.int32)[None, :]).astype(source.dtype)
    return jnp.dot(chosen, source, preferred_element_type=jnp.float32).astype(source.dtype)


def pad_rows(block, count):
    return jnp.pad(block, ((0, count - block.shape[0]), (0, 0)))


def local(integrals, tile_mask, virt_irrep, occ_pairs, virt_energy, occ_energy, amp_ab, amp_cd):
    rows_dev = integrals.shape[0]
    cols_dev = integrals.shape[1]
    nzl, nx, ncore, ny, nzh = (lax.axis_size(a) for a in ("zl", "x", "core", "y", "zh"))
    zl, x, core, y, zh = (lax.axis_index(a) for a in ("zl", "x", "core", "y", "zh"))
    row_group = (zl * nx + x) * ncore + core
    col_group = y * nzh + zh
    nab = rows_dev * nzl * nx * ncore
    cd_count = amp_cd.shape[0]
    ab_count = amp_ab.shape[0]
    npair = cd_count * nzl * nx * ncore

    own = pad_rows(amp_cd, 8)
    part = jnp.concatenate([own] + [send(own, "zl", nzl, -s) for s in range(1, nzl)], axis=0)
    part = jnp.concatenate([part] + [send(part, "x", nx, -t) for t in range(1, nx)], axis=0)
    all_cd = jnp.concatenate([part, send(part, "core", ncore, 1)], axis=0)

    own = jnp.concatenate([amp_ab, send(amp_ab, "zh", nzh, 1)], axis=0)
    block = 40
    own = pad_rows(own, block)
    pieces = {0: own}
    up = down = own
    for step in range(1, ny // 2):
        up = send(up, "y", ny, 1)
        down = send(down, "y", ny, -1)
        pieces[ny - step] = up
        pieces[step] = down
    half = block // 2
    pieces[ny // 2] = jnp.concatenate([send(up[:24], "y", ny, 1), send(down[24:], "y", ny, -1)], axis=0)
    all_ab = jnp.concatenate([pieces[d] for d in range(ny)], axis=0)

    row_first = row_group * rows_dev
    col_first = nab + col_group * cols_dev
    row_irrep, row_energy = pair_data(row_first, rows_dev, virt_irrep, virt_energy)
    col_irrep, col_energy = pair_data(col_first, cols_dev, virt_irrep, virt_energy)
    tiles = jnp.repeat(jnp.repeat(tile_mask, TILE, axis=0), TILE, axis=1)
    keep = (tiles == 1) & (row_irrep[:, None] == col_irrep[None, :])
    masked = jnp.where(keep, integrals, jnp.zeros_like(integrals))

    out = jnp.arange(npair, dtype=jnp.int32)
    chunk = nzh * ab_count
    k = ((y + out // chunk) % ny) * chunk + out % chunk
    group = k // cd_count
    z_off = (group // (nx * ncore) - zl) % nzl
    x_off = ((group // ncore) % nx - x) % nx
    core_off = (group % ncore - core) % ncore
    amp = pick(all_cd, ((core_off * nx + x_off) * nzl + z_off) * 8 + k % cd_count)
    partial_ab = lax.dot_general(amp, masked, (((1,), (1,)), ((), ())), preferred_element_type=jnp.float32)
    partial_ab = partial_ab.reshape(ny, nzh, ab_count, rows_dev)

    r = out % cd_count
    s = (out // cd_count) % nzl
    t = (out // (cd_count * nzl)) % nx
    u = out // (cd_count * nzl * nx)
    k = ((((zl + s) % nzl) * nx + (x + t) % nx) * ncore + (core + u) % ncore) * cd_count + r
    group = k // ab_count
    amp = pick(all_ab, ((group // nzh - y) % ny) * block + ((group % nzh - zh) % nzh) * ab_count + k % ab_count)
    partial_cd = jnp.dot(amp, masked, preferred_element_type=jnp.float32)

    up = send(partial_ab[ny // 2, 0], "y", ny, 1)
    down = send(partial_ab[ny // 2, 1], "y", ny, -1)
    mine = partial_ab[ny // 2 - 1]
    up = jnp.stack([mine[0] + up, mine[1]])
    mine = partial_ab[ny // 2 + 1]
    down = jnp.stack([mine[0], mine[1] + down])
    for step in range(ny // 2 - 1, 0, -1):
        up = send(up, "y", ny, 1) + partial_ab[step - 1]
        down = send(down, "y", ny, -1)
        if step > 1:
            down = down + partial_ab[ny - step + 1]
    total = up + down
    keep_half = lax.dynamic_index_in_dim(total, zh, 0, keepdims=False)
    give_half = lax.dynamic_index_in_dim(total, 1 - zh, 0, keepdims=False)
    ladder_ab = keep_half + send(give_half, "zh", nzh, 1)

    per_core = npair // ncore
    total = partial_cd[:per_core] + send(partial_cd[per_core:], "core", ncore, 1)
    total = total.reshape(nx, nzl * cd_count, cols_dev)
    total = total[0] + sum(send(total[t], "x", nx, t) for t in range(1, nx))
    total = total.reshape(nzl, cd_count, cols_dev)
    ladder_cd = total[0] + sum(send(total[s], "zl", nzl, s) for s in range(1, nzl))

    occ_ab = occ_sums(occ_pairs, occ_energy, col_group * ab_count, ab_count)
    occ_cd = occ_sums(occ_pairs, occ_energy, row_group * cd_count, cd_count)
    update_ab = ladder_ab / (row_energy[None, :] - occ_ab[:, None])
    update_cd = ladder_cd / (col_energy[None, :] - occ_cd[:, None])
    return (update_ab, update_cd)


def solution(mesh):
    fine = Mesh(mesh.devices.reshape(6, 4, 2, 8, 2), AB + CD)
    return jax.shard_map(
        local,
        mesh=fine,
        in_specs=(P(AB, CD), P(AB, CD), P(), P(), P(), P(), P(CD, AB), P(AB, CD)),
        out_specs=(P(CD, AB), P(AB, CD)),
        check_vma=False,
    )
```

time: 603 us -> 229 us (0.38)
  the two profiles are of different devices: /device:TPU:1 before, /device:TPU:70 now
where the time goes in v1:
time: 229 us; the launch traced here: 227 us
  starting transfers between devices  137 us (60%)
  waiting for transfers between devices  33.7 us (15%)
  other arithmetic  28.3 us (12%)
  local copies, waits for them, and re-layouts  18.6 us (8%)
  matrix products  8.17 us (4%)
    ppermute x36, starting transfers between devices, send(): lax.ppermute(block, axis, [(i, (i + shift) % size) for i in range(size)])  137 us
    ppermute x36, waiting for transfers between devices, send(): lax.ppermute(block, axis, [(i, (i + shift) % size) for i in range(size)])  33.7 us
    reduce_sum x6, other arithmetic, lookup(): jnp.sum(jnp.where(equal, table[None, :], jnp.zeros_like(table)[None, :]),...  12 us
    unnamed x28, local copies, waits for them, and re-layouts  8.2 us
    select_n x1, other arithmetic, local(): masked = jnp.where(keep, integrals, jnp.zeros_like(integrals))  5.76 us
  transfers between devices with their start and end apart: 36, of which 9 were waited for; matrix products, arithmetic and copies ran while one was open for 20% of the time, Pallas kernels for 0%

profile of v1, /device:TPU:70, one launch (start us, length us, event | category | flops | bytes accessed | tf_op | source)
XLA Modules:
  0.0 227.0 jit_solution(5757057602965938048)
XLA Ops:
  1.4 1.9 collective-permute-start
  3.3 10.9 %collective-permute-start.1 = (bf16[8,1280]{1,0:T(8,128)(2,1)S(1)}, bf16[8,1280]{1,0:T(8,128)(2,1)S(1)}, u32[]{:S(2)}, u32[]{:S(2)}) collective-permute-start(bf16[8,1280]{1,0:T(8,128)(2,1)S(1)} %get-tuple-element.59), channel_id=1, source_target_pairs={{0,512},{128,640},{256,0},{384,128},{512,256},{640,384},{1,513},{1... | collective-permute-start | bytes 61448 | tf_op jit(solution)/shard_map/ppermute | solution.py:34
  14.2 1.9 collective-permute-start.2
  16.2 5.7 %collective-permute-start.3 = (bf16[8,1280]{1,0:T(8,128)(2,1)S(1)}, bf16[8,1280]{1,0:T(8,128)(2,1)S(1)}, u32[]{:S(2)}, u32[]{:S(2)}) collective-permute-start(bf16[8,1280]{1,0:T(8,128)(2,1)S(1)} %get-tuple-element.59), channel_id=1, source_target_pairs={{0,256},{128,384},{256,512},{384,640},{512,0},{640,128},{1,257},{1... | collective-permute-start | bytes 61448 | tf_op jit(solution)/shard_map/ppermute | solution.py:34
  21.9 3.7 %collective-permute-start.4 = (bf16[8,1280]{1,0:T(8,128)(2,1)S(1)}, bf16[8,1280]{1,0:T(8,128)(2,1)S(1)}, u32[]{:S(2)}, u32[]{:S(2)}) collective-permute-start(bf16[8,1280]{1,0:T(8,128)(2,1)S(1)} %get-tuple-element.59), channel_id=1, source_target_pairs={{0,128},{128,256},{256,384},{384,512},{512,640},{640,0},{1,129},{1... | collective-permute-start | bytes 61448 | tf_op jit(solution)/shard_map/ppermute | solution.py:34
  27.9 2.4 %select_reduce_fusion.6 = (s32[1280]{0:T(1024)S(1)}, s32[1280]{0:T(1024)S(1)}) fusion(s32[1280]{0:T(1024)S(1)} %get-tuple-element.64, s32[1000]{0:T(1024)} %param.10, s32[1280]{0:T(1024)S(1)} %get-tuple-element.65), kind=kLoop, calls=%fused_computation.10 | loop fusion | flops 7677440 | bytes 24480 | tf_op jit(solution)/shard_map/reduce_sum | solution.py:15
  30.3 2.4 %select_reduce_fusion.4 = (f32[1280]{0:T(1024)S(1)}, f32[1280]{0:T(1024)S(1)}) fusion(f32[1000]{0:T(1024)} %param.12, s32[1280]{0:T(1024)S(1)} %get-tuple-element.64, s32[1280]{0:T(1024)S(1)} %get-tuple-element.65), kind=kLoop, calls=%fused_computation.8 | loop fusion | flops 7677440 | bytes 24480 | tf_op jit(solution)/shard_map/reduce_sum | solution.py:15
  32.8 2.7 %select_reduce_fusion.2 = (s32[1536]{0:T(1024)S(1)}, s32[1536]{0:T(1024)S(1)}) fusion(s32[1536]{0:T(1024)S(1)} %get-tuple-element.62, s32[1000]{0:T(1024)} %param.10, s32[1536]{0:T(1024)S(1)} %get-tuple-element.63), kind=kLoop, calls=%fused_computation.4 | loop fusion | flops 9212928 | bytes 28576 | tf_op jit(solution)/shard_map/reduce_sum | solution.py:15
  37.3 6.3 %copy.13 = bf16[1536,1280]{0,1:T(8,128)(2,1)} copy(bf16[1536,1280]{1,0:T(8,128)(2,1)} %param.8) | data formatting | bytes 7864320 | tf_op args[0]
  45.4 5.8 %fusion = bf16[1536,1280]{0,1:T(8,128)(2,1)} fusion(bf16[1536,1280]{0,1:T(8,128)(2,1)} %copy.13, s32[1536]{0:T(1024)S(1)} %xor.14, s32[1280]{0:T(1024)S(1)} %xor.15, pred[1536,5]{0,1:T(8,128)(4,1)S(1)} %bitcast.39), kind=kLoop, calls=%fused_computation.1 | loop fusion | flops 5898240 | bytes 7883264 | tf_op jit(solution)/shard_map/jit(_where)/select_n | solution.py:83
  51.2 10.0 %collective-permute-start.18 = (bf16[18,1536]{1,0:T(8,128)(2,1)S(1)}, bf16[18,1536]{1,0:T(8,128)(2,1)S(1)}, u32[]{:S(2)}, u32[]{:S(2)}) collective-permute-start(bf16[18,1536]{1,0:T(8,128)(2,1)S(1)} %copy-done), channel_id=1, source_target_pairs={{0,1},{1,0},{2,3},{3,2},{4,5},{5,4},{6,7},{7,6},{8,9},{9,8},{10,11... | collective-permute-start | bytes 165896 | tf_op jit(solution)/shard_map/ppermute | solution.py:34
  61.3 2.7 %collective-permute-start.5 = (bf16[48,1280]{1,0:T(8,128)(2,1)S(1)}, bf16[48,1280]{1,0:T(8,128)(2,1)S(1)}, u32[]{:S(2)}, u32[]{:S(2)}) collective-permute-start(bf16[48,1280]{1,0:T(8,128)(2,1)S(1)} %get-tuple-element.43), channel_id=1, source_target_pairs={{0,96},{32,0},{64,32},{96,64},{1,97},{33,1},{65,33},{97,65},{2,98}... | collective-permute-start | bytes 368648 | tf_op jit(solution)/shard_map/ppermute | solution.py:34
  64.0 3.0 %collective-permute-start.6 = (bf16[48,1280]{1,0:T(8,128)(2,1)S(1)}, bf16[48,1280]{1,0:T(8,128)(2,1)S(1)}, u32[]{:S(2)}, u32[]{:S(2)}) collective-permute-start(bf16[48,1280]{1,0:T(8,128)(2,1)S(1)} %get-tuple-element.43), channel_id=1, source_target_pairs={{0,64},{32,96},{64,0},{96,32},{1,65},{33,97},{65,1},{97,33},{2,66}... | collective-permute-start | bytes 368648 | tf_op jit(solution)/shard_map/ppermute | solution.py:34
  67.0 4.0 %collective-permute-start.7 = (bf16[48,1280]{1,0:T(8,128)(2,1)S(1)}, bf16[48,1280]{1,0:T(8,128)(2,1)S(1)}, u32[]{:S(2)}, u32[]{:S(2)}) collective-permute-start(bf16[48,1280]{1,0:T(8,128)(2,1)S(1)} %get-tuple-element.43), channel_id=1, source_target_pairs={{0,32},{32,64},{64,96},{96,0},{1,33},{33,65},{65,97},{97,1},{2,34}... | collective-permute-start | bytes 368648 | tf_op jit(solution)/shard_map/ppermute | solution.py:34
  71.1 5.4 %collective-permute-start.19 = (bf16[40,1536]{1,0:T(8,128)(2,1)S(1)}, bf16[40,1536]{1,0:T(8,128)(2,1)S(1)}, u32[]{:S(2)}, u32[]{:S(2)}) collective-permute-start(bf16[40,1536]{1,0:T(8,128)(2,1)S(1)} %get-tuple-element.15), channel_id=1, source_target_pairs={{0,14},{2,0},{4,2},{6,4},{8,6},{10,8},{12,10},{14,12},{1,15},{3,1}... | collective-permute-start | bytes 368648 | tf_op jit(solution)/shard_map/ppermute | solution.py:34
  76.5 1.9 collective-permute-start.22
  78.5 1.9 collective-permute-start.8
  80.5 5.1 %collective-permute-start.20 = (bf16[40,1536]{1,0:T(8,128)(2,1)S(1)}, bf16[40,1536]{1,0:T(8,128)(2,1)S(1)}, u32[]{:S(2)}, u32[]{:S(2)}) collective-permute-start(bf16[40,1536]{1,0:T(8,128)(2,1)S(1)} %collective-permute-done.19), channel_id=1, source_target_pairs={{0,14},{2,0},{4,2},{6,4},{8,6},{10,8},{12,10},{14,12},{1,15},{3,1}... | collective-permute-start | bytes 368648 | tf_op jit(solution)/shard_map/ppermute | solution.py:34
  85.6 1.9 collective-permute-start.23
  88.8 5.6 %collective-permute-start.21 = (bf16[40,1536]{1,0:T(8,128)(2,1)S(1)}, bf16[40,1536]{1,0:T(8,128)(2,1)S(1)}, u32[]{:S(2)}, u32[]{:S(2)}) collective-permute-start(bf16[40,1536]{1,0:T(8,128)(2,1)S(1)} %collective-permute-done.20), channel_id=1, source_target_pairs={{0,14},{2,0},{4,2},{6,4},{8,6},{10,8},{12,10},{14,12},{1,15},{3,1}... | collective-permute-start | bytes 368648 | tf_op jit(solution)/shard_map/ppermute | solution.py:34
  94.4 1.9 collective-permute-start.24
  96.4 6.0 %collective-permute-done.24 = bf16[40,1536]{1,0:T(8,128)(2,1)S(1)} collective-permute-done((bf16[40,1536]{1,0:T(8,128)(2,1)S(1)}, bf16[40,1536]{1,0:T(8,128)(2,1)S(1)}, u32[]{:S(2)}, u32[]{:S(2)}) %collective-permute-start.24) | collective-permute-done | bytes 122912 | tf_op jit(solution)/shard_map/ppermute | solution.py:34
  104.4 5.1 %collective-permute-start.26 = (bf16[16,1536]{1,0:T(8,128)(2,1)S(1)}, bf16[16,1536]{1,0:T(8,128)(2,1)S(1)}, u32[]{:S(2)}, u32[]{:S(2)}) collective-permute-start(bf16[16,1536]{1,0:T(8,128)(2,1)S(1)} %slice.155), channel_id=1, source_target_pairs={{0,14},{2,0},{4,2},{6,4},{8,6},{10,8},{12,10},{14,12},{1,15},{3,1}... | collective-permute-start | bytes 147464 | tf_op jit(solution)/shard_map/ppermute | solution.py:34
  112.3 3.8 %fusion.2 = f32[288,1536]{1,0:T(8,128)S(1)} fusion(bf16[1536,1280]{0,1:T(8,128)(2,1)} %fusion, bf16[384,1280]{1,0:T(8,128)(2,1)S(1)} %constant_dynamic-update-slice_fusion.15, s32[288]{0:T(512)S(1)} %fusion.42), kind=kOutput, calls=%fused_computation.17 | convolution fusion | flops 1416056832 | bytes 6685824 | tf_op jit(solution)/shard_map/dot_general | solution.py:93
  119.5 5.5 %collective-permute-start.13 = (f32[18,1536]{1,0:T(8,128)}, f32[18,1536]{1,0:T(8,128)S(1)}, u32[]{:S(2)}, u32[]{:S(2)}) collective-permute-start(f32[18,1536]{1,0:T(8,128)} %get-tuple-element.17), channel_id=1, source_target_pairs={{0,14},{2,0},{4,2},{6,4},{8,6},{10,8},{12,10},{14,12},{1,15},{3,1}... | collective-permute-start | bytes 331784 | tf_op jit(solution)/shard_map/ppermute | solution.py:34
  124.9 2.1 collective-permute-start.9
  127.1 4.3 %fusion.1 = f32[288,1280]{1,0:T(8,128)S(1)} fusion(bf16[1536,1280]{0,1:T(8,128)(2,1)} %fusion, bf16[320,1536]{1,0:T(8,128)(2,1)} %copy-done.2, s32[288]{0:T(512)} %fusion.66), kind=kOutput, calls=%fused_computation.16 | convolution fusion | flops 1416112128 | bytes 6390912 | tf_op jit(solution)/shard_map/dot_general | solution.py:103
  132.3 1.9 collective-permute-start.27
  137.7 5.1 %collective-permute-start.14 = (f32[2,18,1536]{2,1,0:T(8,128)}, f32[2,18,1536]{2,1,0:T(8,128)}, u32[]{:S(2)}, u32[]{:S(2)}) collective-permute-start(f32[2,18,1536]{2,1,0:T(8,128)} %pad_maximum_fusion.1), channel_id=1, source_target_pairs={{0,14},{2,0},{4,2},{6,4},{8,6},{10,8},{12,10},{14,12},{1,15},{3,1}... | collective-permute-start | bytes 663560 | tf_op jit(solution)/shard_map/ppermute | solution.py:34
  145.8 2.4 %collective-permute-done.10 = f32[2,18,1536]{2,1,0:T(8,128)} collective-permute-done((f32[2,18,1536]{2,1,0:T(8,128)}, f32[2,18,1536]{2,1,0:T(8,128)}, u32[]{:S(2)}, u32[]{:S(2)}) %collective-permute-start.10) | collective-permute-done | bytes 221216 | tf_op jit(solution)/shard_map/ppermute | solution.py:34
  149.2 1.9 collective-permute-start.11
  152.1 5.1 %collective-permute-start.15 = (f32[2,18,1536]{2,1,0:T(8,128)S(1)}, f32[2,18,1536]{2,1,0:T(8,128)}, u32[]{:S(2)}, u32[]{:S(2)}) collective-permute-start(f32[2,18,1536]{2,1,0:T(8,128)S(1)} %add.481), channel_id=1, source_target_pairs={{0,14},{2,0},{4,2},{6,4},{8,6},{10,8},{12,10},{14,12},{1,15},{3,1}... | collective-permute-start | bytes 663560 | tf_op jit(solution)/shard_map/ppermute | solution.py:34
  157.2 2.9 %select_reduce_fusion = (f32[1536]{0:T(1024)S(1)}, f32[1536]{0:T(1024)S(1)}) fusion(f32[1000]{0:T(1024)} %param.12, s32[1536]{0:T(1024)S(1)} %get-tuple-element.62, s32[1536]{0:T(1024)S(1)} %get-tuple-element.63), kind=kLoop, calls=%fused_computation.2 | loop fusion | flops 9212928 | bytes 28576 | tf_op jit(solution)/shard_map/reduce_sum | solution.py:15
  162.2 1.9 collective-permute-start.12
  165.1 5.1 %collective-permute-start.16 = (f32[2,18,1536]{2,1,0:T(8,128)S(1)}, f32[2,18,1536]{2,1,0:T(8,128)S(1)}, u32[]{:S(2)}, u32[]{:S(2)}) collective-permute-start(f32[2,18,1536]{2,1,0:T(8,128)S(1)} %add.482), channel_id=1, source_target_pairs={{0,14},{2,0},{4,2},{6,4},{8,6},{10,8},{12,10},{14,12},{1,15},{3,1}... | collective-permute-start | bytes 663560 | tf_op jit(solution)/shard_map/ppermute | solution.py:34
  171.5 2.8 %collective-permute-start.28 = (f32[36,1280]{1,0:T(8,128)S(1)}, f32[36,1280]{1,0:T(8,128)S(1)}, u32[]{:S(2)}, u32[]{:S(2)}) collective-permute-start(f32[36,1280]{1,0:T(8,128)S(1)} %get-tuple-element.29), channel_id=1, source_target_pairs={{0,32},{32,64},{64,96},{96,0},{1,33},{33,65},{65,97},{97,1},{2,34}... | collective-permute-start | bytes 552968 | tf_op jit(solution)/shard_map/ppermute | solution.py:34
  174.3 3.2 %collective-permute-start.29 = (f32[36,1280]{1,0:T(8,128)S(1)}, f32[36,1280]{1,0:T(8,128)S(1)}, u32[]{:S(2)}, u32[]{:S(2)}) collective-permute-start(f32[36,1280]{1,0:T(8,128)S(1)} %get-tuple-element.27), channel_id=1, source_target_pairs={{0,64},{32,96},{64,0},{96,32},{1,65},{33,97},{65,1},{97,33},{2,66}... | collective-permute-start | bytes 552968 | tf_op jit(solution)/shard_map/ppermute | solution.py:34
  177.5 3.3 %collective-permute-start.30 = (f32[36,1280]{1,0:T(8,128)S(1)}, f32[36,1280]{1,0:T(8,128)S(1)}, u32[]{:S(2)}, u32[]{:S(2)}) collective-permute-start(f32[36,1280]{1,0:T(8,128)S(1)} %get-tuple-element.28), channel_id=1, source_target_pairs={{0,96},{32,0},{64,32},{96,64},{1,97},{33,1},{65,33},{97,65},{2,98}... | collective-permute-start | bytes 552968 | tf_op jit(solution)/shard_map/ppermute | solution.py:34
  180.9 3.8 %collective-permute-done.29 = f32[36,1280]{1,0:T(8,128)S(1)} collective-permute-done((f32[36,1280]{1,0:T(8,128)S(1)}, f32[36,1280]{1,0:T(8,128)S(1)}, u32[]{:S(2)}, u32[]{:S(2)}) %collective-permute-start.29) | collective-permute-done | bytes 184352 | tf_op jit(solution)/shard_map/ppermute | solution.py:34
  184.7 3.1 %collective-permute-done.30 = f32[36,1280]{1,0:T(8,128)S(1)} collective-permute-done((f32[36,1280]{1,0:T(8,128)S(1)}, f32[36,1280]{1,0:T(8,128)S(1)}, u32[]{:S(2)}, u32[]{:S(2)}) %collective-permute-start.30) | collective-permute-done | bytes 184352 | tf_op jit(solution)/shard_map/ppermute | solution.py:34
  187.9 3.7 %collective-permute-start.31 = (f32[6,1280]{1,0:T(8,128)S(1)}, f32[6,1280]{1,0:T(8,128)S(1)}, u32[]{:S(2)}, u32[]{:S(2)}) collective-permute-start(f32[6,1280]{1,0:T(8,128)S(1)} %get-tuple-element.34), channel_id=1, source_target_pairs={{0,128},{128,256},{256,384},{384,512},{512,640},{640,0},{1,129},{1... | collective-permute-start | bytes 92168 | tf_op jit(solution)/shard_map/ppermute | solution.py:34
  191.6 3.1 %collective-permute-start.32 = (f32[6,1280]{1,0:T(8,128)S(1)}, f32[6,1280]{1,0:T(8,128)S(1)}, u32[]{:S(2)}, u32[]{:S(2)}) collective-permute-start(f32[6,1280]{1,0:T(8,128)S(1)} %get-tuple-element.30), channel_id=1, source_target_pairs={{0,256},{128,384},{256,512},{384,640},{512,0},{640,128},{1,257},{1... | collective-permute-start | bytes 92168 | tf_op jit(solution)/shard_map/ppermute | solution.py:34
  194.8 5.4 %collective-permute-start.33 = (f32[6,1280]{1,0:T(8,128)S(1)}, f32[6,1280]{1,0:T(8,128)S(1)}, u32[]{:S(2)}, u32[]{:S(2)}) collective-permute-start(f32[6,1280]{1,0:T(8,128)S(1)} %get-tuple-element.33), channel_id=1, source_target_pairs={{0,384},{128,512},{256,640},{384,0},{512,128},{640,256},{1,385},{1... | collective-permute-start | bytes 92168 | tf_op jit(solution)/shard_map/ppermute | solution.py:34
  200.2 5.8 %collective-permute-start.34 = (f32[6,1280]{1,0:T(8,128)S(1)}, f32[6,1280]{1,0:T(8,128)S(1)}, u32[]{:S(2)}, u32[]{:S(2)}) collective-permute-start(f32[6,1280]{1,0:T(8,128)S(1)} %get-tuple-element.32), channel_id=1, source_target_pairs={{0,512},{128,640},{256,0},{384,128},{512,256},{640,384},{1,513},{1... | collective-permute-start | bytes 92168 | tf_op jit(solution)/shard_map/ppermute | solution.py:34
  206.0 1.9 collective-permute-start.35
  208.0 2.2 collective-permute-start.17
  210.3 4.0 %collective-permute-done.35 = f32[6,1280]{1,0:T(8,128)S(1)} collective-permute-done((f32[6,1280]{1,0:T(8,128)S(1)}, f32[6,1280]{1,0:T(8,128)S(1)}, u32[]{:S(2)}, u32[]{:S(2)}) %collective-permute-start.35) | collective-permute-done | bytes 30752 | tf_op jit(solution)/shard_map/ppermute | solution.py:34
  215.0 11.2 %collective-permute-done.17 = f32[18,1536]{1,0:T(8,128)S(1)} collective-permute-done((f32[18,1536]{1,0:T(8,128)S(1)}, f32[18,1536]{1,0:T(8,128)S(1)}, u32[]{:S(2)}, u32[]{:S(2)}) %collective-permute-start.17) | collective-permute-done | bytes 110624 | tf_op jit(solution)/shard_map/ppermute | solution.py:34
  (106 shorter events, 31.4 us)
Async XLA Ops:
  1.4 49.8 %collective-permute-start = (bf16[8,1280]{1,0:T(8,128)(2,1)S(1)}, bf16[8,1280]{1,0:T(8,128)(2,1)S(1)}, u32[]{:S(2)}, u32[]{:S(2)}) collective-permute-start(bf16[8,1280]{1,0:T(8,128)(2,1)S(1)} %get-tuple-element.59), channel_id=1, source_target_pairs={{0,640},{128,0},{256,128},{384,256},{512,384},{640,512},{1,641},{1... | collective-permute-start | bytes 61448 | tf_op jit(solution)/shard_map/ppermute | solution.py:34
  3.3 57.9 %collective-permute-start.1 = (bf16[8,1280]{1,0:T(8,128)(2,1)S(1)}, bf16[8,1280]{1,0:T(8,128)(2,1)S(1)}, u32[]{:S(2)}, u32[]{:S(2)}) collective-permute-start(bf16[8,1280]{1,0:T(8,128)(2,1)S(1)} %get-tuple-element.59), channel_id=1, source_target_pairs={{0,512},{128,640},{256,0},{384,128},{512,256},{640,384},{1,513},{1... | collective-permute-start | bytes 61448 | tf_op jit(solution)/shard_map/ppermute | solution.py:34
  14.2 47.0 %collective-permute-start.2 = (bf16[8,1280]{1,0:T(8,128)(2,1)S(1)}, bf16[8,1280]{1,0:T(8,128)(2,1)S(1)}, u32[]{:S(2)}, u32[]{:S(2)}) collective-permute-start(bf16[8,1280]{1,0:T(8,128)(2,1)S(1)} %get-tuple-element.59), channel_id=1, source_target_pairs={{0,384},{128,512},{256,640},{384,0},{512,128},{640,256},{1,385},{1... | collective-permute-start | bytes 61448 | tf_op jit(solution)/shard_map/ppermute | solution.py:34
  16.2 45.1 %collective-permute-start.3 = (bf16[8,1280]{1,0:T(8,128)(2,1)S(1)}, bf16[8,1280]{1,0:T(8,128)(2,1)S(1)}, u32[]{:S(2)}, u32[]{:S(2)}) collective-permute-start(bf16[8,1280]{1,0:T(8,128)(2,1)S(1)} %get-tuple-element.59), channel_id=1, source_target_pairs={{0,256},{128,384},{256,512},{384,640},{512,0},{640,128},{1,257},{1... | collective-permute-start | bytes 61448 | tf_op jit(solution)/shard_map/ppermute | solution.py:34
  21.9 39.3 %collective-permute-start.4 = (bf16[8,1280]{1,0:T(8,128)(2,1)S(1)}, bf16[8,1280]{1,0:T(8,128)(2,1)S(1)}, u32[]{:S(2)}, u32[]{:S(2)}) collective-permute-start(bf16[8,1280]{1,0:T(8,128)(2,1)S(1)} %get-tuple-element.59), channel_id=1, source_target_pairs={{0,128},{128,256},{256,384},{384,512},{512,640},{640,0},{1,129},{1... | collective-permute-start | bytes 61448 | tf_op jit(solution)/shard_map/ppermute | solution.py:34
  45.4 5.8 %copy-start = (bf16[18,1536]{1,0:T(8,128)(2,1)S(1)}, bf16[18,1536]{1,0:T(8,128)(2,1)}, u32[]{:S(2)}) copy-start(bf16[18,1536]{1,0:T(8,128)(2,1)} %param.14) | copy-start | bytes 165892
  51.2 19.9 %collective-permute-start.18 = (bf16[18,1536]{1,0:T(8,128)(2,1)S(1)}, bf16[18,1536]{1,0:T(8,128)(2,1)S(1)}, u32[]{:S(2)}, u32[]{:S(2)}) collective-permute-start(bf16[18,1536]{1,0:T(8,128)(2,1)S(1)} %copy-done), channel_id=1, source_target_pairs={{0,1},{1,0},{2,3},{3,2},{4,5},{5,4},{6,7},{7,6},{8,9},{9,8},{10,11... | collective-permute-start | bytes 165896 | tf_op jit(solution)/shard_map/ppermute | solution.py:34
  61.3 17.2 %collective-permute-start.5 = (bf16[48,1280]{1,0:T(8,128)(2,1)S(1)}, bf16[48,1280]{1,0:T(8,128)(2,1)S(1)}, u32[]{:S(2)}, u32[]{:S(2)}) collective-permute-start(bf16[48,1280]{1,0:T(8,128)(2,1)S(1)} %get-tuple-element.43), channel_id=1, source_target_pairs={{0,96},{32,0},{64,32},{96,64},{1,97},{33,1},{65,33},{97,65},{2,98}... | collective-permute-start | bytes 368648 | tf_op jit(solution)/shard_map/ppermute | solution.py:34
  64.0 14.4 %collective-permute-start.6 = (bf16[48,1280]{1,0:T(8,128)(2,1)S(1)}, bf16[48,1280]{1,0:T(8,128)(2,1)S(1)}, u32[]{:S(2)}, u32[]{:S(2)}) collective-permute-start(bf16[48,1280]{1,0:T(8,128)(2,1)S(1)} %get-tuple-element.43), channel_id=1, source_target_pairs={{0,64},{32,96},{64,0},{96,32},{1,65},{33,97},{65,1},{97,33},{2,66}... | collective-permute-start | bytes 368648 | tf_op jit(solution)/shard_map/ppermute | solution.py:34
  67.0 11.5 %collective-permute-start.7 = (bf16[48,1280]{1,0:T(8,128)(2,1)S(1)}, bf16[48,1280]{1,0:T(8,128)(2,1)S(1)}, u32[]{:S(2)}, u32[]{:S(2)}) collective-permute-start(bf16[48,1280]{1,0:T(8,128)(2,1)S(1)} %get-tuple-element.43), channel_id=1, source_target_pairs={{0,32},{32,64},{64,96},{96,0},{1,33},{33,65},{65,97},{97,1},{2,34}... | collective-permute-start | bytes 368648 | tf_op jit(solution)/shard_map/ppermute | solution.py:34
  71.1 9.4 %collective-permute-start.19 = (bf16[40,1536]{1,0:T(8,128)(2,1)S(1)}, bf16[40,1536]{1,0:T(8,128)(2,1)S(1)}, u32[]{:S(2)}, u32[]{:S(2)}) collective-permute-start(bf16[40,1536]{1,0:T(8,128)(2,1)S(1)} %get-tuple-element.15), channel_id=1, source_target_pairs={{0,14},{2,0},{4,2},{6,4},{8,6},{10,8},{12,10},{14,12},{1,15},{3,1}... | collective-permute-start | bytes 368648 | tf_op jit(solution)/shard_map/ppermute | solution.py:34
  76.5 9.1 %collective-permute-start.22 = (bf16[40,1536]{1,0:T(8,128)(2,1)S(1)}, bf16[40,1536]{1,0:T(8,128)(2,1)S(1)}, u32[]{:S(2)}, u32[]{:S(2)}) collective-permute-start(bf16[40,1536]{1,0:T(8,128)(2,1)S(1)} %get-tuple-element.15), channel_id=1, source_target_pairs={{0,2},{2,4},{4,6},{6,8},{8,10},{10,12},{12,14},{14,0},{1,3},{3,5},... | collective-permute-start | bytes 368648 | tf_op jit(solution)/shard_map/ppermute | solution.py:34
  78.5 32.8 %collective-permute-start.8 = (bf16[192,1280]{1,0:T(8,128)(2,1)S(1)}, bf16[192,1280]{1,0:T(8,128)(2,1)S(1)}, u32[]{:S(2)}, u32[]{:S(2)}) collective-permute-start(bf16[192,1280]{1,0:T(8,128)(2,1)S(1)} %get-tuple-element.35), channel_id=1, source_target_pairs={{0,16},{16,0},{1,17},{17,1},{2,18},{18,2},{3,19},{19,3},{4,20},{20... | collective-permute-start | bytes 1474568 | tf_op jit(solution)/shard_map/ppermute | solution.py:34
  80.5 8.4 %collective-permute-start.20 = (bf16[40,1536]{1,0:T(8,128)(2,1)S(1)}, bf16[40,1536]{1,0:T(8,128)(2,1)S(1)}, u32[]{:S(2)}, u32[]{:S(2)}) collective-permute-start(bf16[40,1536]{1,0:T(8,128)(2,1)S(1)} %collective-permute-done.19), channel_id=1, source_target_pairs={{0,14},{2,0},{4,2},{6,4},{8,6},{10,8},{12,10},{14,12},{1,15},{3,1}... | collective-permute-start | bytes 368648 | tf_op jit(solution)/shard_map/ppermute | solution.py:34
  85.6 8.8 %collective-permute-start.23 = (bf16[40,1536]{1,0:T(8,128)(2,1)S(1)}, bf16[40,1536]{1,0:T(8,128)(2,1)S(1)}, u32[]{:S(2)}, u32[]{:S(2)}) collective-permute-start(bf16[40,1536]{1,0:T(8,128)(2,1)S(1)} %collective-permute-done.22), channel_id=1, source_target_pairs={{0,2},{2,4},{4,6},{6,8},{8,10},{10,12},{12,14},{14,0},{1,3},{3,5},... | collective-permute-start | bytes 368648 | tf_op jit(solution)/shard_map/ppermute | solution.py:34
  88.8 15.5 %collective-permute-start.21 = (bf16[40,1536]{1,0:T(8,128)(2,1)S(1)}, bf16[40,1536]{1,0:T(8,128)(2,1)S(1)}, u32[]{:S(2)}, u32[]{:S(2)}) collective-permute-start(bf16[40,1536]{1,0:T(8,128)(2,1)S(1)} %collective-permute-done.20), channel_id=1, source_target_pairs={{0,14},{2,0},{4,2},{6,4},{8,6},{10,8},{12,10},{14,12},{1,15},{3,1}... | collective-permute-start | bytes 368648 | tf_op jit(solution)/shard_map/ppermute | solution.py:34
  94.4 8.0 %collective-permute-start.24 = (bf16[40,1536]{1,0:T(8,128)(2,1)S(1)}, bf16[40,1536]{1,0:T(8,128)(2,1)S(1)}, u32[]{:S(2)}, u32[]{:S(2)}) collective-permute-start(bf16[40,1536]{1,0:T(8,128)(2,1)S(1)} %collective-permute-done.23), channel_id=1, source_target_pairs={{0,2},{2,4},{4,6},{6,8},{8,10},{10,12},{12,14},{14,0},{1,3},{3,5},... | collective-permute-start | bytes 368648 | tf_op jit(solution)/shard_map/ppermute | solution.py:34
  102.4 7.4 %collective-permute-start.25 = (bf16[24,1536]{1,0:T(8,128)(2,1)S(1)}, bf16[24,1536]{1,0:T(8,128)(2,1)S(1)}, u32[]{:S(2)}, u32[]{:S(2)}) collective-permute-start(bf16[24,1536]{1,0:T(8,128)(2,1)S(1)} %slice.154), channel_id=1, source_target_pairs={{0,2},{2,4},{4,6},{6,8},{8,10},{10,12},{12,14},{14,0},{1,3},{3,5},... | collective-permute-start | bytes 221192 | tf_op jit(solution)/shard_map/ppermute | solution.py:34
  104.4 6.9 %collective-permute-start.26 = (bf16[16,1536]{1,0:T(8,128)(2,1)S(1)}, bf16[16,1536]{1,0:T(8,128)(2,1)S(1)}, u32[]{:S(2)}, u32[]{:S(2)}) collective-permute-start(bf16[16,1536]{1,0:T(8,128)(2,1)S(1)} %slice.155), channel_id=1, source_target_pairs={{0,14},{2,0},{4,2},{6,4},{8,6},{10,8},{12,10},{14,12},{1,15},{3,1}... | collective-permute-start | bytes 147464 | tf_op jit(solution)/shard_map/ppermute | solution.py:34
  111.3 0.9 copy-start.2
  119.5 14.8 %collective-permute-start.13 = (f32[18,1536]{1,0:T(8,128)}, f32[18,1536]{1,0:T(8,128)S(1)}, u32[]{:S(2)}, u32[]{:S(2)}) collective-permute-start(f32[18,1536]{1,0:T(8,128)} %get-tuple-element.17), channel_id=1, source_target_pairs={{0,14},{2,0},{4,2},{6,4},{8,6},{10,8},{12,10},{14,12},{1,15},{3,1}... | collective-permute-start | bytes 331784 | tf_op jit(solution)/shard_map/ppermute | solution.py:34
  124.9 9.3 %collective-permute-start.9 = (f32[18,1536]{1,0:T(8,128)}, f32[18,1536]{1,0:T(8,128)S(1)}, u32[]{:S(2)}, u32[]{:S(2)}) collective-permute-start(f32[18,1536]{1,0:T(8,128)} %get-tuple-element.16), channel_id=1, source_target_pairs={{0,2},{2,4},{4,6},{6,8},{8,10},{10,12},{12,14},{14,0},{1,3},{3,5},... | collective-permute-start | bytes 331784 | tf_op jit(solution)/shard_map/ppermute | solution.py:34
  132.3 37.9 %collective-permute-start.27 = (f32[144,1280]{1,0:T(8,128)}, f32[144,1280]{1,0:T(8,128)}, u32[]{:S(2)}, u32[]{:S(2)}) collective-permute-start(f32[144,1280]{1,0:T(8,128)} %slice.157), channel_id=1, source_target_pairs={{0,16},{16,0},{1,17},{17,1},{2,18},{18,2},{3,19},{19,3},{4,20},{20... | collective-permute-start | bytes 2211848 | tf_op jit(solution)/shard_map/ppermute | solution.py:34
  135.1 13.1 %collective-permute-start.10 = (f32[2,18,1536]{2,1,0:T(8,128)}, f32[2,18,1536]{2,1,0:T(8,128)}, u32[]{:S(2)}, u32[]{:S(2)}) collective-permute-start(f32[2,18,1536]{2,1,0:T(8,128)} %pad_maximum_fusion), channel_id=1, source_target_pairs={{0,2},{2,4},{4,6},{6,8},{8,10},{10,12},{12,14},{14,0},{1,3},{3,5},... | collective-permute-start | bytes 663560 | tf_op jit(solution)/shard_map/ppermute | solution.py:34
  137.7 13.4 %collective-permute-start.14 = (f32[2,18,1536]{2,1,0:T(8,128)}, f32[2,18,1536]{2,1,0:T(8,128)}, u32[]{:S(2)}, u32[]{:S(2)}) collective-permute-start(f32[2,18,1536]{2,1,0:T(8,128)} %pad_maximum_fusion.1), channel_id=1, source_target_pairs={{0,14},{2,0},{4,2},{6,4},{8,6},{10,8},{12,10},{14,12},{1,15},{3,1}... | collective-permute-start | bytes 663560 | tf_op jit(solution)/shard_map/ppermute | solution.py:34
  149.2 13.0 %collective-permute-start.11 = (f32[2,18,1536]{2,1,0:T(8,128)S(1)}, f32[2,18,1536]{2,1,0:T(8,128)S(1)}, u32[]{:S(2)}, u32[]{:S(2)}) collective-permute-start(f32[2,18,1536]{2,1,0:T(8,128)S(1)} %add.477), channel_id=1, source_target_pairs={{0,2},{2,4},{4,6},{6,8},{8,10},{10,12},{12,14},{14,0},{1,3},{3,5},... | collective-permute-start | bytes 663560 | tf_op jit(solution)/shard_map/ppermute | solution.py:34
  152.1 12.0 %collective-permute-start.15 = (f32[2,18,1536]{2,1,0:T(8,128)S(1)}, f32[2,18,1536]{2,1,0:T(8,128)}, u32[]{:S(2)}, u32[]{:S(2)}) collective-permute-start(f32[2,18,1536]{2,1,0:T(8,128)S(1)} %add.481), channel_id=1, source_target_pairs={{0,14},{2,0},{4,2},{6,4},{8,6},{10,8},{12,10},{14,12},{1,15},{3,1}... | collective-permute-start | bytes 663560 | tf_op jit(solution)/shard_map/ppermute | solution.py:34
  162.1 52.2 %copy-start.1 = (f32[1280]{0:T(1024)S(1)}, f32[1280]{0:T(1024)}, u32[]{:S(2)}) copy-start(f32[1280]{0:T(1024)} %add.517) | copy-start | bytes 15364
  162.1 52.2 %copy-start.4 = (f32[6]{0:T(128)S(1)}, f32[6]{0:T(128)}, u32[]{:S(2)}) copy-start(f32[6]{0:T(128)} %add.519) | copy-start | bytes 76
  162.2 64.1 %copy-start.3 = (f32[18]{0:T(128)S(1)}, f32[18]{0:T(128)}, u32[]{:S(2)}) copy-start(f32[18]{0:T(128)} %add.489) | copy-start | bytes 220
  162.2 18.6 %collective-permute-start.12 = (f32[2,18,1536]{2,1,0:T(8,128)S(1)}, f32[2,18,1536]{2,1,0:T(8,128)S(1)}, u32[]{:S(2)}, u32[]{:S(2)}) collective-permute-start(f32[2,18,1536]{2,1,0:T(8,128)S(1)} %add.478), channel_id=1, source_target_pairs={{0,2},{2,4},{4,6},{6,8},{8,10},{10,12},{12,14},{14,0},{1,3},{3,5},... | collective-permute-start | bytes 663560 | tf_op jit(solution)/shard_map/ppermute | solution.py:34
  165.1 15.7 %collective-permute-start.16 = (f32[2,18,1536]{2,1,0:T(8,128)S(1)}, f32[2,18,1536]{2,1,0:T(8,128)S(1)}, u32[]{:S(2)}, u32[]{:S(2)}) collective-permute-start(f32[2,18,1536]{2,1,0:T(8,128)S(1)} %add.482), channel_id=1, source_target_pairs={{0,14},{2,0},{4,2},{6,4},{8,6},{10,8},{12,10},{14,12},{1,15},{3,1}... | collective-permute-start | bytes 663560 | tf_op jit(solution)/shard_map/ppermute | solution.py:34
  171.5 9.4 %collective-permute-start.28 = (f32[36,1280]{1,0:T(8,128)S(1)}, f32[36,1280]{1,0:T(8,128)S(1)}, u32[]{:S(2)}, u32[]{:S(2)}) collective-permute-start(f32[36,1280]{1,0:T(8,128)S(1)} %get-tuple-element.29), channel_id=1, source_target_pairs={{0,32},{32,64},{64,96},{96,0},{1,33},{33,65},{65,97},{97,1},{2,34}... | collective-permute-start | bytes 552968 | tf_op jit(solution)/shard_map/ppermute | solution.py:34
  174.3 10.4 %collective-permute-start.29 = (f32[36,1280]{1,0:T(8,128)S(1)}, f32[36,1280]{1,0:T(8,128)S(1)}, u32[]{:S(2)}, u32[]{:S(2)}) collective-permute-start(f32[36,1280]{1,0:T(8,128)S(1)} %get-tuple-element.27), channel_id=1, source_target_pairs={{0,64},{32,96},{64,0},{96,32},{1,65},{33,97},{65,1},{97,33},{2,66}... | collective-permute-start | bytes 552968 | tf_op jit(solution)/shard_map/ppermute | solution.py:34
  177.5 10.4 %collective-permute-start.30 = (f32[36,1280]{1,0:T(8,128)S(1)}, f32[36,1280]{1,0:T(8,128)S(1)}, u32[]{:S(2)}, u32[]{:S(2)}) collective-permute-start(f32[36,1280]{1,0:T(8,128)S(1)} %get-tuple-element.28), channel_id=1, source_target_pairs={{0,96},{32,0},{64,32},{96,64},{1,97},{33,1},{65,33},{97,65},{2,98}... | collective-permute-start | bytes 552968 | tf_op jit(solution)/shard_map/ppermute | solution.py:34
  187.9 20.0 %collective-permute-start.31 = (f32[6,1280]{1,0:T(8,128)S(1)}, f32[6,1280]{1,0:T(8,128)S(1)}, u32[]{:S(2)}, u32[]{:S(2)}) collective-permute-start(f32[6,1280]{1,0:T(8,128)S(1)} %get-tuple-element.34), channel_id=1, source_target_pairs={{0,128},{128,256},{256,384},{384,512},{512,640},{640,0},{1,129},{1... | collective-permute-start | bytes 92168 | tf_op jit(solution)/shard_map/ppermute | solution.py:34
  191.6 18.6 %collective-permute-start.32 = (f32[6,1280]{1,0:T(8,128)S(1)}, f32[6,1280]{1,0:T(8,128)S(1)}, u32[]{:S(2)}, u32[]{:S(2)}) collective-permute-start(f32[6,1280]{1,0:T(8,128)S(1)} %get-tuple-element.30), channel_id=1, source_target_pairs={{0,256},{128,384},{256,512},{384,640},{512,0},{640,128},{1,257},{1... | collective-permute-start | bytes 92168 | tf_op jit(solution)/shard_map/ppermute | solution.py:34
  194.8 15.5 %collective-permute-start.33 = (f32[6,1280]{1,0:T(8,128)S(1)}, f32[6,1280]{1,0:T(8,128)S(1)}, u32[]{:S(2)}, u32[]{:S(2)}) collective-permute-start(f32[6,1280]{1,0:T(8,128)S(1)} %get-tuple-element.33), channel_id=1, source_target_pairs={{0,384},{128,512},{256,640},{384,0},{512,128},{640,256},{1,385},{1... | collective-permute-start | bytes 92168 | tf_op jit(solution)/shard_map/ppermute | solution.py:34
  200.2 10.1 %collective-permute-start.34 = (f32[6,1280]{1,0:T(8,128)S(1)}, f32[6,1280]{1,0:T(8,128)S(1)}, u32[]{:S(2)}, u32[]{:S(2)}) collective-permute-start(f32[6,1280]{1,0:T(8,128)S(1)} %get-tuple-element.32), channel_id=1, source_target_pairs={{0,512},{128,640},{256,0},{384,128},{512,256},{640,384},{1,513},{1... | collective-permute-start | bytes 92168 | tf_op jit(solution)/shard_map/ppermute | solution.py:34
  206.0 8.3 %collective-permute-start.35 = (f32[6,1280]{1,0:T(8,128)S(1)}, f32[6,1280]{1,0:T(8,128)S(1)}, u32[]{:S(2)}, u32[]{:S(2)}) collective-permute-start(f32[6,1280]{1,0:T(8,128)S(1)} %get-tuple-element.31), channel_id=1, source_target_pairs={{0,640},{128,0},{256,128},{384,256},{512,384},{640,512},{1,641},{1... | collective-permute-start | bytes 92168 | tf_op jit(solution)/shard_map/ppermute | solution.py:34
  208.0 18.2 %collective-permute-start.17 = (f32[18,1536]{1,0:T(8,128)S(1)}, f32[18,1536]{1,0:T(8,128)S(1)}, u32[]{:S(2)}, u32[]{:S(2)}) collective-permute-start(f32[18,1536]{1,0:T(8,128)S(1)} %dynamic-slice_bitcast_fusion), channel_id=1, source_target_pairs={{0,1},{1,0},{2,3},{3,2},{4,5},{5,4},{6,7},{7,6},{8,9},{9,8},{10,11... | collective-permute-start | bytes 331784 | tf_op jit(solution)/shard_map/ppermute | solution.py:34

commit v2 on v0

v2 whole, which is shorter than its diff:
```python
import jax
import jax.numpy as jnp
from jax import lax
from jax.sharding import Mesh
from jax.sharding import PartitionSpec as P

NV = 1000
TILE = 256
AB = ("zl", "x", "core")
CD = ("y", "zh")


def window(table, first, count):
    spans = (count + NV - 1) // NV + 1
    start = first % NV
    heads = lax.dynamic_slice_in_dim(table, first // NV, spans, 0)
    step = (start + jnp.arange(count, dtype=jnp.int32)) // NV
    left = jnp.where(step == 0, heads[0], heads[spans - 1])
    for j in range(1, spans - 1):
        left = jnp.where(step == j, heads[j], left)
    right = lax.dynamic_slice_in_dim(jnp.concatenate([table] * (spans + 1)), start, count, 0)
    return left, right


def send(block, axis, pairs):
    return lax.ppermute(block, axis, pairs)


def shift(size, by):
    return [(i, (i + by) % size) for i in range(size)]


def pick(source, rows):
    chosen = (rows[:, None] == jnp.arange(source.shape[0], dtype=jnp.int32)[None, :]).astype(source.dtype)
    return jnp.dot(chosen, source, preferred_element_type=jnp.float32).astype(source.dtype)


def pad_rows(block, count):
    return jnp.pad(block, ((0, count - block.shape[0]), (0, 0)))


def local(integrals, tile_mask, virt_irrep, occ_pairs, virt_energy, occ_energy, amp_ab, amp_cd):
    rows_dev = integrals.shape[0]
    cols_dev = integrals.shape[1]
    nzl, nx, ncore, ny, nzh = (lax.axis_size(a) for a in ("zl", "x", "core", "y", "zh"))
    zl, x, core, y, zh = (lax.axis_index(a) for a in ("zl", "x", "core", "y", "zh"))
    row_group = (zl * nx + x) * ncore + core
    col_group = y * nzh + zh
    nab = rows_dev * nzl * nx * ncore
    cd_count = amp_cd.shape[0]
    ab_count = amp_ab.shape[0]
    y_rows = nzh * ab_count
    y_pad = 40
    x_rows = nzl * cd_count
    x_pad = 40

    other = send(amp_ab, "zh", shift(nzh, 1))

    own = pad_rows(amp_cd, 8)
    own = jnp.concatenate([own, send(own, "zl", [(i, i ^ 1) for i in range(nzl)])], axis=0)
    own = jnp.concatenate([own] + [send(own, "zl", shift(nzl, -s)) for s in (2, 4)], axis=0)

    row_first = row_group * rows_dev
    col_first = nab + col_group * cols_dev
    left, right = window(virt_irrep, row_first, rows_dev)
    row_irrep = jnp.bitwise_xor(left, right)
    left, right = window(virt_irrep, col_first, cols_dev)
    col_irrep = jnp.bitwise_xor(left, right)
    tiles = jnp.repeat(tile_mask, TILE, axis=1)
    col_code = jnp.where(tiles == 1, col_irrep[None, :], -1)
    keep = row_irrep.reshape(-1, TILE)[:, :, None] == col_code[:, None, :]
    blocks = integrals.reshape(-1, TILE, cols_dev)
    masked = jnp.where(keep, blocks, jnp.zeros_like(blocks)).reshape(rows_dev, cols_dev)

    all_cd = lax.all_gather(own, ("x", "core"), axis=0, tiled=True)

    first = jnp.where(zh == 0, amp_ab, other)
    second = jnp.where(zh == 0, other, amp_ab)
    both = pad_rows(jnp.concatenate([first, second], axis=0), y_pad)
    all_ab = lax.all_gather(both, "y", axis=0, tiled=True)

    out = jnp.arange(ny * y_pad, dtype=jnp.int32)
    r = out % y_pad
    to_zh = (zh + 1 + r // ab_count) % nzh
    k = ((out // y_pad) * nzh + to_zh) * ab_count + r % ab_count
    group = k // cd_count
    z = group // (nx * ncore)
    place = (group % (nx * ncore)) * nzl + (z // 2 - zl // 2) % (nzl // 2) * 2 + (z - zl) % 2
    amp = pick(all_cd, jnp.where(r < y_rows, place * 8 + k % cd_count, -1))
    partial_ab = lax.dot_general(amp, masked, (((1,), (1,)), ((), ())), preferred_element_type=jnp.float32)
    partial_ab = partial_ab.reshape(ny, y_pad, rows_dev)

    out = jnp.arange(ncore * nx * x_pad, dtype=jnp.int32)
    r = out % x_pad
    to_x = (out // x_pad) % nx
    to_core = (core + out // (x_pad * nx)) % ncore
    k = ((r // cd_count * nx + to_x) * ncore + to_core) * cd_count + r % cd_count
    amp = pick(all_ab, jnp.where(r < x_rows, k // y_rows * y_pad + k % y_rows, -1))
    partial_cd = jnp.dot(amp, masked, preferred_element_type=jnp.float32)

    total = lax.psum_scatter(partial_ab, "y", scatter_dimension=0, tiled=False)
    ladder_ab = total[ab_count:y_rows] + send(total[:ab_count], "zh", shift(nzh, 1))

    half = nx * x_pad
    total = partial_cd[:half] + send(partial_cd[half:], "core", shift(ncore, 1))
    total = jnp.sum(lax.all_to_all(total.reshape(nx, x_pad, cols_dev), "x", 0, 0), axis=0)
    total = total[:x_rows].reshape(nzl, cd_count, cols_dev)
    ladder_cd = jnp.sum(lax.all_to_all(total, "zl", 0, 0), axis=0)

    places = jnp.concatenate(
        [
            lax.dynamic_slice_in_dim(occ_pairs, col_group * ab_count, ab_count, 1),
            lax.dynamic_slice_in_dim(occ_pairs, row_group * cd_count, cd_count, 1),
        ],
        axis=1,
    )
    equal = places[:, :, None] == jnp.arange(occ_energy.shape[0], dtype=jnp.int32)[None, None, :]
    occ = jnp.sum(jnp.where(equal, occ_energy[None, None, :], 0.0), axis=2)
    occ = occ[0] + occ[1]
    left, right = window(virt_energy, row_first, rows_dev)
    update_ab = ladder_ab / ((left + right)[None, :] - occ[:ab_count, None])
    left, right = window(virt_energy, col_first, cols_dev)
    update_cd = ladder_cd / ((left + right)[None, :] - occ[ab_count:, None])
    return (update_ab, update_cd)


def solution(mesh):
    fine = Mesh(mesh.devices.reshape(6, 4, 2, 8, 2), AB + CD)
    return jax.shard_map(
        local,
        mesh=fine,
        in_specs=(P(AB, CD), P(AB, CD), P(), P(), P(), P(), P(CD, AB), P(AB, CD)),
        out_specs=(P(CD, AB), P(AB, CD)),
        check_vma=False,
    )
```

time: 603 us -> 167 us (0.28); the launches traced: 595 us -> 166 us
  blocking collectives: 516 us -> 40.3 us
  waiting for transfers between devices: 3.69 us -> 33.5 us
  between operations: 2.45 us -> 14.4 us
  starting transfers between devices: 41 us -> 48.7 us
  local copies, waits for them, and re-layouts: 13.7 us -> 6.11 us
    unnamed x2 -> x0, blocking collectives: 317 us -> none
    all_gather x2, blocking collectives: 199 us -> 40.3 us  [the longest x1 24.6 us: local(): all_ab = lax.all_gather(both, 'y', axis=0, tiled=True)]
    unnamed x16 -> x0, starting transfers between devices: 41 us -> none
    ppermute x0 -> x6, starting transfers between devices: none -> 38.9 us  [send(): return lax.ppermute(block, axis, pairs)]
    all_to_all x0 -> x2, waiting for transfers between devices: none -> 19.5 us  [the longest x1 10.5 us: local(): ladder_cd = jnp.sum(lax.all_to_all(total, 'zl', 0, 0), axis=0)]
    ppermute x0 -> x6, waiting for transfers between devices: none -> 13.9 us  [send(): return lax.ppermute(block, axis, pairs)]
    unnamed x27 -> x10, local copies, waits for them, and re-layouts: 13.5 us -> 0.03 us
    all_to_all x0 -> x2, starting transfers between devices: none -> 9.82 us  [the longest x1 5.82 us: local(): ladder_cd = jnp.sum(lax.all_to_all(total, 'zl', 0, 0), axis=0)]
  transfers between devices with their start and end apart: 16 -> 9, of which waited for: 2 -> 4; matrix products, arithmetic and copies ran while one was open for 28% -> 16% of each run, Pallas kernels for 0% -> 0%
where the time goes in v2:
time: 167 us; the launch traced here: 166 us
  starting transfers between devices  48.7 us (29%)
  blocking collectives  40.3 us (24%)
  waiting for transfers between devices  33.5 us (20%)
  other arithmetic  15.5 us (9%)
  between operations  14.4 us (9%)
  matrix products  7.73 us (5%)
  local copies, waits for them, and re-layouts  6.11 us (4%)
    ppermute x6, starting transfers between devices, send(): return lax.ppermute(block, axis, pairs)  38.9 us
    all_gather x1, blocking collectives, local(): all_ab = lax.all_gather(both, 'y', axis=0, tiled=True)  24.6 us
    all_gather x1, blocking collectives, local(): all_cd = lax.all_gather(own, ('x', 'core'), axis=0, tiled=True)  15.7 us
    ppermute x6, waiting for transfers between devices, send(): return lax.ppermute(block, axis, pairs)  13.9 us
    all_to_all x1, waiting for transfers between devices, local(): ladder_cd = jnp.sum(lax.all_to_all(total, 'zl', 0, 0), axis=0)  10.5 us
    all_to_all x1, waiting for transfers between devices, local(): lax.all_to_all(total.reshape(nx, x_pad, cols_dev), 'x', 0, 0)  9.06 us
    all_to_all x1, starting transfers between devices, local(): ladder_cd = jnp.sum(lax.all_to_all(total, 'zl', 0, 0), axis=0)  5.82 us
    dot_general x1, matrix products, local(): partial_cd = jnp.dot(amp, masked, preferred_element_type=jnp.float32)  4.27 us
  transfers between devices with their start and end apart: 9, of which 4 were waited for; matrix products, arithmetic and copies ran while one was open for 16% of the time, Pallas kernels for 0%

profile of v2, /device:TPU:1, one launch (start us, length us, event | category | flops | bytes accessed | tf_op | source)
XLA Modules:
  0.0 166.2 jit_solution(245832637723722516)
XLA Ops:
  7.2 0.0 copy-start
  7.2 0.0 reduce-scatter.2.cloned.1.call-start
  7.2 0.7 pad.8
  8.0 4.8 %collective-permute-start = (bf16[8,1280]{1,0:T(8,128)(2,1)S(1)}, bf16[8,1280]{1,0:T(8,128)(2,1)S(1)}, u32[]{:S(2)}, u32[]{:S(2)}) collective-permute-start(bf16[8,1280]{1,0:T(8,128)(2,1)S(1)} %pad.8), channel_id=1, source_target_pairs={{0,128},{128,0},{256,384},{384,256},{512,640},{640,512},{1,129},{1... | collective-permute-start | bytes 61448 | tf_op jit(solution)/shard_map/ppermute | solution.py:26
  12.8 14.6 %collective-permute-start.4 = (bf16[18,1536]{1,0:T(8,128)(2,1)}, bf16[18,1536]{1,0:T(8,128)(2,1)S(1)}, u32[]{:S(2)}, u32[]{:S(2)}) collective-permute-start(bf16[18,1536]{1,0:T(8,128)(2,1)} %param.14), channel_id=1, source_target_pairs={{0,1},{1,0},{2,3},{3,2},{4,5},{5,4},{6,7},{7,6},{8,9},{9,8},{10,11... | collective-permute-start | bytes 165896 | tf_op jit(solution)/shard_map/ppermute | solution.py:26
  27.4 0.7 broadcast_compare_fusion.4
  28.1 0.1 copy.11
  28.2 0.9 concatenate.23
  29.2 0.8 fusion.54
  30.0 0.7 fusion.57
  30.7 1.9 %dynamic-slice_xor_fusion = s32[1280]{0:T(1024)S(1)} fusion(s32[4000]{0:T(1024)S(1)} %concatenate.23, s32[]{:T(128)S(6)} %select_n.333, s32[]{:T(128)} %bitcast.7, s32[]{:T(128)} %bitcast.6, s32[]{:T(128)} %bitcast.5, s32[]{:T(128)S(6)} %select_n.327), kind=kLoop, calls=%fused_computation.32 | loop fusion | flops 17920 | bytes 10260 | tf_op jit(solution)/shard_map/xor | solution.py:68
  32.6 0.1 broadcast_in_dim.97
  32.6 2.0 %dynamic-slice_xor_fusion.1 = s32[1536]{0:T(1024)S(1)} fusion(s32[4000]{0:T(1024)S(1)} %concatenate.23, s32[]{:T(128)S(6)} %select_n.326, s32[]{:T(128)} %bitcast.3, s32[]{:T(128)} %bitcast.2, s32[]{:T(128)} %bitcast.1, s32[]{:T(128)S(6)} %select_n.320), kind=kLoop, calls=%fused_computation.36 | loop fusion | flops 21504 | bytes 12308 | tf_op jit(solution)/shard_map/xor | solution.py:66
  34.7 2.8 %collective-permute-start.2 = (bf16[16,1280]{1,0:T(8,128)(2,1)S(1)}, bf16[16,1280]{1,0:T(8,128)(2,1)S(1)}, u32[]{:S(2)}, u32[]{:S(2)}) collective-permute-start(bf16[16,1280]{1,0:T(8,128)(2,1)S(1)} %pad_maximum_fusion.1), channel_id=1, source_target_pairs={{0,256},{128,384},{256,512},{384,640},{512,0},{640,128},{1,257},{1... | collective-permute-start | bytes 122888 | tf_op jit(solution)/shard_map/ppermute | solution.py:26
  37.5 6.4 %collective-permute-start.1 = (bf16[16,1280]{1,0:T(8,128)(2,1)S(1)}, bf16[16,1280]{1,0:T(8,128)(2,1)S(1)}, u32[]{:S(2)}, u32[]{:S(2)}) collective-permute-start(bf16[16,1280]{1,0:T(8,128)(2,1)S(1)} %pad_maximum_fusion.1), channel_id=1, source_target_pairs={{0,512},{128,640},{256,0},{384,128},{512,256},{640,384},{1,513},{1... | collective-permute-start | bytes 122888 | tf_op jit(solution)/shard_map/ppermute | solution.py:26
  43.9 0.1 fusion.25
  44.0 3.1 %fusion = bf16[1536,1280]{1,0:T(8,128)(2,1)S(1)} fusion(bf16[1536,1280]{1,0:T(8,128)(2,1)} %param.8, s32[6,1280]{1,0:T(8,128)S(1)} %broadcast_select_fusion.2, s32[1536]{0:T(1024)S(1)} %dynamic-slice_xor_fusion.1), kind=kLoop, calls=%fused_computation.1 | loop fusion | flops 3932160 | bytes 7901184 | tf_op jit(solution)/shard_map/jit(_where)/select_n | solution.py:73
  47.1 15.7 %all_gather.6 = bf16[384,1280]{1,0:T(8,128)(2,1)S(1)} all-gather(bf16[48,1280]{1,0:T(8,128)(2,1)S(1)} %pad_maximum_fusion), channel_id=1, replica_groups=mesh['zl'=6,'x'=4,'core'=2,'y'=8,'zh'=2] {'x','core'}, dimensions={0}, use_global_device_ids=true | all-gather | bytes 1105920 | tf_op jit(solution)/shard_map/all_gather | solution.py:75
  62.9 0.6 convolution_convert_fusion.1
  63.5 2.8 %fusion.1 = f32[8,40,1536]{2,1,0:T(8,128)} fusion(bf16[8,40,1280]{2,1,0:T(8,128)(2,1)S(1)} %bitcast.40, bf16[1536,1280]{1,0:T(8,128)(2,1)S(1)} %fusion), kind=kOutput, calls=%fused_computation.2 | convolution fusion | flops 1258291200 | bytes 6717440 | tf_op jit(solution)/shard_map/dot_general | solution.py:90
  66.3 0.0 reduce-scatter.2.cloned.1.call-update
  66.5 24.6 %all_gather.7 = bf16[320,1536]{1,0:T(8,128)(2,1)S(1)} all-gather(bf16[40,1536]{1,0:T(8,128)(2,1)S(1)} %fusion.11), channel_id=1, replica_groups=mesh['zl'=6,'x'=4,'core'=2,'y'=8,'zh'=2] {'y'}, dimensions={0}, use_global_device_ids=true | all-gather | bytes 1105920 | tf_op jit(solution)/shard_map/all_gather | solution.py:80
  91.0 4.3 %fusion.3 = f32[320,1280]{1,0:T(8,128)S(1)} fusion(bf16[1536,1280]{1,0:T(8,128)(2,1)} %copy-done.1, bf16[320,1536]{1,0:T(8,128)(2,1)S(1)} %all_gather.7, s32[320]{0:T(512)S(1)} %fusion.40), kind=kOutput, calls=%fused_computation.6 | convolution fusion | flops 1573457920 | bytes 6554880 | tf_op jit(solution)/shard_map/dot_general | solution.py:99
  95.3 0.1 slice.103
  95.4 7.1 %collective-permute-start.5 = (f32[160,1280]{1,0:T(8,128)S(1)}, f32[160,1280]{1,0:T(8,128)S(1)}, u32[]{:S(2)}, u32[]{:S(2)}) collective-permute-start(f32[160,1280]{1,0:T(8,128)S(1)} %slice.103), channel_id=1, source_target_pairs={{0,16},{16,0},{1,17},{17,1},{2,18},{18,2},{3,19},{19,3},{4,20},{20... | collective-permute-start | bytes 2457608 | tf_op jit(solution)/shard_map/ppermute | solution.py:26
  102.5 0.1 constant_dynamic-slice_fusion
  102.6 0.1 constant_dynamic-slice_fusion.1
  102.6 0.1 fusion.53
  102.7 1.7 %collective-permute-done.5 = f32[160,1280]{1,0:T(8,128)S(1)} collective-permute-done((f32[160,1280]{1,0:T(8,128)S(1)}, f32[160,1280]{1,0:T(8,128)S(1)}, u32[]{:S(2)}, u32[]{:S(2)}) %collective-permute-start.5) | collective-permute-done | bytes 819232 | tf_op jit(solution)/shard_map/ppermute | solution.py:26
  104.4 1.0 slice_add_fusion
  105.4 4.0 %all-to-all-start = ((f32[4,40,1280]{2,1,0:T(8,128)}), f32[4,40,1280]{2,1,0:T(8,128)S(1)}, u32[]{:S(2)}, u32[]{:S(2)}) async-start(f32[4,40,1280]{2,1,0:T(8,128)} %bitcast.16), calls=%async_computation.1 | async-start | bytes 1638400 | tf_op jit(solution)/shard_map/all_to_all | solution.py:106
  109.4 0.1 pad_add_fusion
  109.5 0.1 concatenate.24
  109.6 0.7 fusion.55
  110.2 2.0 %dynamic-slice_add_fusion.1 = f32[1536]{0:T(1024)S(1)} fusion(f32[4000]{0:T(1024)S(1)} %concatenate.24, s32[]{:T(128)S(6)} %select_n.326, f32[]{:T(128)} %bitcast.14, f32[]{:T(128)} %bitcast.13, f32[]{:T(128)} %bitcast.12, s32[]{:T(128)S(6)} %select_n.320), kind=kLoop, calls=%fused_computation.31 | loop fusion | flops 21504 | bytes 12308 | tf_op jit(solution)/shard_map/add | solution.py:121
  112.2 0.2 select_reduce_fusion
  112.4 9.1 %all-to-all-done = f32[4,40,1280]{2,1,0:T(8,128)S(1)} async-done(((f32[4,40,1280]{2,1,0:T(8,128)}), f32[4,40,1280]{2,1,0:T(8,128)S(1)}, u32[]{:S(2)}, u32[]{:S(2)}) %all-to-all-start) | async-done | bytes 819232 | tf_op jit(solution)/shard_map/all_to_all | solution.py:106
  121.5 0.7 reshape.241
  122.2 5.8 %all-to-all-start.1 = ((f32[6,6,1280]{2,1,0:T(8,128)}), f32[6,6,1280]{2,1,0:T(8,128)S(1)}, u32[]{:S(2)}, u32[]{:S(2)}) async-start(f32[6,6,1280]{2,1,0:T(8,128)} %reshape.241), calls=%async_computation.2 | async-start | bytes 491520 | tf_op jit(solution)/shard_map/all_to_all | solution.py:108
  128.1 1.9 %dynamic-slice_add_fusion = f32[1280]{0:T(1024)S(1)} fusion(f32[4000]{0:T(1024)S(1)} %concatenate.24, s32[]{:T(128)S(6)} %select_n.333, f32[]{:T(128)} %bitcast.19, f32[]{:T(128)} %bitcast.18, f32[]{:T(128)} %bitcast.17, s32[]{:T(128)S(6)} %select_n.327), kind=kLoop, calls=%fused_computation.30 | loop fusion | flops 17920 | bytes 10260 | tf_op jit(solution)/shard_map/add | solution.py:123
  130.0 0.1 slice_bitcast_fusion.2
  130.1 10.5 %all-to-all-done.1 = f32[6,6,1280]{2,1,0:T(8,128)S(1)} async-done(((f32[6,6,1280]{2,1,0:T(8,128)}), f32[6,6,1280]{2,1,0:T(8,128)S(1)}, u32[]{:S(2)}, u32[]{:S(2)}) %all-to-all-start.1) | async-done | bytes 184352 | tf_op jit(solution)/shard_map/all_to_all | solution.py:108
  140.6 0.0 reduce-scatter.2.cloned.1.call-done
  140.6 0.9 slice_bitcast_fusion
  141.5 3.2 %collective-permute-start.3 = (f32[18,1536]{1,0:T(8,128)S(1)}, f32[18,1536]{1,0:T(8,128)S(1)}, u32[]{:S(2)}, u32[]{:S(2)}) collective-permute-start(f32[18,1536]{1,0:T(8,128)S(1)} %slice_bitcast_fusion), channel_id=1, source_target_pairs={{0,1},{1,0},{2,3},{3,2},{4,5},{5,4},{6,7},{7,6},{8,9},{9,8},{10,11... | collective-permute-start | bytes 331784 | tf_op jit(solution)/shard_map/ppermute | solution.py:26
  144.8 0.7 subtract_divide_fusion
  145.5 12.2 %collective-permute-done.3 = f32[18,1536]{1,0:T(8,128)S(1)} collective-permute-done((f32[18,1536]{1,0:T(8,128)S(1)}, f32[18,1536]{1,0:T(8,128)S(1)}, u32[]{:S(2)}, u32[]{:S(2)}) %collective-permute-start.3) | collective-permute-done | bytes 110624 | tf_op jit(solution)/shard_map/ppermute | solution.py:26
  157.7 1.7 %fusion.10 = f32[18,1536]{1,0:T(8,128)} fusion(f32[18,1536]{1,0:T(8,128)S(1)} %collective-permute-done.3, f32[1,40,1536]{2,1,0:T(8,128)} %reduce-scatter.2.cloned.1.call-done, f32[18]{0:T(128)S(1)} %slice_bitcast_fusion.3, f32[1536]{0:T(1024)S(1)} %dynamic-slice_add_fusion.1), kind=kLoop, calls=%fused_computation.18 | loop fusion | flops 82944 | bytes 337992 | tf_op jit(solution)/shard_map/div | solution.py:121
  (23 shorter events, 0.2 us)
Async XLA Ops:
  7.2 95.3 %copy-start = (s32[2,288]{1,0:T(2,128)S(1)}, s32[2,288]{1,0:T(2,128)}, u32[]{:S(2)}) copy-start(s32[2,288]{1,0:T(2,128)} %param.11) | copy-start | bytes 6916
  7.2 133.4 %reduce-scatter.2.cloned.1.call-start = ((), (), s32[]{:S(2)}) async-start(), calls=%async_computation.3 | async-start | bytes 2211840 | tf_op jit(solution)/shard_map/reduce_scatter | solution.py:101
  8.0 26.7 %collective-permute-start = (bf16[8,1280]{1,0:T(8,128)(2,1)S(1)}, bf16[8,1280]{1,0:T(8,128)(2,1)S(1)}, u32[]{:S(2)}, u32[]{:S(2)}) collective-permute-start(bf16[8,1280]{1,0:T(8,128)(2,1)S(1)} %pad.8), channel_id=1, source_target_pairs={{0,128},{128,0},{256,384},{384,256},{512,640},{640,512},{1,129},{1... | collective-permute-start | bytes 61448 | tf_op jit(solution)/shard_map/ppermute | solution.py:26
  12.8 53.6 %collective-permute-start.4 = (bf16[18,1536]{1,0:T(8,128)(2,1)}, bf16[18,1536]{1,0:T(8,128)(2,1)S(1)}, u32[]{:S(2)}, u32[]{:S(2)}) collective-permute-start(bf16[18,1536]{1,0:T(8,128)(2,1)} %param.14), channel_id=1, source_target_pairs={{0,1},{1,0},{2,3},{3,2},{4,5},{5,4},{6,7},{7,6},{8,9},{9,8},{10,11... | collective-permute-start | bytes 165896 | tf_op jit(solution)/shard_map/ppermute | solution.py:26
  34.7 12.4 %collective-permute-start.2 = (bf16[16,1280]{1,0:T(8,128)(2,1)S(1)}, bf16[16,1280]{1,0:T(8,128)(2,1)S(1)}, u32[]{:S(2)}, u32[]{:S(2)}) collective-permute-start(bf16[16,1280]{1,0:T(8,128)(2,1)S(1)} %pad_maximum_fusion.1), channel_id=1, source_target_pairs={{0,256},{128,384},{256,512},{384,640},{512,0},{640,128},{1,257},{1... | collective-permute-start | bytes 122888 | tf_op jit(solution)/shard_map/ppermute | solution.py:26
  37.5 9.6 %collective-permute-start.1 = (bf16[16,1280]{1,0:T(8,128)(2,1)S(1)}, bf16[16,1280]{1,0:T(8,128)(2,1)S(1)}, u32[]{:S(2)}, u32[]{:S(2)}) collective-permute-start(bf16[16,1280]{1,0:T(8,128)(2,1)S(1)} %pad_maximum_fusion.1), channel_id=1, source_target_pairs={{0,512},{128,640},{256,0},{384,128},{512,256},{640,384},{1,513},{1... | collective-permute-start | bytes 122888 | tf_op jit(solution)/shard_map/ppermute | solution.py:26
  47.1 16.4 %copy-start.1 = (bf16[1536,1280]{1,0:T(8,128)(2,1)}, bf16[1536,1280]{1,0:T(8,128)(2,1)S(1)}, u32[]{:S(2)}) copy-start(bf16[1536,1280]{1,0:T(8,128)(2,1)S(1)} %fusion) | copy-start | bytes 11796484
  63.5 2.9 %copy-start.3 = (bf16[18,1536]{1,0:T(8,128)(2,1)S(1)}, bf16[18,1536]{1,0:T(8,128)(2,1)}, u32[]{:S(2)}) copy-start(bf16[18,1536]{1,0:T(8,128)(2,1)} %param.14) | copy-start | bytes 165892
  91.0 11.6 %copy-start.2 = (f32[1000]{0:T(1024)S(1)}, f32[1000]{0:T(1024)}, u32[]{:S(2)}) copy-start(f32[1000]{0:T(1024)} %param.12) | copy-start | bytes 12004
  95.3 16.9 %copy-start.4 = (f32[100]{0:T(128)S(1)}, f32[100]{0:T(128)}, u32[]{:S(2)}) copy-start(f32[100]{0:T(128)} %param.13) | copy-start | bytes 1204
  95.4 9.0 %collective-permute-start.5 = (f32[160,1280]{1,0:T(8,128)S(1)}, f32[160,1280]{1,0:T(8,128)S(1)}, u32[]{:S(2)}, u32[]{:S(2)}) collective-permute-start(f32[160,1280]{1,0:T(8,128)S(1)} %slice.103), channel_id=1, source_target_pairs={{0,16},{16,0},{1,17},{17,1},{2,18},{18,2},{3,19},{19,3},{4,20},{20... | collective-permute-start | bytes 2457608 | tf_op jit(solution)/shard_map/ppermute | solution.py:26
  105.4 16.1 %all-to-all-start = ((f32[4,40,1280]{2,1,0:T(8,128)}), f32[4,40,1280]{2,1,0:T(8,128)S(1)}, u32[]{:S(2)}, u32[]{:S(2)}) async-start(f32[4,40,1280]{2,1,0:T(8,128)} %bitcast.16), calls=%async_computation.1 | async-start | bytes 1638400 | tf_op jit(solution)/shard_map/all_to_all | solution.py:106
  122.2 18.3 %all-to-all-start.1 = ((f32[6,6,1280]{2,1,0:T(8,128)}), f32[6,6,1280]{2,1,0:T(8,128)S(1)}, u32[]{:S(2)}, u32[]{:S(2)}) async-start(f32[6,6,1280]{2,1,0:T(8,128)} %reshape.241), calls=%async_computation.2 | async-start | bytes 491520 | tf_op jit(solution)/shard_map/all_to_all | solution.py:108
  141.5 16.2 %collective-permute-start.3 = (f32[18,1536]{1,0:T(8,128)S(1)}, f32[18,1536]{1,0:T(8,128)S(1)}, u32[]{:S(2)}, u32[]{:S(2)}) collective-permute-start(f32[18,1536]{1,0:T(8,128)S(1)} %slice_bitcast_fusion), channel_id=1, source_target_pairs={{0,1},{1,0},{2,3},{3,2},{4,5},{5,4},{6,7},{7,6},{8,9},{9,8},{10,11... | collective-permute-start | bytes 331784 | tf_op jit(solution)/shard_map/ppermute | solution.py:26
Sparse Core Ops, SparseCore 0:
  66.5 42.0 reduce-scatter.1

commit v3 on v2

--- a/solution.py
+++ b/solution.py
@@ -28,6 +28,10 @@
 
 def shift(size, by):
     return [(i, (i + by) % size) for i in range(size)]
+
+
+def gather(block, axis, size):
+    return lax.all_to_all(jnp.broadcast_to(block[None], (size,) + block.shape), axis, 0, 0)
 
 
 def pick(source, rows):
@@ -77,7 +81,7 @@
     first = jnp.where(zh == 0, amp_ab, other)
     second = jnp.where(zh == 0, other, amp_ab)
     both = pad_rows(jnp.concatenate([first, second], axis=0), y_pad)
-    all_ab = lax.all_gather(both, "y", axis=0, tiled=True)
+    all_ab = gather(both, "y", ny).reshape(ny * y_pad, rows_dev)
 
     out = jnp.arange(ny * y_pad, dtype=jnp.int32)
     r = out % y_pad
@@ -98,12 +102,13 @@
     amp = pick(all_ab, jnp.where(r < x_rows, k // y_rows * y_pad + k % y_rows, -1))
     partial_cd = jnp.dot(amp, masked, preferred_element_type=jnp.float32)
 
-    total = lax.psum_scatter(partial_ab, "y", scatter_dimension=0, tiled=False)
-    ladder_ab = total[ab_count:y_rows] + send(total[:ab_count], "zh", shift(nzh, 1))
+    total_ab = lax.psum_scatter(partial_ab, "y", scatter_dimension=0, tiled=False)
 
     half = nx * x_pad
     total = partial_cd[:half] + send(partial_cd[half:], "core", shift(ncore, 1))
     total = jnp.sum(lax.all_to_all(total.reshape(nx, x_pad, cols_dev), "x", 0, 0), axis=0)
+    total, total_ab = lax.optimization_barrier((total, total_ab))
+    ladder_ab = total_ab[ab_count:y_rows] + send(total_ab[:ab_count], "zh", shift(nzh, 1))
     total = total[:x_rows].reshape(nzl, cd_count, cols_dev)
     ladder_cd = jnp.sum(lax.all_to_all(total, "zl", 0, 0), axis=0)
 

time: 167 us -> 158 us (0.946)
  the two profiles are of different devices: /device:TPU:1 before, /device:TPU:4 now
where the time goes in v3:
time: 158 us; the launch traced here: 157 us
  starting transfers between devices  55 us (35%)
  waiting for transfers between devices  41.3 us (26%)
  other arithmetic  17.3 us (11%)
  between operations  14.3 us (9%)
  blocking collectives  12.5 us (8%)
  matrix products  9.76 us (6%)
  local copies, waits for them, and re-layouts  7.13 us (5%)
    ppermute x6, starting transfers between devices, send(): return lax.ppermute(block, axis, pairs)  39.6 us
    reduce_scatter x1, waiting for transfers between devices, local(): lax.psum_scatter(partial_ab, 'y', scatter_dimension=0, tiled=False)  14.5 us
    all_gather x1, blocking collectives, local(): all_cd = lax.all_gather(own, ('x', 'core'), axis=0, tiled=True)  12.5 us
    all_to_all x1, waiting for transfers between devices, local(): ladder_cd = jnp.sum(lax.all_to_all(total, 'zl', 0, 0), axis=0)  8.74 us
    all_to_all x1, waiting for transfers between devices, gather(): lax.all_to_all(jnp.broadcast_to(block[None], (size,) + block.shape), axis...  8.27 us
    all_to_all x1, waiting for transfers between devices, local(): lax.all_to_all(total.reshape(nx, x_pad, cols_dev), 'x', 0, 0)  7.21 us
    all_to_all x1, starting transfers between devices, gather(): lax.all_to_all(jnp.broadcast_to(block[None], (size,) + block.shape), axis...  7.1 us
    select_n x1, other arithmetic, local(): jnp.where(keep, blocks, jnp.zeros_like(blocks)).reshape(rows_dev, cols_dev)  4.98 us
  transfers between devices with their start and end apart: 10, of which 6 were waited for; matrix products, arithmetic and copies ran while one was open for 21% of the time, Pallas kernels for 0%

profile of v3, /device:TPU:4, one launch (start us, length us, event | category | flops | bytes accessed | tf_op | source)
XLA Modules:
  0.0 157.3 jit_solution(913423096626761751)
XLA Ops:
  7.2 15.1 %collective-permute-start = (bf16[18,1536]{1,0:T(8,128)(2,1)}, bf16[18,1536]{1,0:T(8,128)(2,1)S(1)}, u32[]{:S(2)}, u32[]{:S(2)}) collective-permute-start(bf16[18,1536]{1,0:T(8,128)(2,1)} %param.14), channel_id=1, source_target_pairs={{0,1},{1,0},{2,3},{3,2},{4,5},{5,4},{6,7},{7,6},{8,9},{9,8},{10,11... | collective-permute-start | bytes 165896 | tf_op jit(solution)/shard_map/ppermute | solution.py:26
  22.3 0.7 pad.9
  23.1 3.4 %collective-permute-start.2 = (bf16[8,1280]{1,0:T(8,128)(2,1)S(1)}, bf16[8,1280]{1,0:T(8,128)(2,1)S(1)}, u32[]{:S(2)}, u32[]{:S(2)}) collective-permute-start(bf16[8,1280]{1,0:T(8,128)(2,1)S(1)} %pad.9), channel_id=1, source_target_pairs={{0,128},{128,0},{256,384},{384,256},{512,640},{640,512},{1,129},{1... | collective-permute-start | bytes 61448 | tf_op jit(solution)/shard_map/ppermute | solution.py:26
  26.5 0.9 concatenate.22
  27.4 0.7 broadcast_compare_fusion.4
  28.1 0.1 copy.11
  28.3 0.8 fusion.52
  29.1 0.7 fusion.55
  29.7 1.9 %dynamic-slice_xor_fusion = s32[1280]{0:T(1024)S(1)} fusion(s32[4000]{0:T(1024)S(1)} %concatenate.22, s32[]{:T(128)S(6)} %select_n.332, s32[]{:T(128)} %bitcast.7, s32[]{:T(128)} %bitcast.6, s32[]{:T(128)} %bitcast.5, s32[]{:T(128)S(6)} %select_n.326), kind=kLoop, calls=%fused_computation.29 | loop fusion | flops 17920 | bytes 10260 | tf_op jit(solution)/shard_map/xor | solution.py:72
  31.6 0.1 broadcast_in_dim.104
  31.7 2.0 %dynamic-slice_xor_fusion.1 = s32[1536]{0:T(1024)S(1)} fusion(s32[4000]{0:T(1024)S(1)} %concatenate.22, s32[]{:T(128)S(6)} %select_n.325, s32[]{:T(128)} %bitcast.3, s32[]{:T(128)} %bitcast.2, s32[]{:T(128)} %bitcast.1, s32[]{:T(128)S(6)} %select_n.319), kind=kLoop, calls=%fused_computation.33 | loop fusion | flops 21504 | bytes 12308 | tf_op jit(solution)/shard_map/xor | solution.py:70
  33.7 0.1 fusion.33
  33.8 5.0 %fusion = bf16[1536,1280]{1,0:T(8,128)(2,1)} fusion(bf16[1536,1280]{1,0:T(8,128)(2,1)} %param.8, s32[6,1280]{1,0:T(8,128)S(1)} %broadcast_select_fusion.2, s32[1536]{0:T(1024)S(1)} %dynamic-slice_xor_fusion.1), kind=kLoop, calls=%fused_computation.1 | loop fusion | flops 3932160 | bytes 7901184 | tf_op jit(solution)/shard_map/jit(_where)/select_n | solution.py:77
  38.8 6.1 %collective-permute-start.3 = (bf16[16,1280]{1,0:T(8,128)(2,1)S(1)}, bf16[16,1280]{1,0:T(8,128)(2,1)S(1)}, u32[]{:S(2)}, u32[]{:S(2)}) collective-permute-start(bf16[16,1280]{1,0:T(8,128)(2,1)S(1)} %pad_maximum_fusion.1), channel_id=1, source_target_pairs={{0,512},{128,640},{256,0},{384,128},{512,256},{640,384},{1,513},{1... | collective-permute-start | bytes 122888 | tf_op jit(solution)/shard_map/ppermute | solution.py:26
  44.9 1.9 %collective-permute-start.4 = (bf16[16,1280]{1,0:T(8,128)(2,1)S(1)}, bf16[16,1280]{1,0:T(8,128)(2,1)S(1)}, u32[]{:S(2)}, u32[]{:S(2)}) collective-permute-start(bf16[16,1280]{1,0:T(8,128)(2,1)S(1)} %pad_maximum_fusion.1), channel_id=1, source_target_pairs={{0,256},{128,384},{256,512},{384,640},{512,0},{640,128},{1,257},{1... | collective-permute-start | bytes 122888 | tf_op jit(solution)/shard_map/ppermute | solution.py:26
  46.9 1.0 broadcast_in_dim.100
  48.0 7.1 %all-to-all-start = ((bf16[8,40,1536]{2,1,0:T(8,128)(2,1)}), bf16[8,40,1536]{2,1,0:T(8,128)(2,1)S(1)}, u32[]{:S(2)}, u32[]{:S(2)}) async-start(bf16[8,40,1536]{2,1,0:T(8,128)(2,1)} %broadcast_in_dim.100), calls=%async_computation | async-start | bytes 1966080 | tf_op jit(solution)/shard_map/all_to_all | solution.py:34
  55.1 0.0 reduce-scatter.2.cloned.1.call-start
  55.1 12.5 %all_gather.3 = bf16[384,1280]{1,0:T(8,128)(2,1)S(1)} all-gather(bf16[48,1280]{1,0:T(8,128)(2,1)S(1)} %pad_maximum_fusion), channel_id=1, replica_groups=mesh['zl'=6,'x'=4,'core'=2,'y'=8,'zh'=2] {'x','core'}, dimensions={0}, use_global_device_ids=true | all-gather | bytes 1105920 | tf_op jit(solution)/shard_map/all_gather | solution.py:79
  67.7 0.6 convolution_convert_fusion.1
  68.3 4.9 %fusion.1 = f32[8,40,1536]{2,1,0:T(8,128)} fusion(bf16[8,40,1280]{2,1,0:T(8,128)(2,1)S(1)} %bitcast.35, bf16[1536,1280]{1,0:T(8,128)(2,1)} %fusion), kind=kOutput, calls=%fused_computation.2 | convolution fusion | flops 1258291200 | bytes 6717440 | tf_op jit(solution)/shard_map/dot_general | solution.py:94
  73.3 8.3 %all-to-all-done = bf16[8,40,1536]{2,1,0:T(8,128)(2,1)S(1)} async-done(((bf16[8,40,1536]{2,1,0:T(8,128)(2,1)}), bf16[8,40,1536]{2,1,0:T(8,128)(2,1)S(1)}, u32[]{:S(2)}, u32[]{:S(2)}) %all-to-all-start) | async-done | bytes 983072 | tf_op jit(solution)/shard_map/all_to_all | solution.py:34
  81.5 4.2 %fusion.3 = f32[320,1280]{1,0:T(8,128)S(1)} fusion(bf16[1536,1280]{1,0:T(8,128)(2,1)} %fusion, bf16[320,1536]{1,0:T(8,128)(2,1)S(1)} %bitcast.33, s32[320]{0:T(512)S(1)} %fusion.23), kind=kOutput, calls=%fused_computation.6 | convolution fusion | flops 1573457920 | bytes 6554880 | tf_op jit(solution)/shard_map/dot_general | solution.py:103
  85.8 0.1 slice.93
  85.8 1.9 %collective-permute-start.1 = (f32[160,1280]{1,0:T(8,128)S(1)}, f32[160,1280]{1,0:T(8,128)S(1)}, u32[]{:S(2)}, u32[]{:S(2)}) collective-permute-start(f32[160,1280]{1,0:T(8,128)S(1)} %slice.93), channel_id=1, source_target_pairs={{0,16},{16,0},{1,17},{17,1},{2,18},{18,2},{3,19},{19,3},{4,20},{20... | collective-permute-start | bytes 2457608 | tf_op jit(solution)/shard_map/ppermute | solution.py:26
  87.8 0.1 fusion.51
  87.9 0.1 constant_dynamic-slice_fusion
  87.9 0.1 constant_dynamic-slice_fusion.1
  88.0 0.1 pad_add_fusion
  88.1 0.2 select_reduce_fusion
  88.3 1.8 %collective-permute-done.1 = f32[160,1280]{1,0:T(8,128)S(1)} collective-permute-done((f32[160,1280]{1,0:T(8,128)S(1)}, f32[160,1280]{1,0:T(8,128)S(1)}, u32[]{:S(2)}, u32[]{:S(2)}) %collective-permute-start.1) | collective-permute-done | bytes 819232 | tf_op jit(solution)/shard_map/ppermute | solution.py:26
  90.1 1.0 slice_add_fusion
  91.1 4.8 %all-to-all-start.1 = ((f32[4,40,1280]{2,1,0:T(8,128)}), f32[4,40,1280]{2,1,0:T(8,128)S(1)}, u32[]{:S(2)}, u32[]{:S(2)}) async-start(f32[4,40,1280]{2,1,0:T(8,128)} %bitcast.9), calls=%async_computation.1 | async-start | bytes 1638400 | tf_op jit(solution)/shard_map/all_to_all | solution.py:109
  95.9 0.7 fusion.53
  96.5 0.1 concatenate.25
  96.6 1.9 %dynamic-slice_add_fusion = f32[1280]{0:T(1024)S(1)} fusion(f32[4000]{0:T(1024)S(1)} %concatenate.25, s32[]{:T(128)S(6)} %select_n.332, f32[]{:T(128)} %bitcast.19, f32[]{:T(128)} %bitcast.18, f32[]{:T(128)} %bitcast.17, s32[]{:T(128)S(6)} %select_n.326), kind=kLoop, calls=%fused_computation.27 | loop fusion | flops 17920 | bytes 10260 | tf_op jit(solution)/shard_map/add | solution.py:128
  98.6 0.1 slice_bitcast_fusion
  98.6 7.2 %all-to-all-done.1 = f32[4,40,1280]{2,1,0:T(8,128)S(1)} async-done(((f32[4,40,1280]{2,1,0:T(8,128)}), f32[4,40,1280]{2,1,0:T(8,128)S(1)}, u32[]{:S(2)}, u32[]{:S(2)}) %all-to-all-start.1) | async-done | bytes 819232 | tf_op jit(solution)/shard_map/all_to_all | solution.py:109
  105.9 14.5 %reduce-scatter.2.cloned.1.call-done = f32[1,40,1536]{2,1,0:T(8,128)} async-done(((f32[8,40,1536]{2,1,0:T(8,128)}), f32[1,40,1536]{2,1,0:T(8,128)}) %reduce-scatter.2.cloned.1.call-update) | async-done | bytes 245776 | tf_op jit(solution)/shard_map/reduce_scatter | solution.py:105
  120.4 0.9 slice.78
  121.3 11.2 %collective-permute-start.5 = (f32[18,1536]{1,0:T(8,128)S(1)}, f32[18,1536]{1,0:T(8,128)S(1)}, u32[]{:S(2)}, u32[]{:S(2)}) collective-permute-start(f32[18,1536]{1,0:T(8,128)S(1)} %slice.78), channel_id=1, source_target_pairs={{0,1},{1,0},{2,3},{3,2},{4,5},{5,4},{6,7},{7,6},{8,9},{9,8},{10,11... | collective-permute-start | bytes 331784 | tf_op jit(solution)/shard_map/ppermute | solution.py:26
  132.5 2.0 %dynamic-slice_add_fusion.1 = f32[1536]{0:T(1024)S(1)} fusion(f32[4000]{0:T(1024)S(1)} %concatenate.25, s32[]{:T(128)S(6)} %select_n.325, f32[]{:T(128)} %bitcast.15, f32[]{:T(128)} %bitcast.14, f32[]{:T(128)} %bitcast.13, s32[]{:T(128)S(6)} %select_n.319), kind=kLoop, calls=%fused_computation.28 | loop fusion | flops 21504 | bytes 12308 | tf_op jit(solution)/shard_map/add | solution.py:126
  134.5 0.7 reshape.242
  135.2 3.4 %all-to-all-start.2 = ((f32[6,6,1280]{2,1,0:T(8,128)}), f32[6,6,1280]{2,1,0:T(8,128)S(1)}, u32[]{:S(2)}, u32[]{:S(2)}) async-start(f32[6,6,1280]{2,1,0:T(8,128)} %reshape.242), calls=%async_computation.3 | async-start | bytes 491520 | tf_op jit(solution)/shard_map/all_to_all | solution.py:113
  138.6 0.7 collective-permute-done.5
  139.4 1.7 %subtract_divide_fusion = f32[18,1536]{1,0:T(8,128)} fusion(f32[18,1536]{1,0:T(8,128)S(1)} %collective-permute-done.5, f32[40,1536]{1,0:T(8,128)} %bitcast.37, f32[18]{0:T(128)S(1)} %slice_bitcast_fusion.1, f32[1536]{0:T(1024)S(1)} %dynamic-slice_add_fusion.1), kind=kLoop, calls=%fused_computation.15 | loop fusion | flops 82944 | bytes 337992 | tf_op jit(solution)/shard_map/div | solution.py:126
  141.0 8.7 %all-to-all-done.2 = f32[6,6,1280]{2,1,0:T(8,128)S(1)} async-done(((f32[6,6,1280]{2,1,0:T(8,128)}), f32[6,6,1280]{2,1,0:T(8,128)S(1)}, u32[]{:S(2)}, u32[]{:S(2)}) %all-to-all-start.2) | async-done | bytes 184352 | tf_op jit(solution)/shard_map/all_to_all | solution.py:113
  149.8 0.7 subtract_divide_fusion.1
  (23 shorter events, 0.2 us)
Async XLA Ops:
  7.2 80.7 %copy-start = (s32[2,288]{1,0:T(2,128)S(1)}, s32[2,288]{1,0:T(2,128)}, u32[]{:S(2)}) copy-start(s32[2,288]{1,0:T(2,128)} %param.11) | copy-start | bytes 6916
  7.2 39.7 %collective-permute-start = (bf16[18,1536]{1,0:T(8,128)(2,1)}, bf16[18,1536]{1,0:T(8,128)(2,1)S(1)}, u32[]{:S(2)}, u32[]{:S(2)}) collective-permute-start(bf16[18,1536]{1,0:T(8,128)(2,1)} %param.14), channel_id=1, source_target_pairs={{0,1},{1,0},{2,3},{3,2},{4,5},{5,4},{6,7},{7,6},{8,9},{9,8},{10,11... | collective-permute-start | bytes 165896 | tf_op jit(solution)/shard_map/ppermute | solution.py:26
  23.1 15.7 %collective-permute-start.2 = (bf16[8,1280]{1,0:T(8,128)(2,1)S(1)}, bf16[8,1280]{1,0:T(8,128)(2,1)S(1)}, u32[]{:S(2)}, u32[]{:S(2)}) collective-permute-start(bf16[8,1280]{1,0:T(8,128)(2,1)S(1)} %pad.9), channel_id=1, source_target_pairs={{0,128},{128,0},{256,384},{384,256},{512,640},{640,512},{1,129},{1... | collective-permute-start | bytes 61448 | tf_op jit(solution)/shard_map/ppermute | solution.py:26
  33.8 13.1 %copy-start.2 = (bf16[18,1536]{1,0:T(8,128)(2,1)S(1)}, bf16[18,1536]{1,0:T(8,128)(2,1)}, u32[]{:S(2)}) copy-start(bf16[18,1536]{1,0:T(8,128)(2,1)} %param.14) | copy-start | bytes 165892
  38.8 16.3 %collective-permute-start.3 = (bf16[16,1280]{1,0:T(8,128)(2,1)S(1)}, bf16[16,1280]{1,0:T(8,128)(2,1)S(1)}, u32[]{:S(2)}, u32[]{:S(2)}) collective-permute-start(bf16[16,1280]{1,0:T(8,128)(2,1)S(1)} %pad_maximum_fusion.1), channel_id=1, source_target_pairs={{0,512},{128,640},{256,0},{384,128},{512,256},{640,384},{1,513},{1... | collective-permute-start | bytes 122888 | tf_op jit(solution)/shard_map/ppermute | solution.py:26
  44.9 10.2 %collective-permute-start.4 = (bf16[16,1280]{1,0:T(8,128)(2,1)S(1)}, bf16[16,1280]{1,0:T(8,128)(2,1)S(1)}, u32[]{:S(2)}, u32[]{:S(2)}) collective-permute-start(bf16[16,1280]{1,0:T(8,128)(2,1)S(1)} %pad_maximum_fusion.1), channel_id=1, source_target_pairs={{0,256},{128,384},{256,512},{384,640},{512,0},{640,128},{1,257},{1... | collective-permute-start | bytes 122888 | tf_op jit(solution)/shard_map/ppermute | solution.py:26
  48.0 33.6 %all-to-all-start = ((bf16[8,40,1536]{2,1,0:T(8,128)(2,1)}), bf16[8,40,1536]{2,1,0:T(8,128)(2,1)S(1)}, u32[]{:S(2)}, u32[]{:S(2)}) async-start(bf16[8,40,1536]{2,1,0:T(8,128)(2,1)} %broadcast_in_dim.100), calls=%async_computation | async-start | bytes 1966080 | tf_op jit(solution)/shard_map/all_to_all | solution.py:34
  55.1 65.4 %reduce-scatter.2.cloned.1.call-start = ((), (), s32[]{:S(2)}) async-start(), calls=%async_computation.4 | async-start | bytes 2211840 | tf_op jit(solution)/shard_map/reduce_scatter | solution.py:105
  81.5 6.2 %copy-start.1 = (f32[1000]{0:T(1024)S(1)}, f32[1000]{0:T(1024)}, u32[]{:S(2)}) copy-start(f32[1000]{0:T(1024)} %param.12) | copy-start | bytes 12004
  81.5 6.5 %copy-start.3 = (f32[100]{0:T(128)S(1)}, f32[100]{0:T(128)}, u32[]{:S(2)}) copy-start(f32[100]{0:T(128)} %param.13) | copy-start | bytes 1204
  85.8 4.2 %collective-permute-start.1 = (f32[160,1280]{1,0:T(8,128)S(1)}, f32[160,1280]{1,0:T(8,128)S(1)}, u32[]{:S(2)}, u32[]{:S(2)}) collective-permute-start(f32[160,1280]{1,0:T(8,128)S(1)} %slice.93), channel_id=1, source_target_pairs={{0,16},{16,0},{1,17},{17,1},{2,18},{18,2},{3,19},{19,3},{4,20},{20... | collective-permute-start | bytes 2457608 | tf_op jit(solution)/shard_map/ppermute | solution.py:26
  91.1 14.8 %all-to-all-start.1 = ((f32[4,40,1280]{2,1,0:T(8,128)}), f32[4,40,1280]{2,1,0:T(8,128)S(1)}, u32[]{:S(2)}, u32[]{:S(2)}) async-start(f32[4,40,1280]{2,1,0:T(8,128)} %bitcast.9), calls=%async_computation.1 | async-start | bytes 1638400 | tf_op jit(solution)/shard_map/all_to_all | solution.py:109
  121.3 18.0 %collective-permute-start.5 = (f32[18,1536]{1,0:T(8,128)S(1)}, f32[18,1536]{1,0:T(8,128)S(1)}, u32[]{:S(2)}, u32[]{:S(2)}) collective-permute-start(f32[18,1536]{1,0:T(8,128)S(1)} %slice.78), channel_id=1, source_target_pairs={{0,1},{1,0},{2,3},{3,2},{4,5},{5,4},{6,7},{7,6},{8,9},{9,8},{10,11... | collective-permute-start | bytes 331784 | tf_op jit(solution)/shard_map/ppermute | solution.py:26
  135.2 14.6 %all-to-all-start.2 = ((f32[6,6,1280]{2,1,0:T(8,128)}), f32[6,6,1280]{2,1,0:T(8,128)S(1)}, u32[]{:S(2)}, u32[]{:S(2)}) async-start(f32[6,6,1280]{2,1,0:T(8,128)} %reshape.242), calls=%async_computation.3 | async-start | bytes 491520 | tf_op jit(solution)/shard_map/all_to_all | solution.py:113
Sparse Core Ops, SparseCore 0:
  73.4 47.0 reduce-scatter.1

commit v4 on v3

--- a/solution.py
+++ b/solution.py
@@ -39,6 +39,19 @@
     return jnp.dot(chosen, source, preferred_element_type=jnp.float32).astype(source.dtype)
 
 
+def encode(sums, rows, axis_rows):
+    largest = jnp.max(jnp.abs(sums), axis=1, keepdims=True)
+    scale = jnp.ceil(jnp.log2(jnp.maximum(largest, 2.0**-120)) * 256.0)
+    parts = jnp.floor(sums * jnp.exp2(scale * (-1.0 / 256.0)) * 32767.0 + 0.5)
+    row = lax.broadcasted_iota(jnp.int32, (1, axis_rows, 1), 1)
+    return jnp.clip(jnp.where(row == rows, scale, parts), -32767.0, 32767.0).astype(jnp.int16)
+
+
+def decode_sum(coded, rows):
+    scale = jnp.exp2(coded[:, rows : rows + 1].astype(jnp.float32) * (1.0 / 256.0)) * (1.0 / 32767.0)
+    return jnp.sum(coded[:, :rows].astype(jnp.float32) * scale, axis=0)
+
+
 def pad_rows(block, count):
     return jnp.pad(block, ((0, count - block.shape[0]), (0, 0)))
 
@@ -62,7 +75,6 @@
 
     own = pad_rows(amp_cd, 8)
     own = jnp.concatenate([own, send(own, "zl", [(i, i ^ 1) for i in range(nzl)])], axis=0)
-    own = jnp.concatenate([own] + [send(own, "zl", shift(nzl, -s)) for s in (2, 4)], axis=0)
 
     row_first = row_group * rows_dev
     col_first = nab + col_group * cols_dev
@@ -72,6 +84,8 @@
     col_irrep = jnp.bitwise_xor(left, right)
     tiles = jnp.repeat(tile_mask, TILE, axis=1)
     col_code = jnp.where(tiles == 1, col_irrep[None, :], -1)
+    own, row_irrep, col_code = lax.optimization_barrier((own, row_irrep, col_code))
+    own = jnp.concatenate([own] + [send(own, "zl", shift(nzl, -s)) for s in (2, 4)], axis=0)
     keep = row_irrep.reshape(-1, TILE)[:, :, None] == col_code[:, None, :]
     blocks = integrals.reshape(-1, TILE, cols_dev)
     masked = jnp.where(keep, blocks, jnp.zeros_like(blocks)).reshape(rows_dev, cols_dev)
@@ -96,19 +110,24 @@
 
     out = jnp.arange(ncore * nx * x_pad, dtype=jnp.int32)
     r = out % x_pad
-    to_x = (out // x_pad) % nx
+    to_x = (x + out // x_pad) % nx
     to_core = (core + out // (x_pad * nx)) % ncore
     k = ((r // cd_count * nx + to_x) * ncore + to_core) * cd_count + r % cd_count
     amp = pick(all_ab, jnp.where(r < x_rows, k // y_rows * y_pad + k % y_rows, -1))
     partial_cd = jnp.dot(amp, masked, preferred_element_type=jnp.float32)
 
-    total_ab = lax.psum_scatter(partial_ab, "y", scatter_dimension=0, tiled=False)
+    coded = encode(partial_ab, y_rows, y_pad)
+    coded, virt_energy, occ_pairs = lax.optimization_barrier((coded, virt_energy, occ_pairs))
+    coded = lax.all_to_all(coded, "y", 0, 0)
 
     half = nx * x_pad
     total = partial_cd[:half] + send(partial_cd[half:], "core", shift(ncore, 1))
-    total = jnp.sum(lax.all_to_all(total.reshape(nx, x_pad, cols_dev), "x", 0, 0), axis=0)
-    total, total_ab = lax.optimization_barrier((total, total_ab))
-    ladder_ab = total_ab[ab_count:y_rows] + send(total_ab[:ab_count], "zh", shift(nzh, 1))
+    total = total.reshape(nx, x_pad, cols_dev)
+    near, far, back = (send(total[t], "x", shift(nx, t)) for t in range(1, nx))
+    coded, near = lax.optimization_barrier((coded, near))
+    total_ab = decode_sum(coded, y_rows)
+    ladder_ab = total_ab[ab_count:] + send(total_ab[:ab_count], "zh", shift(nzh, 1))
+    total = (total[0] + near) + (far + back)
     total = total[:x_rows].reshape(nzl, cd_count, cols_dev)
     ladder_cd = jnp.sum(lax.all_to_all(total, "zl", 0, 0), axis=0)
 

time: 158 us -> 133 us (0.84)
  the two profiles are of different devices: /device:TPU:4 before, /device:TPU:1 now
where the time goes in v4:
time: 133 us; the launch traced here: 131 us
  starting transfers between devices  56.7 us (43%)
  waiting for transfers between devices  22.8 us (17%)
  other arithmetic  17.5 us (13%)
  blocking collectives  16 us (12%)
  matrix products  8.77 us (7%)
  local copies, waits for them, and re-layouts  8.08 us (6%)
    ppermute x9, starting transfers between devices, send(): return lax.ppermute(block, axis, pairs)  42.9 us
    all_gather x1, blocking collectives, local(): all_cd = lax.all_gather(own, ('x', 'core'), axis=0, tiled=True)  16 us
    ppermute x9, waiting for transfers between devices, send(): return lax.ppermute(block, axis, pairs)  7.7 us
    all_to_all x1, waiting for transfers between devices, local(): ladder_cd = jnp.sum(lax.all_to_all(total, 'zl', 0, 0), axis=0)  7.41 us
    all_to_all x1, starting transfers between devices, gather(): lax.all_to_all(jnp.broadcast_to(block[None], (size,) + block.shape), axis...  6.82 us
    select_n x1, other arithmetic, local(): jnp.where(keep, blocks, jnp.zeros_like(blocks)).reshape(rows_dev, cols_dev)  4.94 us
    dot_general x1, matrix products, local(): partial_cd = jnp.dot(amp, masked, preferred_element_type=jnp.float32)  4.51 us
    all_to_all x1, waiting for transfers between devices, gather(): lax.all_to_all(jnp.broadcast_to(block[None], (size,) + block.shape), axis...  4.45 us
  transfers between devices with their start and end apart: 12, of which 5 were waited for; matrix products, arithmetic and copies ran while one was open for 25% of the time, Pallas kernels for 0%

profile of v4, /device:TPU:1, one launch (start us, length us, event | category | flops | bytes accessed | tf_op | source)
XLA Modules:
  0.0 130.9 jit_solution(17269765239919882208)
XLA Ops:
  0.6 0.7 pad.8
  1.4 4.8 %collective-permute-start = (bf16[8,1280]{1,0:T(8,128)(2,1)S(1)}, bf16[8,1280]{1,0:T(8,128)(2,1)S(1)}, u32[]{:S(2)}, u32[]{:S(2)}) collective-permute-start(bf16[8,1280]{1,0:T(8,128)(2,1)S(1)} %pad.8), channel_id=1, source_target_pairs={{0,128},{128,0},{256,384},{384,256},{512,640},{640,512},{1,129},{1... | collective-permute-start | bytes 61448 | tf_op jit(solution)/shard_map/ppermute | solution.py:26
  6.2 14.6 %collective-permute-start.3 = (bf16[18,1536]{1,0:T(8,128)(2,1)}, bf16[18,1536]{1,0:T(8,128)(2,1)S(1)}, u32[]{:S(2)}, u32[]{:S(2)}) collective-permute-start(bf16[18,1536]{1,0:T(8,128)(2,1)} %param.14), channel_id=1, source_target_pairs={{0,1},{1,0},{2,3},{3,2},{4,5},{5,4},{6,7},{7,6},{8,9},{9,8},{10,11... | collective-permute-start | bytes 165896 | tf_op jit(solution)/shard_map/ppermute | solution.py:26
  20.9 0.9 concatenate.21
  21.8 0.7 broadcast_compare_fusion.4
  22.5 0.1 copy.14
  22.6 0.8 fusion.55
  23.5 0.7 fusion.58
  24.1 1.9 %dynamic-slice_xor_fusion = s32[1280]{0:T(1024)S(1)} fusion(s32[4000]{0:T(1024)S(1)} %concatenate.21, s32[]{:T(128)S(6)} %select_n.333, s32[]{:T(128)} %bitcast.6, s32[]{:T(128)} %bitcast.5, s32[]{:T(128)} %bitcast.4, s32[]{:T(128)S(6)} %select_n.327), kind=kLoop, calls=%fused_computation.39 | loop fusion | flops 17920 | bytes 10260 | tf_op jit(solution)/shard_map/xor | solution.py:84
  26.1 0.1 broadcast_in_dim.121
  26.2 0.1 fusion.25
  26.2 2.0 %dynamic-slice_xor_fusion.1 = s32[1536]{0:T(1024)S(1)} fusion(s32[4000]{0:T(1024)S(1)} %concatenate.21, s32[]{:T(128)S(6)} %select_n.326, s32[]{:T(128)} %bitcast.2, s32[]{:T(128)} %bitcast.1, s32[]{:T(128)} %bitcast, s32[]{:T(128)S(6)} %select_n.320), kind=kLoop, calls=%fused_computation.43 | loop fusion | flops 21504 | bytes 12308 | tf_op jit(solution)/shard_map/xor | solution.py:82
  28.3 2.9 %collective-permute-start.2 = (bf16[16,1280]{1,0:T(8,128)(2,1)S(1)}, bf16[16,1280]{1,0:T(8,128)(2,1)S(1)}, u32[]{:S(2)}, u32[]{:S(2)}) collective-permute-start(bf16[16,1280]{1,0:T(8,128)(2,1)S(1)} %pad_maximum_fusion.1), channel_id=1, source_target_pairs={{0,256},{128,384},{256,512},{384,640},{512,0},{640,128},{1,257},{1... | collective-permute-start | bytes 122888 | tf_op jit(solution)/shard_map/ppermute | solution.py:26
  31.2 6.4 %collective-permute-start.1 = (bf16[16,1280]{1,0:T(8,128)(2,1)S(1)}, bf16[16,1280]{1,0:T(8,128)(2,1)S(1)}, u32[]{:S(2)}, u32[]{:S(2)}) collective-permute-start(bf16[16,1280]{1,0:T(8,128)(2,1)S(1)} %pad_maximum_fusion.1), channel_id=1, source_target_pairs={{0,512},{128,640},{256,0},{384,128},{512,256},{640,384},{1,513},{1... | collective-permute-start | bytes 122888 | tf_op jit(solution)/shard_map/ppermute | solution.py:26
  37.6 4.9 %fusion = bf16[1536,1280]{1,0:T(8,128)(2,1)} fusion(bf16[1536,1280]{1,0:T(8,128)(2,1)} %param.8, s32[6,1280]{1,0:T(8,128)S(1)} %broadcast_select_fusion.2, s32[1536]{0:T(1024)S(1)} %dynamic-slice_xor_fusion.1), kind=kLoop, calls=%fused_computation.1 | loop fusion | flops 3932160 | bytes 7901184 | tf_op jit(solution)/shard_map/jit(_where)/select_n | solution.py:91
  42.6 1.0 broadcast_in_dim.129
  43.7 6.8 %all-to-all-start.1 = ((bf16[8,40,1536]{2,1,0:T(8,128)(2,1)}), bf16[8,40,1536]{2,1,0:T(8,128)(2,1)S(1)}, u32[]{:S(2)}, u32[]{:S(2)}) async-start(bf16[8,40,1536]{2,1,0:T(8,128)(2,1)} %broadcast_in_dim.129), calls=%async_computation.1 | async-start | bytes 1966080 | tf_op jit(solution)/shard_map/all_to_all | solution.py:34
  50.5 16.0 %all_gather.3 = bf16[384,1280]{1,0:T(8,128)(2,1)S(1)} all-gather(bf16[48,1280]{1,0:T(8,128)(2,1)S(1)} %pad_maximum_fusion), channel_id=1, replica_groups=mesh['zl'=6,'x'=4,'core'=2,'y'=8,'zh'=2] {'x','core'}, dimensions={0}, use_global_device_ids=true | all-gather | bytes 1105920 | tf_op jit(solution)/shard_map/all_gather | solution.py:93
  66.5 0.6 convolution_convert_fusion.1
  67.2 3.6 %abs_reduce_fusion = (f32[8,1536]{1,0:T(8,128)S(1)}, f32[8,40,1536]{2,1,0:T(8,128)S(1)}) fusion(bf16[8,40,1280]{2,1,0:T(8,128)(2,1)S(1)} %bitcast.35, bf16[1536,1280]{1,0:T(8,128)(2,1)} %fusion), kind=kOutput, calls=%fused_computation.8 | convolution fusion | flops 1259261952 | bytes 6766592 | tf_op jit(solution)/shard_map/dot_general | solution.py:108
  70.8 1.5 %clamp_convert_fusion = s16[8,40,1536]{2,1,0:T(8,128)(2,1)} fusion(f32[8,40,1536]{2,1,0:T(8,128)S(1)} %get-tuple-element.43, f32[8,1536]{1,0:T(8,128)S(1)} %get-tuple-element.25, f32[8,1536]{1,0:T(8,128)S(1)} %get-tuple-element.24, pred[40]{0:T(512)(128)(4,1)S(1)} %iota_compare_fusion.7), kind=kLoop, calls=%fused_computation.7 | loop fusion | flops 3440640 | bytes 3047464 | tf_op jit(solution)/shard_map/convert_element_type | solution.py:47
  72.5 0.1 fusion.54
  72.6 0.6 fusion.57
  73.2 0.7 fusion.56
  73.8 4.4 %all-to-all-done.1 = bf16[8,40,1536]{2,1,0:T(8,128)(2,1)S(1)} async-done(((bf16[8,40,1536]{2,1,0:T(8,128)(2,1)}), bf16[8,40,1536]{2,1,0:T(8,128)(2,1)S(1)}, u32[]{:S(2)}, u32[]{:S(2)}) %all-to-all-start.1) | async-done | bytes 983072 | tf_op jit(solution)/shard_map/all_to_all | solution.py:34
  78.3 3.6 %all-to-all-start = ((s16[8,40,1536]{2,1,0:T(8,128)(2,1)}), s16[8,40,1536]{2,1,0:T(8,128)(2,1)S(1)}, u32[]{:S(2)}, u32[]{:S(2)}) async-start(s16[8,40,1536]{2,1,0:T(8,128)(2,1)} %clamp_convert_fusion), calls=%async_computation | async-start | bytes 1966080 | tf_op jit(solution)/shard_map/all_to_all | solution.py:121
  81.9 4.5 %fusion.3 = f32[320,1280]{1,0:T(8,128)S(1)} fusion(bf16[1536,1280]{1,0:T(8,128)(2,1)} %fusion, bf16[320,1536]{1,0:T(8,128)(2,1)} %bitcast.34, s32[320]{0:T(512)S(1)} %fusion.40), kind=kOutput, calls=%fused_computation.9 | convolution fusion | flops 1573457920 | bytes 6554880 | tf_op jit(solution)/shard_map/dot_general | solution.py:117
  86.4 1.0 slice.121
  87.3 2.4 %collective-permute-start.4 = (f32[160,1280]{1,0:T(8,128)}, f32[160,1280]{1,0:T(8,128)S(1)}, u32[]{:S(2)}, u32[]{:S(2)}) collective-permute-start(f32[160,1280]{1,0:T(8,128)} %slice.121), channel_id=1, source_target_pairs={{0,16},{16,0},{1,17},{17,1},{2,18},{18,2},{3,19},{19,3},{4,20},{20... | collective-permute-start | bytes 2457608 | tf_op jit(solution)/shard_map/ppermute | solution.py:26
  89.8 0.1 concatenate.24
  89.9 1.9 %dynamic-slice_add_fusion.1 = f32[1536]{0:T(1024)S(1)} fusion(f32[4000]{0:T(1024)S(1)} %concatenate.24, s32[]{:T(128)S(6)} %select_n.326, f32[]{:T(128)} %bitcast.14, f32[]{:T(128)} %bitcast.13, f32[]{:T(128)} %bitcast.12, s32[]{:T(128)S(6)} %select_n.320), kind=kLoop, calls=%fused_computation.38 | loop fusion | flops 21504 | bytes 12308 | tf_op jit(solution)/shard_map/add | solution.py:145
  91.8 0.2 select_reduce_fusion
  92.0 2.0 %dynamic-slice_add_fusion = f32[1280]{0:T(1024)S(1)} fusion(f32[4000]{0:T(1024)S(1)} %concatenate.24, s32[]{:T(128)S(6)} %select_n.333, f32[]{:T(128)} %bitcast.18, f32[]{:T(128)} %bitcast.17, f32[]{:T(128)} %bitcast.16, s32[]{:T(128)S(6)} %select_n.327), kind=kLoop, calls=%fused_computation.37 | loop fusion | flops 17920 | bytes 10260 | tf_op jit(solution)/shard_map/add | solution.py:147
  94.0 0.1 slice_add_fusion
  94.2 3.1 %collective-permute-start.5 = (f32[40,1280]{1,0:T(8,128)S(1)}, f32[40,1280]{1,0:T(8,128)S(1)}, u32[]{:S(2)}, u32[]{:S(2)}) collective-permute-start(f32[40,1280]{1,0:T(8,128)S(1)} %get-tuple-element.21), channel_id=1, source_target_pairs={{0,32},{32,64},{64,96},{96,0},{1,33},{33,65},{65,97},{97,1},{2,34}... | collective-permute-start | bytes 614408 | tf_op jit(solution)/shard_map/ppermute | solution.py:26
  97.4 3.4 %collective-permute-start.8 = (f32[40,1280]{1,0:T(8,128)S(1)}, f32[40,1280]{1,0:T(8,128)S(1)}, u32[]{:S(2)}, u32[]{:S(2)}) collective-permute-start(f32[40,1280]{1,0:T(8,128)S(1)} %get-tuple-element.19), channel_id=1, source_target_pairs={{0,96},{32,0},{64,32},{96,64},{1,97},{33,1},{65,33},{97,65},{2,98}... | collective-permute-start | bytes 614408 | tf_op jit(solution)/shard_map/ppermute | solution.py:26
  100.7 3.4 %collective-permute-start.7 = (f32[40,1280]{1,0:T(8,128)S(1)}, f32[40,1280]{1,0:T(8,128)S(1)}, u32[]{:S(2)}, u32[]{:S(2)}) collective-permute-start(f32[40,1280]{1,0:T(8,128)S(1)} %get-tuple-element.20), channel_id=1, source_target_pairs={{0,64},{32,96},{64,0},{96,32},{1,65},{33,97},{65,1},{97,33},{2,66}... | collective-permute-start | bytes 614408 | tf_op jit(solution)/shard_map/ppermute | solution.py:26
  104.2 3.2 %all-to-all-done = s16[8,40,1536]{2,1,0:T(8,128)(2,1)S(1)} async-done(((s16[8,40,1536]{2,1,0:T(8,128)(2,1)}), s16[8,40,1536]{2,1,0:T(8,128)(2,1)S(1)}, u32[]{:S(2)}, u32[]{:S(2)}) %all-to-all-start) | async-done | bytes 983072 | tf_op jit(solution)/shard_map/all_to_all | solution.py:121
  107.4 0.3 copy.15
  107.7 0.4 multiply_reduce_fusion
  108.2 1.9 %collective-permute-start.6 = (f32[18,1536]{1,0:T(8,128)S(1)}, f32[18,1536]{1,0:T(8,128)S(1)}, u32[]{:S(2)}, u32[]{:S(2)}) collective-permute-start(f32[18,1536]{1,0:T(8,128)S(1)} %slice.125), channel_id=1, source_target_pairs={{0,1},{1,0},{2,3},{3,2},{4,5},{5,4},{6,7},{7,6},{8,9},{9,8},{10,11... | collective-permute-start | bytes 331784 | tf_op jit(solution)/shard_map/ppermute | solution.py:26
  110.1 0.1 collective-permute-done.7
  110.2 0.7 reshape.256
  111.0 3.4 %all-to-all-start.2 = ((f32[6,6,1280]{2,1,0:T(8,128)}), f32[6,6,1280]{2,1,0:T(8,128)S(1)}, u32[]{:S(2)}, u32[]{:S(2)}) async-start(f32[6,6,1280]{2,1,0:T(8,128)} %reshape.256), calls=%async_computation.2 | async-start | bytes 491520 | tf_op jit(solution)/shard_map/all_to_all | solution.py:132
  114.4 7.6 %collective-permute-done.6 = f32[18,1536]{1,0:T(8,128)S(1)} collective-permute-done((f32[18,1536]{1,0:T(8,128)S(1)}, f32[18,1536]{1,0:T(8,128)S(1)}, u32[]{:S(2)}, u32[]{:S(2)}) %collective-permute-start.6) | collective-permute-done | bytes 110624 | tf_op jit(solution)/shard_map/ppermute | solution.py:26
  122.0 0.8 fusion.10
  122.7 7.4 %all-to-all-done.2 = f32[6,6,1280]{2,1,0:T(8,128)S(1)} async-done(((f32[6,6,1280]{2,1,0:T(8,128)}), f32[6,6,1280]{2,1,0:T(8,128)S(1)}, u32[]{:S(2)}, u32[]{:S(2)}) %all-to-all-start.2) | async-done | bytes 184352 | tf_op jit(solution)/shard_map/all_to_all | solution.py:132
  130.2 0.7 subtract_divide_fusion
  (36 shorter events, 0.7 us)
Async XLA Ops:
  0.6 71.7 %copy-start = (s32[2,288]{1,0:T(2,128)S(1)}, s32[2,288]{1,0:T(2,128)}, u32[]{:S(2)}) copy-start(s32[2,288]{1,0:T(2,128)} %param.11) | copy-start | bytes 6916
  1.4 26.9 %collective-permute-start = (bf16[8,1280]{1,0:T(8,128)(2,1)S(1)}, bf16[8,1280]{1,0:T(8,128)(2,1)S(1)}, u32[]{:S(2)}, u32[]{:S(2)}) collective-permute-start(bf16[8,1280]{1,0:T(8,128)(2,1)S(1)} %pad.8), channel_id=1, source_target_pairs={{0,128},{128,0},{256,384},{384,256},{512,640},{640,512},{1,129},{1... | collective-permute-start | bytes 61448 | tf_op jit(solution)/shard_map/ppermute | solution.py:26
  6.2 36.4 %collective-permute-start.3 = (bf16[18,1536]{1,0:T(8,128)(2,1)}, bf16[18,1536]{1,0:T(8,128)(2,1)S(1)}, u32[]{:S(2)}, u32[]{:S(2)}) collective-permute-start(bf16[18,1536]{1,0:T(8,128)(2,1)} %param.14), channel_id=1, source_target_pairs={{0,1},{1,0},{2,3},{3,2},{4,5},{5,4},{6,7},{7,6},{8,9},{9,8},{10,11... | collective-permute-start | bytes 165896 | tf_op jit(solution)/shard_map/ppermute | solution.py:26
  28.3 14.3 %copy-start.3 = (bf16[18,1536]{1,0:T(8,128)(2,1)S(1)}, bf16[18,1536]{1,0:T(8,128)(2,1)}, u32[]{:S(2)}) copy-start(bf16[18,1536]{1,0:T(8,128)(2,1)} %param.14) | copy-start | bytes 165892
  28.3 22.2 %collective-permute-start.2 = (bf16[16,1280]{1,0:T(8,128)(2,1)S(1)}, bf16[16,1280]{1,0:T(8,128)(2,1)S(1)}, u32[]{:S(2)}, u32[]{:S(2)}) collective-permute-start(bf16[16,1280]{1,0:T(8,128)(2,1)S(1)} %pad_maximum_fusion.1), channel_id=1, source_target_pairs={{0,256},{128,384},{256,512},{384,640},{512,0},{640,128},{1,257},{1... | collective-permute-start | bytes 122888 | tf_op jit(solution)/shard_map/ppermute | solution.py:26
  31.2 19.3 %collective-permute-start.1 = (bf16[16,1280]{1,0:T(8,128)(2,1)S(1)}, bf16[16,1280]{1,0:T(8,128)(2,1)S(1)}, u32[]{:S(2)}, u32[]{:S(2)}) collective-permute-start(bf16[16,1280]{1,0:T(8,128)(2,1)S(1)} %pad_maximum_fusion.1), channel_id=1, source_target_pairs={{0,512},{128,640},{256,0},{384,128},{512,256},{640,384},{1,513},{1... | collective-permute-start | bytes 122888 | tf_op jit(solution)/shard_map/ppermute | solution.py:26
  43.7 34.6 %all-to-all-start.1 = ((bf16[8,40,1536]{2,1,0:T(8,128)(2,1)}), bf16[8,40,1536]{2,1,0:T(8,128)(2,1)S(1)}, u32[]{:S(2)}, u32[]{:S(2)}) async-start(bf16[8,40,1536]{2,1,0:T(8,128)(2,1)} %broadcast_in_dim.129), calls=%async_computation.1 | async-start | bytes 1966080 | tf_op jit(solution)/shard_map/all_to_all | solution.py:34
  70.8 1.7 %copy-start.2 = (f32[1000]{0:T(1024)S(1)}, f32[1000]{0:T(1024)}, u32[]{:S(2)}) copy-start(f32[1000]{0:T(1024)} %param.12) | copy-start | bytes 12004
  78.3 3.6 %copy-start.1 = (bf16[8,40,1536]{2,1,0:T(8,128)(2,1)}, bf16[8,40,1536]{2,1,0:T(8,128)(2,1)S(1)}, u32[]{:S(2)}) copy-start(bf16[8,40,1536]{2,1,0:T(8,128)(2,1)S(1)} %all-to-all-done.1) | copy-start | bytes 2949124
  78.3 29.1 %all-to-all-start = ((s16[8,40,1536]{2,1,0:T(8,128)(2,1)}), s16[8,40,1536]{2,1,0:T(8,128)(2,1)S(1)}, u32[]{:S(2)}, u32[]{:S(2)}) async-start(s16[8,40,1536]{2,1,0:T(8,128)(2,1)} %clamp_convert_fusion), calls=%async_computation | async-start | bytes 1966080 | tf_op jit(solution)/shard_map/all_to_all | solution.py:121
  81.8 10.0 %copy-start.4 = (f32[100]{0:T(128)S(1)}, f32[100]{0:T(128)}, u32[]{:S(2)}) copy-start(f32[100]{0:T(128)} %param.13) | copy-start | bytes 1204
  87.3 6.7 %collective-permute-start.4 = (f32[160,1280]{1,0:T(8,128)}, f32[160,1280]{1,0:T(8,128)S(1)}, u32[]{:S(2)}, u32[]{:S(2)}) collective-permute-start(f32[160,1280]{1,0:T(8,128)} %slice.121), channel_id=1, source_target_pairs={{0,16},{16,0},{1,17},{17,1},{2,18},{18,2},{3,19},{19,3},{4,20},{20... | collective-permute-start | bytes 2457608 | tf_op jit(solution)/shard_map/ppermute | solution.py:26
  94.2 13.2 %collective-permute-start.5 = (f32[40,1280]{1,0:T(8,128)S(1)}, f32[40,1280]{1,0:T(8,128)S(1)}, u32[]{:S(2)}, u32[]{:S(2)}) collective-permute-start(f32[40,1280]{1,0:T(8,128)S(1)} %get-tuple-element.21), channel_id=1, source_target_pairs={{0,32},{32,64},{64,96},{96,0},{1,33},{33,65},{65,97},{97,1},{2,34}... | collective-permute-start | bytes 614408 | tf_op jit(solution)/shard_map/ppermute | solution.py:26
  97.4 12.7 %collective-permute-start.8 = (f32[40,1280]{1,0:T(8,128)S(1)}, f32[40,1280]{1,0:T(8,128)S(1)}, u32[]{:S(2)}, u32[]{:S(2)}) collective-permute-start(f32[40,1280]{1,0:T(8,128)S(1)} %get-tuple-element.19), channel_id=1, source_target_pairs={{0,96},{32,0},{64,32},{96,64},{1,97},{33,1},{65,33},{97,65},{2,98}... | collective-permute-start | bytes 614408 | tf_op jit(solution)/shard_map/ppermute | solution.py:26
  100.7 9.5 %collective-permute-start.7 = (f32[40,1280]{1,0:T(8,128)S(1)}, f32[40,1280]{1,0:T(8,128)S(1)}, u32[]{:S(2)}, u32[]{:S(2)}) collective-permute-start(f32[40,1280]{1,0:T(8,128)S(1)} %get-tuple-element.20), channel_id=1, source_target_pairs={{0,64},{32,96},{64,0},{96,32},{1,65},{33,97},{65,1},{97,33},{2,66}... | collective-permute-start | bytes 614408 | tf_op jit(solution)/shard_map/ppermute | solution.py:26
  108.2 13.8 %collective-permute-start.6 = (f32[18,1536]{1,0:T(8,128)S(1)}, f32[18,1536]{1,0:T(8,128)S(1)}, u32[]{:S(2)}, u32[]{:S(2)}) collective-permute-start(f32[18,1536]{1,0:T(8,128)S(1)} %slice.125), channel_id=1, source_target_pairs={{0,1},{1,0},{2,3},{3,2},{4,5},{5,4},{6,7},{7,6},{8,9},{9,8},{10,11... | collective-permute-start | bytes 331784 | tf_op jit(solution)/shard_map/ppermute | solution.py:26
  111.0 19.2 %all-to-all-start.2 = ((f32[6,6,1280]{2,1,0:T(8,128)}), f32[6,6,1280]{2,1,0:T(8,128)S(1)}, u32[]{:S(2)}, u32[]{:S(2)}) async-start(f32[6,6,1280]{2,1,0:T(8,128)} %reshape.256), calls=%async_computation.2 | async-start | bytes 491520 | tf_op jit(solution)/shard_map/all_to_all | solution.py:132

commit v5 on v4

v5 whole, which is shorter than its diff:
```python
import functools

import jax
import jax.numpy as jnp
from jax import lax
from jax.experimental import pallas as pl
from jax.experimental.pallas import tpu as pltpu
from jax.sharding import Mesh
from jax.sharding import PartitionSpec as P

NV = 1000
TILE = 256
LANES = 128
TABLE = 2048
AB = ("zl", "x", "core")
CD = ("y", "zh")
VMEM_LIMIT = 52 * 1024 * 1024
MASK_LIMIT = 60 * 1024 * 1024


def send(block, axis, pairs):
    return lax.ppermute(block, axis, pairs)


def shift(size, by):
    return [(i, (i + by) % size) for i in range(size)]


def gather(block, axis, size):
    return lax.all_to_all(jnp.broadcast_to(block[None], (size,) + block.shape), axis, 0, 0)


def chooser(rows, count):
    return (rows[:, None] == jnp.arange(count, dtype=jnp.int32)[None, :]).astype(jnp.bfloat16)


def pad_rows(block, count):
    return jnp.pad(block, ((0, count - block.shape[0]), (0, 0)))


def masked_kernel(
    place, tile_mask, irrep, energy, pairs, occ, irreps, energies, blocks, masked, den_ab, den_cd, table, row, col
):
    step = pl.program_id(0)
    rows_dev = row.shape[1]
    cols_dev = col.shape[1]

    def window(start, head, count):
        lane = lax.broadcasted_iota(jnp.int32, (1, count), 1)
        labels = jnp.zeros((1, count), jnp.int32)
        sums = jnp.zeros((1, count), jnp.float32)
        for j in range((count + NV - 1) // NV + 1):
            offset = j * NV - start
            turned = pltpu.roll(table[...], (offset + TABLE) % TABLE, 1)[:, :count]
            inside = (lane >= offset) & (lane < offset + NV)
            labels = jnp.where(inside, turned[0:1].astype(jnp.int32) ^ irrep[head + j], labels)
            sums = jnp.where(inside, turned[1:2] + energy[head + j], sums)
        return labels.astype(jnp.float32), sums

    def denominators(out, sums, first):
        for r in range(out.shape[0]):
            out[r : r + 1, :] = sums - (occ[pairs[0, first + r]] + occ[pairs[1, first + r]])

    @pl.when(step == 0)
    def _():
        table[...] = jnp.zeros_like(table)
        table[0:1, :NV] = irreps[...].astype(jnp.float32)
        table[1:2, :NV] = energies[...]
        labels, sums = window(place[0], place[1], rows_dev)
        row[...] = jnp.broadcast_to(labels, row.shape)
        denominators(den_ab, sums, place[4])
        labels, sums = window(place[2], place[3], cols_dev)
        col[...] = jnp.broadcast_to(labels, col.shape)
        denominators(den_cd, sums, place[5])

    across = row[0:1, pl.ds(pl.multiple_of(step * TILE, TILE), TILE)]
    down = jnp.transpose(jnp.broadcast_to(across, (LANES, TILE)))
    for c in range(cols_dev // LANES):
        lanes = slice(c * LANES, (c + 1) * LANES)
        label = jnp.where(tile_mask[step, c * LANES // TILE] == 1, col[0:1, lanes], -1.0)
        block = blocks[:, lanes].astype(jnp.float32)
        masked[:, lanes] = jnp.where(down == label, block, 0.0).astype(masked.dtype)


def ab_kernel(groups, used, choose, amps, masked, coded, chosen):
    @pl.when(pl.program_id(0) == 0)
    def _():
        for c in range(0, amps.shape[1], TILE):
            part = jnp.dot(choose[...], amps[:, c : c + TILE], preferred_element_type=jnp.float32)
            chosen[:, c : c + TILE] = part.astype(chosen.dtype)

    sums = lax.dot_general(
        chosen[...], masked[...], (((1,), (1,)), ((), ())), preferred_element_type=jnp.float32
    )
    rows, columns = sums.shape
    sums = sums.reshape(groups, rows // groups, columns)
    largest = jnp.max(jnp.abs(sums), axis=1, keepdims=True)
    scale = jnp.ceil(jnp.log2(jnp.maximum(largest, 2.0**-120)) * 256.0)
    parts = jnp.floor(sums * jnp.exp2(scale * (-1.0 / 256.0)) * 32767.0 + 0.5)
    place = lax.broadcasted_iota(jnp.int32, sums.shape, 1)
    parts = jnp.clip(jnp.where(place == used, scale, parts), -32767.0, 32767.0)
    coded[...] = parts.reshape(rows, columns).astype(jnp.int32).astype(jnp.int16)


def cd_kernel(choose, amps, masked, keep, give, chosen):
    @pl.when(pl.program_id(0) == 0)
    def _():
        for c in range(0, amps.shape[1], TILE):
            part = jnp.dot(choose[...], amps[:, c : c + TILE], preferred_element_type=jnp.float32)
            chosen[:, c : c + TILE] = part.astype(chosen.dtype)

    sums = jnp.dot(chosen[...], masked[...], preferred_element_type=jnp.float32)
    half = keep.shape[0]
    keep[...] = sums[:half]
    give[...] = sums[half:]


def decode_sum(coded, rows):
    scale = jnp.exp2(coded[:, rows : rows + 1].astype(jnp.float32) * (1.0 / 256.0)) * (1.0 / 32767.0)
    return jnp.sum(coded[:, :rows].astype(jnp.float32) * scale, axis=0)


def local(integrals, tile_mask, virt_irrep, occ_pairs, virt_energy, occ_energy, amp_ab, amp_cd):
    rows_dev = integrals.shape[0]
    cols_dev = integrals.shape[1]
    nzl, nx, ncore, ny, nzh = (lax.axis_size(a) for a in ("zl", "x", "core", "y", "zh"))
    zl, x, core, y, zh = (lax.axis_index(a) for a in ("zl", "x", "core", "y", "zh"))
    row_group = (zl * nx + x) * ncore + core
    col_group = y * nzh + zh
    nab = rows_dev * nzl * nx * ncore
    cd_count = amp_cd.shape[0]
    ab_count = amp_ab.shape[0]
    y_rows = nzh * ab_count
    y_pad = 40
    x_rows = nzl * cd_count
    x_pad = 40
    ab_rows = ny * y_pad
    cd_rows = ncore * nx * x_pad
    params = pltpu.CompilerParams(vmem_limit_bytes=VMEM_LIMIT)

    count = nzl * nx * ncore * 8
    half = cd_rows // ncore

    def ab_chooser():
        out = jnp.arange(ab_rows, dtype=jnp.int32)
        r = out % y_pad
        to_zh = (zh + 1 + r // ab_count) % nzh
        k = ((out // y_pad) * nzh + to_zh) * ab_count + r % ab_count
        group = k // cd_count
        offset = ((group - core) % ncore) * nx + (group // ncore) % nx
        source = (offset * nzl + group // (nx * ncore)) * 8 + k % cd_count
        return chooser(jnp.where(r < y_rows, source, -1), count)

    def cd_chooser():
        out = jnp.arange(cd_rows, dtype=jnp.int32)
        r = out % x_pad
        to_x = (x + out // x_pad) % nx
        to_core = (core + out // (x_pad * nx)) % ncore
        k = ((r // cd_count * nx + to_x) * ncore + to_core) * cd_count + r % cd_count
        return chooser(jnp.where(r < x_rows, k // y_rows * y_pad + k % y_rows, -1), ab_rows)

    other = send(amp_ab, "zh", shift(nzh, 1))
    first = jnp.where(zh == 0, amp_ab, other)
    second = jnp.where(zh == 0, other, amp_ab)
    both = pad_rows(jnp.concatenate([first, second], axis=0), y_pad)

    own = gather(pad_rows(amp_cd, 8), "zl", nzl).reshape(nzl * 8, cols_dev)

    row_first = row_group * rows_dev
    col_first = nab + col_group * cols_dev
    place = jnp.stack(
        [row_first % NV, row_first // NV, col_first % NV, col_first // NV, col_group * ab_count, row_group * cd_count]
    ).astype(jnp.int32)
    smem = pl.BlockSpec(memory_space=pltpu.SMEM)
    masked, den_ab, den_cd = pl.pallas_call(
        masked_kernel,
        grid=(rows_dev // TILE,),
        in_specs=[smem] * 6
        + [
            pl.BlockSpec((1, NV), lambda i: (0, 0)),
            pl.BlockSpec((1, NV), lambda i: (0, 0)),
            pl.BlockSpec((TILE, cols_dev), lambda i: (i, 0)),
        ],
        out_specs=[
            pl.BlockSpec((TILE, cols_dev), lambda i: (i, 0)),
            pl.BlockSpec((ab_count, rows_dev), lambda i: (0, 0)),
            pl.BlockSpec((cd_count, cols_dev), lambda i: (0, 0)),
        ],
        out_shape=[
            jax.ShapeDtypeStruct(integrals.shape, integrals.dtype),
            jax.ShapeDtypeStruct((ab_count, rows_dev), jnp.float32),
            jax.ShapeDtypeStruct((cd_count, cols_dev), jnp.float32),
        ],
        scratch_shapes=[
            pltpu.VMEM((8, TABLE), jnp.float32),
            pltpu.VMEM((8, rows_dev), jnp.float32),
            pltpu.VMEM((8, cols_dev), jnp.float32),
        ],
        compiler_params=pltpu.CompilerParams(vmem_limit_bytes=MASK_LIMIT),
        cost_estimate=pl.CostEstimate(flops=4 * rows_dev * cols_dev, bytes_accessed=4 * rows_dev * cols_dev, transcendentals=0),
        name="masked",
    )(
        place,
        tile_mask,
        virt_irrep,
        virt_energy,
        occ_pairs,
        occ_energy,
        virt_irrep.reshape(1, NV),
        virt_energy.reshape(1, NV),
        integrals,
    )

    choose_ab, choose_cd = ab_chooser(), cd_chooser()
    own, masked, both, choose_ab, choose_cd = lax.optimization_barrier((own, masked, both, choose_ab, choose_cd))
    own = lax.all_gather(own, "x", axis=0, tiled=True)
    all_cd = jnp.concatenate([own, send(own, "core", shift(ncore, 1))], axis=0)
    all_ab = gather(both, "y", ny).reshape(ab_rows, rows_dev)

    coded = pl.pallas_call(
        functools.partial(ab_kernel, ny, y_rows),
        grid=(rows_dev // TILE,),
        in_specs=[
            pl.BlockSpec((ab_rows, count), lambda i: (0, 0)),
            pl.BlockSpec((count, cols_dev), lambda i: (0, 0)),
            pl.BlockSpec((TILE, cols_dev), lambda i: (i, 0)),
        ],
        out_specs=pl.BlockSpec((ab_rows, TILE), lambda i: (0, i)),
        out_shape=jax.ShapeDtypeStruct((ab_rows, rows_dev), jnp.int16),
        scratch_shapes=[pltpu.VMEM((ab_rows, cols_dev), jnp.bfloat16)],
        compiler_params=params,
        cost_estimate=pl.CostEstimate(
            flops=2 * ab_rows * cols_dev * (rows_dev + count), bytes_accessed=2 * rows_dev * cols_dev, transcendentals=0
        ),
        name="ab_product",
    )(choose_ab, all_cd, masked)

    all_ab, coded = lax.optimization_barrier((all_ab, coded))
    keep, give = pl.pallas_call(
        cd_kernel,
        grid=(cols_dev // TILE,),
        in_specs=[
            pl.BlockSpec((cd_rows, ab_rows), lambda i: (0, 0)),
            pl.BlockSpec((ab_rows, rows_dev), lambda i: (0, 0)),
            pl.BlockSpec((rows_dev, TILE), lambda i: (0, i)),
        ],
        out_specs=[pl.BlockSpec((half, TILE), lambda i: (0, i))] * 2,
        out_shape=[jax.ShapeDtypeStruct((half, cols_dev), jnp.float32)] * 2,
        scratch_shapes=[pltpu.VMEM((cd_rows, rows_dev), jnp.bfloat16)],
        compiler_params=params,
        cost_estimate=pl.CostEstimate(
            flops=2 * cd_rows * rows_dev * (cols_dev + ab_rows), bytes_accessed=2 * rows_dev * cols_dev, transcendentals=0
        ),
        name="cd_product",
    )(choose_cd, all_ab, masked)

    coded = lax.all_to_all(coded.reshape(ny, y_pad, rows_dev), "y", 0, 0)

    total = keep + send(give, "core", shift(ncore, 1))
    total = total.reshape(nx, x_pad, cols_dev)
    near, far, back = (send(total[t], "x", shift(nx, t)) for t in range(1, nx))
    coded, near = lax.optimization_barrier((coded, near))
    total_ab = decode_sum(coded, y_rows)
    ladder_ab = total_ab[ab_count:] + send(total_ab[:ab_count], "zh", shift(nzh, 1))
    total = (total[0] + near) + (far + back)
    total = total[:x_rows].reshape(nzl, cd_count, cols_dev)
    ladder_cd = jnp.sum(lax.all_to_all(total, "zl", 0, 0), axis=0)
    return (ladder_ab / den_ab, ladder_cd / den_cd)


def solution(mesh):
    fine = Mesh(mesh.devices.reshape(6, 4, 2, 8, 2), AB + CD)
    return jax.shard_map(
        local,
        mesh=fine,
        in_specs=(P(AB, CD), P(AB, CD), P(), P(), P(), P(), P(CD, AB), P(AB, CD)),
        out_specs=(P(CD, AB), P(AB, CD)),
        check_vma=False,
    )
```

time: 133 us -> 130 us (0.977)
  Pallas kernels: 0 us -> 19.8 us
  other arithmetic: 17.5 us -> 3.29 us
  matrix products: 8.77 us -> 0 us
  starting transfers between devices: 56.7 us -> 64.1 us
  blocking collectives: 16 us -> 10.2 us
  local copies, waits for them, and re-layouts: 8.08 us -> 4.19 us
  waiting for transfers between devices: 22.8 us -> 26.5 us
    pallas_call x0 -> x3, Pallas kernels: none -> 19.8 us  [the longest x1 7.3 us: local(): pl.pallas_call(functools.partial(ab_kernel, ny, y_rows), grid=(rows_dev /...]
    dot_general x3 -> x0, matrix products: 8.77 us -> none  [the longest x1 4.51 us: local(): partial_cd = jnp.dot(amp, masked, preferred_element_type=jnp.float32)]
    all_to_all x1 -> x2, starting transfers between devices: 6.82 us -> 12.9 us  [gather(): lax.all_to_all(jnp.broadcast_to(block[None], (size,) + block.shape), axis...]
    all_gather x1, blocking collectives: 16 us -> 10.2 us  [local(): own = lax.all_gather(own, 'x', axis=0, tiled=True)]
    select_n x4 -> x1, other arithmetic: 5.07 us -> 0.06 us  [ab_chooser(): return chooser(jnp.where(r < y_rows, source, -1), count)]
    all_to_all x1, waiting for transfers between devices: 3.21 us -> 7.94 us  [local(): coded = lax.all_to_all(coded.reshape(ny, y_pad, rows_dev), 'y', 0, 0)]
    ppermute x9 -> x7, starting transfers between devices: 42.9 us -> 38.5 us  [send(): return lax.ppermute(block, axis, pairs)]
    all_to_all x1 -> x2, waiting for transfers between devices: 4.45 us -> 0.04 us  [gather(): lax.all_to_all(jnp.broadcast_to(block[None], (size,) + block.shape), axis...]
  transfers between devices with their start and end apart: 12 -> 11, of which waited for: 5 -> 6; matrix products, arithmetic and copies ran while one was open for 25% -> 4% of each run, Pallas kernels for 0% -> 15%
where the time goes in v5:
time: 130 us; the launch traced here: 129 us
  starting transfers between devices  64.1 us (49%)
  waiting for transfers between devices  26.5 us (20%)
  Pallas kernels  19.8 us (15%)
  blocking collectives  10.2 us (8%)
  local copies, waits for them, and re-layouts  4.19 us (3%)
  other arithmetic  3.29 us (3%)
    ppermute x7, starting transfers between devices, send(): return lax.ppermute(block, axis, pairs)  38.5 us
    all_to_all x2, starting transfers between devices, gather(): lax.all_to_all(jnp.broadcast_to(block[None], (size,) + block.shape), axis...  12.9 us
    all_gather x1, blocking collectives, local(): own = lax.all_gather(own, 'x', axis=0, tiled=True)  10.2 us
    all_to_all x1, waiting for transfers between devices, local(): ladder_cd = jnp.sum(lax.all_to_all(total, 'zl', 0, 0), axis=0)  10.1 us
    ppermute x7, waiting for transfers between devices, send(): return lax.ppermute(block, axis, pairs)  8.4 us
    all_to_all x1, waiting for transfers between devices, local(): coded = lax.all_to_all(coded.reshape(ny, y_pad, rows_dev), 'y', 0, 0)  7.94 us
    pallas_call x1, Pallas kernels, local(): pl.pallas_call(functools.partial(ab_kernel, ny, y_rows), grid=(rows_dev /...  7.3 us
    pallas_call x1, Pallas kernels, local(): pl.pallas_call(masked_kernel, grid=(rows_dev // TILE,), in_specs=[smem] *...  6.71 us
  transfers between devices with their start and end apart: 11, of which 6 were waited for; matrix products, arithmetic and copies ran while one was open for 4% of the time, Pallas kernels for 15%

profile of v5, /device:TPU:1, one launch (start us, length us, event | category | flops | bytes accessed | tf_op | source)
XLA Modules:
  0.0 128.9 jit_solution(3968790518575498954)
XLA Ops:
  0.6 15.7 %collective-permute-start = (bf16[18,1536]{1,0:T(8,128)(2,1)}, bf16[18,1536]{1,0:T(8,128)(2,1)S(1)}, u32[]{:S(2)}, u32[]{:S(2)}) collective-permute-start(bf16[18,1536]{1,0:T(8,128)(2,1)} %param.14), channel_id=1, source_target_pairs={{0,1},{1,0},{2,3},{3,2},{4,5},{5,4},{6,7},{7,6},{8,9},{9,8},{10,11... | collective-permute-start | bytes 165896 | tf_op jit(solution)/shard_map/ppermute | solution.py:22
  16.3 0.7 pad.8
  17.1 0.7 broadcast_in_dim.7
  17.7 6.1 %all-to-all-start = ((bf16[6,8,1280]{2,1,0:T(8,128)(2,1)}), bf16[6,8,1280]{2,1,0:T(8,128)(2,1)S(1)}, u32[]{:S(2)}, u32[]{:S(2)}) async-start(bf16[6,8,1280]{2,1,0:T(8,128)(2,1)} %broadcast_in_dim.7), calls=%async_computation | async-start | bytes 245760 | tf_op jit(solution)/shard_map/all_to_all | solution.py:30
  23.8 0.1 fusion.20
  23.9 0.1 fusion.choose
  24.0 0.1 fusion.1.choose
  24.2 0.7 stack.27.place
  24.9 6.7 %masked.1 = (bf16[1536,1280]{1,0:T(8,128)(2,1)}, f32[18,1536]{1,0:T(8,128)}, f32[6,1280]{1,0:T(8,128)}) custom-call(s32[6]{0:T(128)} %stack.27.place, s32[6,5]{1,0:T(8,128)} %tile_mask.1, s32[1000]{0:T(1024)} %irrep.1, f32[1000]{0:T(1024)} %energy.1, s32[2,288]{1,0:T(2,128)} %pairs.1, f32[100]{0:T(128)} %occ.1, s32[1,1000]{1,0:T(1,128)} %bitcast.15, ...), custom_call_target="tpu_custom_call" | custom-call | flops 7864320 | bytes 7864320 | tf_op jit(solution)/shard_map/masked/pallas_call | solution.py:175
  31.6 0.0 collective-permute-done
  31.6 0.0 copy-done.2
  31.7 0.0 all-to-all-done
  31.7 1.0 broadcast_in_dim.8
  32.7 6.8 %all-to-all-start.1 = ((bf16[8,40,1536]{2,1,0:T(8,128)(2,1)}), bf16[8,40,1536]{2,1,0:T(8,128)(2,1)S(1)}, u32[]{:S(2)}, u32[]{:S(2)}) async-start(bf16[8,40,1536]{2,1,0:T(8,128)(2,1)} %broadcast_in_dim.8), calls=%async_computation.1 | async-start | bytes 1966080 | tf_op jit(solution)/shard_map/all_to_all | solution.py:30
  39.5 10.2 %all_gather.3 = bf16[192,1280]{1,0:T(8,128)(2,1)S(1)} all-gather(bf16[48,1280]{1,0:T(8,128)(2,1)S(1)} %bitcast.14), channel_id=1, replica_groups=mesh['zl'=6,'x'=4,'core'=2,'y'=8,'zh'=2] {'x'}, dimensions={0}, use_global_device_ids=true | all-gather | bytes 614400 | tf_op jit(solution)/shard_map/all_gather | solution.py:216
  49.7 8.2 %collective-permute-start.1 = (bf16[192,1280]{1,0:T(8,128)(2,1)S(1)}, bf16[192,1280]{1,0:T(8,128)(2,1)S(1)}, u32[]{:S(2)}, u32[]{:S(2)}) collective-permute-start(bf16[192,1280]{1,0:T(8,128)(2,1)S(1)} %all_gather.3), channel_id=1, source_target_pairs={{0,16},{16,0},{1,17},{17,1},{2,18},{18,2},{3,19},{19,3},{4,20},{20... | collective-permute-start | bytes 1474568 | tf_op jit(solution)/shard_map/ppermute | solution.py:22
  57.9 1.5 %collective-permute-done.1 = bf16[192,1280]{1,0:T(8,128)(2,1)S(1)} collective-permute-done((bf16[192,1280]{1,0:T(8,128)(2,1)S(1)}, bf16[192,1280]{1,0:T(8,128)(2,1)S(1)}, u32[]{:S(2)}, u32[]{:S(2)}) %collective-permute-start.1) | collective-permute-done | bytes 491552 | tf_op jit(solution)/shard_map/ppermute | solution.py:22
  59.4 1.0 pad_maximum_fusion.amps
  60.4 7.3 %ab_product.1 = s16[320,1536]{1,0:T(8,128)(2,1)} custom-call(bf16[320,384]{1,0:T(8,128)(2,1)S(1)} %fusion.choose, bf16[384,1280]{1,0:T(8,128)(2,1)} %pad_maximum_fusion.amps, bf16[1536,1280]{1,0:T(8,128)(2,1)} %get-tuple-element.20.masked), custom_call_target="tpu_custom_call" | custom-call | flops 1572864000 | bytes 3932160 | tf_op jit(solution)/shard_map/ab_product/pallas_call | solution.py:220
  67.7 0.0 all-to-all-done.1
  67.7 6.6 %all-to-all-start.2 = ((s16[8,40,1536]{2,1,0:T(8,128)(2,1)}), s16[8,40,1536]{2,1,0:T(8,128)(2,1)S(1)}, u32[]{:S(2)}, u32[]{:S(2)}) async-start(s16[8,40,1536]{2,1,0:T(8,128)(2,1)} %bitcast.10), calls=%async_computation.2 | async-start | bytes 1966080 | tf_op jit(solution)/shard_map/all_to_all | solution.py:257
  74.4 0.0 copy-done
  74.4 5.8 %cd_product.1 = (f32[160,1280]{1,0:T(8,128)S(1)}, f32[160,1280]{1,0:T(8,128)S(1)}) custom-call(bf16[320,320]{1,0:T(8,128)(2,1)S(1)} %fusion.1.choose, bf16[320,1536]{1,0:T(8,128)(2,1)} %bitcast.13, bf16[1536,1280]{1,0:T(8,128)(2,1)} %get-tuple-element.20.masked), custom_call_target="tpu_custom_call" | custom-call | flops 1572864000 | bytes 3932160 | tf_op jit(solution)/shard_map/cd_product/pallas_call | solution.py:239
  80.2 2.6 %collective-permute-start.2 = (f32[160,1280]{1,0:T(8,128)S(1)}, f32[160,1280]{1,0:T(8,128)S(1)}, u32[]{:S(2)}, u32[]{:S(2)}) collective-permute-start(f32[160,1280]{1,0:T(8,128)S(1)} %get-tuple-element.25), channel_id=1, source_target_pairs={{0,16},{16,0},{1,17},{17,1},{2,18},{18,2},{3,19},{19,3},{4,20},{20... | collective-permute-start | bytes 2457608 | tf_op jit(solution)/shard_map/ppermute | solution.py:22
  82.7 1.9 %collective-permute-done.2 = f32[160,1280]{1,0:T(8,128)S(1)} collective-permute-done((f32[160,1280]{1,0:T(8,128)S(1)}, f32[160,1280]{1,0:T(8,128)S(1)}, u32[]{:S(2)}, u32[]{:S(2)}) %collective-permute-start.2) | collective-permute-done | bytes 819232 | tf_op jit(solution)/shard_map/ppermute | solution.py:22
  84.7 0.1 add.301
  84.8 0.1 fusion.44
  84.8 2.8 %collective-permute-start.3 = (f32[40,1280]{1,0:T(8,128)S(1)}, f32[40,1280]{1,0:T(8,128)S(1)}, u32[]{:S(2)}, u32[]{:S(2)}) collective-permute-start(f32[40,1280]{1,0:T(8,128)S(1)} %get-tuple-element.33), channel_id=1, source_target_pairs={{0,32},{32,64},{64,96},{96,0},{1,33},{33,65},{65,97},{97,1},{2,34}... | collective-permute-start | bytes 614408 | tf_op jit(solution)/shard_map/ppermute | solution.py:22
  87.6 3.7 %collective-permute-start.6 = (f32[40,1280]{1,0:T(8,128)S(1)}, f32[40,1280]{1,0:T(8,128)S(1)}, u32[]{:S(2)}, u32[]{:S(2)}) collective-permute-start(f32[40,1280]{1,0:T(8,128)S(1)} %get-tuple-element.31), channel_id=1, source_target_pairs={{0,96},{32,0},{64,32},{96,64},{1,97},{33,1},{65,33},{97,65},{2,98}... | collective-permute-start | bytes 614408 | tf_op jit(solution)/shard_map/ppermute | solution.py:22
  91.3 2.5 %collective-permute-start.5 = (f32[40,1280]{1,0:T(8,128)S(1)}, f32[40,1280]{1,0:T(8,128)S(1)}, u32[]{:S(2)}, u32[]{:S(2)}) collective-permute-start(f32[40,1280]{1,0:T(8,128)S(1)} %get-tuple-element.32), channel_id=1, source_target_pairs={{0,64},{32,96},{64,0},{96,32},{1,65},{33,97},{65,1},{97,33},{2,66}... | collective-permute-start | bytes 614408 | tf_op jit(solution)/shard_map/ppermute | solution.py:22
  93.8 0.4 collective-permute-done.3
  94.2 7.9 %all-to-all-done.2 = s16[8,40,1536]{2,1,0:T(8,128)(2,1)S(1)} async-done(((s16[8,40,1536]{2,1,0:T(8,128)(2,1)}), s16[8,40,1536]{2,1,0:T(8,128)(2,1)S(1)}, u32[]{:S(2)}, u32[]{:S(2)}) %all-to-all-start.2) | async-done | bytes 983072 | tf_op jit(solution)/shard_map/all_to_all | solution.py:257
  102.2 0.3 copy.11
  102.5 0.0 copy-start.1
  102.5 0.0 copy-start.3
  102.5 0.4 multiply_reduce_fusion
  103.0 3.1 %collective-permute-start.4 = (f32[18,1536]{1,0:T(8,128)S(1)}, f32[18,1536]{1,0:T(8,128)S(1)}, u32[]{:S(2)}, u32[]{:S(2)}) collective-permute-start(f32[18,1536]{1,0:T(8,128)S(1)} %slice.43), channel_id=1, source_target_pairs={{0,1},{1,0},{2,3},{3,2},{4,5},{5,4},{6,7},{7,6},{8,9},{9,8},{10,11... | collective-permute-start | bytes 331784 | tf_op jit(solution)/shard_map/ppermute | solution.py:22
  106.0 0.0 collective-permute-done.6
  106.0 0.0 collective-permute-done.5
  106.1 0.1 fusion.4
  106.1 0.7 reshape.218
  106.8 6.1 %all-to-all-start.3 = ((f32[6,6,1280]{2,1,0:T(8,128)}), f32[6,6,1280]{2,1,0:T(8,128)S(1)}, u32[]{:S(2)}, u32[]{:S(2)}) async-start(f32[6,6,1280]{2,1,0:T(8,128)} %reshape.218), calls=%async_computation.3 | async-start | bytes 491520 | tf_op jit(solution)/shard_map/all_to_all | solution.py:267
  112.9 4.6 %collective-permute-done.4 = f32[18,1536]{1,0:T(8,128)S(1)} collective-permute-done((f32[18,1536]{1,0:T(8,128)S(1)}, f32[18,1536]{1,0:T(8,128)S(1)}, u32[]{:S(2)}, u32[]{:S(2)}) %collective-permute-start.4) | collective-permute-done | bytes 110624 | tf_op jit(solution)/shard_map/ppermute | solution.py:22
  117.5 0.0 copy-done.1
  117.5 0.7 fusion.5
  118.2 10.1 %all-to-all-done.3 = f32[6,6,1280]{2,1,0:T(8,128)S(1)} async-done(((f32[6,6,1280]{2,1,0:T(8,128)}), f32[6,6,1280]{2,1,0:T(8,128)S(1)}, u32[]{:S(2)}, u32[]{:S(2)}) %all-to-all-start.3) | async-done | bytes 184352 | tf_op jit(solution)/shard_map/all_to_all | solution.py:267
  128.3 0.0 copy-done.3
  128.3 0.6 div.101
  (7 shorter events, 0.1 us)
Async XLA Ops:
  0.6 30.9 %collective-permute-start = (bf16[18,1536]{1,0:T(8,128)(2,1)}, bf16[18,1536]{1,0:T(8,128)(2,1)S(1)}, u32[]{:S(2)}, u32[]{:S(2)}) collective-permute-start(bf16[18,1536]{1,0:T(8,128)(2,1)} %param.14), channel_id=1, source_target_pairs={{0,1},{1,0},{2,3},{3,2},{4,5},{5,4},{6,7},{7,6},{8,9},{9,8},{10,11... | collective-permute-start | bytes 165896 | tf_op jit(solution)/shard_map/ppermute | solution.py:22
  17.7 14.0 %all-to-all-start = ((bf16[6,8,1280]{2,1,0:T(8,128)(2,1)}), bf16[6,8,1280]{2,1,0:T(8,128)(2,1)S(1)}, u32[]{:S(2)}, u32[]{:S(2)}) async-start(bf16[6,8,1280]{2,1,0:T(8,128)(2,1)} %broadcast_in_dim.7), calls=%async_computation | async-start | bytes 245760 | tf_op jit(solution)/shard_map/all_to_all | solution.py:30
  24.9 6.7 %copy-start.2 = (bf16[18,1536]{1,0:T(8,128)(2,1)S(1)}, bf16[18,1536]{1,0:T(8,128)(2,1)}, u32[]{:S(2)}) copy-start(bf16[18,1536]{1,0:T(8,128)(2,1)} %param.14) | copy-start | bytes 165892
  32.7 35.0 %all-to-all-start.1 = ((bf16[8,40,1536]{2,1,0:T(8,128)(2,1)}), bf16[8,40,1536]{2,1,0:T(8,128)(2,1)S(1)}, u32[]{:S(2)}, u32[]{:S(2)}) async-start(bf16[8,40,1536]{2,1,0:T(8,128)(2,1)} %broadcast_in_dim.8), calls=%async_computation.1 | async-start | bytes 1966080 | tf_op jit(solution)/shard_map/all_to_all | solution.py:30
  49.7 9.7 %collective-permute-start.1 = (bf16[192,1280]{1,0:T(8,128)(2,1)S(1)}, bf16[192,1280]{1,0:T(8,128)(2,1)S(1)}, u32[]{:S(2)}, u32[]{:S(2)}) collective-permute-start(bf16[192,1280]{1,0:T(8,128)(2,1)S(1)} %all_gather.3), channel_id=1, source_target_pairs={{0,16},{16,0},{1,17},{17,1},{2,18},{18,2},{3,19},{19,3},{4,20},{20... | collective-permute-start | bytes 1474568 | tf_op jit(solution)/shard_map/ppermute | solution.py:22
  67.7 6.7 %copy-start = (bf16[8,40,1536]{2,1,0:T(8,128)(2,1)}, bf16[8,40,1536]{2,1,0:T(8,128)(2,1)S(1)}, u32[]{:S(2)}) copy-start(bf16[8,40,1536]{2,1,0:T(8,128)(2,1)S(1)} %all-to-all-done.1) | copy-start | bytes 2949124
  67.7 34.4 %all-to-all-start.2 = ((s16[8,40,1536]{2,1,0:T(8,128)(2,1)}), s16[8,40,1536]{2,1,0:T(8,128)(2,1)S(1)}, u32[]{:S(2)}, u32[]{:S(2)}) async-start(s16[8,40,1536]{2,1,0:T(8,128)(2,1)} %bitcast.10), calls=%async_computation.2 | async-start | bytes 1966080 | tf_op jit(solution)/shard_map/all_to_all | solution.py:257
  80.2 4.5 %collective-permute-start.2 = (f32[160,1280]{1,0:T(8,128)S(1)}, f32[160,1280]{1,0:T(8,128)S(1)}, u32[]{:S(2)}, u32[]{:S(2)}) collective-permute-start(f32[160,1280]{1,0:T(8,128)S(1)} %get-tuple-element.25), channel_id=1, source_target_pairs={{0,16},{16,0},{1,17},{17,1},{2,18},{18,2},{3,19},{19,3},{4,20},{20... | collective-permute-start | bytes 2457608 | tf_op jit(solution)/shard_map/ppermute | solution.py:22
  84.8 9.4 %collective-permute-start.3 = (f32[40,1280]{1,0:T(8,128)S(1)}, f32[40,1280]{1,0:T(8,128)S(1)}, u32[]{:S(2)}, u32[]{:S(2)}) collective-permute-start(f32[40,1280]{1,0:T(8,128)S(1)} %get-tuple-element.33), channel_id=1, source_target_pairs={{0,32},{32,64},{64,96},{96,0},{1,33},{33,65},{65,97},{97,1},{2,34}... | collective-permute-start | bytes 614408 | tf_op jit(solution)/shard_map/ppermute | solution.py:22
  87.6 18.4 %collective-permute-start.6 = (f32[40,1280]{1,0:T(8,128)S(1)}, f32[40,1280]{1,0:T(8,128)S(1)}, u32[]{:S(2)}, u32[]{:S(2)}) collective-permute-start(f32[40,1280]{1,0:T(8,128)S(1)} %get-tuple-element.31), channel_id=1, source_target_pairs={{0,96},{32,0},{64,32},{96,64},{1,97},{33,1},{65,33},{97,65},{2,98}... | collective-permute-start | bytes 614408 | tf_op jit(solution)/shard_map/ppermute | solution.py:22
  91.3 14.7 %collective-permute-start.5 = (f32[40,1280]{1,0:T(8,128)S(1)}, f32[40,1280]{1,0:T(8,128)S(1)}, u32[]{:S(2)}, u32[]{:S(2)}) collective-permute-start(f32[40,1280]{1,0:T(8,128)S(1)} %get-tuple-element.32), channel_id=1, source_target_pairs={{0,64},{32,96},{64,0},{96,32},{1,65},{33,97},{65,1},{97,33},{2,66}... | collective-permute-start | bytes 614408 | tf_op jit(solution)/shard_map/ppermute | solution.py:22
  102.5 15.0 %copy-start.1 = (f32[18,1536]{1,0:T(8,128)S(1)}, f32[18,1536]{1,0:T(8,128)}, u32[]{:S(2)}) copy-start(f32[18,1536]{1,0:T(8,128)} %get-tuple-element.27) | copy-start | bytes 331780
  102.5 25.8 %copy-start.3 = (f32[6,1280]{1,0:T(8,128)S(1)}, f32[6,1280]{1,0:T(8,128)}, u32[]{:S(2)}) copy-start(f32[6,1280]{1,0:T(8,128)} %get-tuple-element.29) | copy-start | bytes 92164
  103.0 14.5 %collective-permute-start.4 = (f32[18,1536]{1,0:T(8,128)S(1)}, f32[18,1536]{1,0:T(8,128)S(1)}, u32[]{:S(2)}, u32[]{:S(2)}) collective-permute-start(f32[18,1536]{1,0:T(8,128)S(1)} %slice.43), channel_id=1, source_target_pairs={{0,1},{1,0},{2,3},{3,2},{4,5},{5,4},{6,7},{7,6},{8,9},{9,8},{10,11... | collective-permute-start | bytes 331784 | tf_op jit(solution)/shard_map/ppermute | solution.py:22
  106.8 21.5 %all-to-all-start.3 = ((f32[6,6,1280]{2,1,0:T(8,128)}), f32[6,6,1280]{2,1,0:T(8,128)S(1)}, u32[]{:S(2)}, u32[]{:S(2)}) async-start(f32[6,6,1280]{2,1,0:T(8,128)} %reshape.218), calls=%async_computation.3 | async-start | bytes 491520 | tf_op jit(solution)/shard_map/all_to_all | solution.py:267

commit v6 on v5

--- a/solution.py
+++ b/solution.py
@@ -26,8 +26,8 @@
     return [(i, (i + by) % size) for i in range(size)]
 
 
-def gather(block, axis, size):
-    return lax.all_to_all(jnp.broadcast_to(block[None], (size,) + block.shape), axis, 0, 0)
+def copied(block, size):
+    return jnp.broadcast_to(block[None], (size,) + block.shape)
 
 
 def chooser(rows, count):
@@ -38,12 +38,23 @@
     return jnp.pad(block, ((0, count - block.shape[0]), (0, 0)))
 
 
+def copies(masked, held, arrived, axis):
+    parts = []
+    for j in range(masked.shape[axis] // TILE):
+        span = pl.ds(j * TILE, TILE)
+        at = (span, slice(None)) if axis == 0 else (slice(None), span)
+        parts.append(pltpu.make_async_copy(masked.at[at], held.at[at], arrived.at[j]))
+        parts[-1].start()
+    return parts
+
+
 def masked_kernel(
-    place, tile_mask, irrep, energy, pairs, occ, irreps, energies, blocks, masked, den_ab, den_cd, table, row, col
+    place, tile_mask, irrep, energy, pairs, occ, irreps, energies, blocks, masked, den_ab, den_cd,
+    table, held, kept, arrived, stored
 ):
-    step = pl.program_id(0)
-    rows_dev = row.shape[1]
-    cols_dev = col.shape[1]
+    rows_dev = den_ab.shape[1]
+    cols_dev = den_cd.shape[1]
+    parts = copies(blocks, held, arrived, 0)
 
     def window(start, head, count):
         lane = lax.broadcasted_iota(jnp.int32, (1, count), 1)
@@ -61,25 +72,27 @@
         for r in range(out.shape[0]):
             out[r : r + 1, :] = sums - (occ[pairs[0, first + r]] + occ[pairs[1, first + r]])
 
-    @pl.when(step == 0)
-    def _():
-        table[...] = jnp.zeros_like(table)
-        table[0:1, :NV] = irreps[...].astype(jnp.float32)
-        table[1:2, :NV] = energies[...]
-        labels, sums = window(place[0], place[1], rows_dev)
-        row[...] = jnp.broadcast_to(labels, row.shape)
-        denominators(den_ab, sums, place[4])
-        labels, sums = window(place[2], place[3], cols_dev)
-        col[...] = jnp.broadcast_to(labels, col.shape)
-        denominators(den_cd, sums, place[5])
-
-    across = row[0:1, pl.ds(pl.multiple_of(step * TILE, TILE), TILE)]
-    down = jnp.transpose(jnp.broadcast_to(across, (LANES, TILE)))
-    for c in range(cols_dev // LANES):
-        lanes = slice(c * LANES, (c + 1) * LANES)
-        label = jnp.where(tile_mask[step, c * LANES // TILE] == 1, col[0:1, lanes], -1.0)
-        block = blocks[:, lanes].astype(jnp.float32)
-        masked[:, lanes] = jnp.where(down == label, block, 0.0).astype(masked.dtype)
+    table[...] = jnp.zeros_like(table)
+    table[0:1, :NV] = irreps[...].astype(jnp.float32)
+    table[1:2, :NV] = energies[...]
+    row, sums = window(place[0], place[1], rows_dev)
+    denominators(den_ab, sums, place[4])
+    col, sums = window(place[2], place[3], cols_dev)
+    denominators(den_cd, sums, place[5])
+    leaving = []
+    for j, part in enumerate(parts):
+        span = slice(j * TILE, (j + 1) * TILE)
+        down = jnp.transpose(jnp.broadcast_to(row[:, span], (LANES, TILE)))
+        part.wait()
+        for c in range(cols_dev // LANES):
+            lanes = slice(c * LANES, (c + 1) * LANES)
+            label = jnp.where(tile_mask[j, c * LANES // TILE] == 1, col[:, lanes], -1.0)
+            block = held[span, lanes].astype(jnp.float32)
+            kept[span, lanes] = jnp.where(down == label, block, 0.0).astype(kept.dtype)
+        leaving.append(pltpu.make_async_copy(kept.at[span, :], masked.at[span, :], stored.at[j]))
+        leaving[-1].start()
+    for part in leaving:
+        part.wait()
 
 
 def ab_kernel(groups, used, choose, amps, masked, coded, chosen):
@@ -147,8 +160,7 @@
         to_zh = (zh + 1 + r // ab_count) % nzh
         k = ((out // y_pad) * nzh + to_zh) * ab_count + r % ab_count
         group = k // cd_count
-        offset = ((group - core) % ncore) * nx + (group // ncore) % nx
-        source = (offset * nzl + group // (nx * ncore)) * 8 + k % cd_count
+        source = ((group % (nx * ncore)) * nzl + group // (nx * ncore)) * 8 + k % cd_count
         return chooser(jnp.where(r < y_rows, source, -1), count)
 
     def cd_chooser():
@@ -162,9 +174,10 @@
     other = send(amp_ab, "zh", shift(nzh, 1))
     first = jnp.where(zh == 0, amp_ab, other)
     second = jnp.where(zh == 0, other, amp_ab)
-    both = pad_rows(jnp.concatenate([first, second], axis=0), y_pad)
-
-    own = gather(pad_rows(amp_cd, 8), "zl", nzl).reshape(nzl * 8, cols_dev)
+    both = copied(pad_rows(jnp.concatenate([first, second], axis=0), y_pad), ny)
+
+    own = jnp.pad(copied(amp_cd, nzl), ((0, 0), (0, 8 - cd_count), (0, 0)))
+    own = lax.all_to_all(own, "zl", 0, 0).reshape(nzl * 8, cols_dev)
 
     row_first = row_group * rows_dev
     col_first = nab + col_group * cols_dev
@@ -172,20 +185,11 @@
         [row_first % NV, row_first // NV, col_first % NV, col_first // NV, col_group * ab_count, row_group * cd_count]
     ).astype(jnp.int32)
     smem = pl.BlockSpec(memory_space=pltpu.SMEM)
+    vmem = pl.BlockSpec(memory_space=pltpu.VMEM)
     masked, den_ab, den_cd = pl.pallas_call(
         masked_kernel,
-        grid=(rows_dev // TILE,),
-        in_specs=[smem] * 6
-        + [
-            pl.BlockSpec((1, NV), lambda i: (0, 0)),
-            pl.BlockSpec((1, NV), lambda i: (0, 0)),
-            pl.BlockSpec((TILE, cols_dev), lambda i: (i, 0)),
-        ],
-        out_specs=[
-            pl.BlockSpec((TILE, cols_dev), lambda i: (i, 0)),
-            pl.BlockSpec((ab_count, rows_dev), lambda i: (0, 0)),
-            pl.BlockSpec((cd_count, cols_dev), lambda i: (0, 0)),
-        ],
+        in_specs=[smem] * 6 + [vmem, vmem, pl.BlockSpec(memory_space=pl.ANY)],
+        out_specs=[pl.BlockSpec(memory_space=pl.ANY), vmem, vmem],
         out_shape=[
             jax.ShapeDtypeStruct(integrals.shape, integrals.dtype),
             jax.ShapeDtypeStruct((ab_count, rows_dev), jnp.float32),
@@ -193,8 +197,10 @@
         ],
         scratch_shapes=[
             pltpu.VMEM((8, TABLE), jnp.float32),
-            pltpu.VMEM((8, rows_dev), jnp.float32),
-            pltpu.VMEM((8, cols_dev), jnp.float32),
+            pltpu.VMEM(integrals.shape, integrals.dtype),
+            pltpu.VMEM(integrals.shape, integrals.dtype),
+            pltpu.SemaphoreType.DMA((rows_dev // TILE,)),
+            pltpu.SemaphoreType.DMA((rows_dev // TILE,)),
         ],
         compiler_params=pltpu.CompilerParams(vmem_limit_bytes=MASK_LIMIT),
         cost_estimate=pl.CostEstimate(flops=4 * rows_dev * cols_dev, bytes_accessed=4 * rows_dev * cols_dev, transcendentals=0),
@@ -213,9 +219,8 @@
 
     choose_ab, choose_cd = ab_chooser(), cd_chooser()
     own, masked, both, choose_ab, choose_cd = lax.optimization_barrier((own, masked, both, choose_ab, choose_cd))
-    own = lax.all_gather(own, "x", axis=0, tiled=True)
-    all_cd = jnp.concatenate([own, send(own, "core", shift(ncore, 1))], axis=0)
-    all_ab = gather(both, "y", ny).reshape(ab_rows, rows_dev)
+    all_cd = lax.all_gather(own, ("x", "core"), axis=0, tiled=True)
+    all_ab = lax.all_to_all(both, "y", 0, 0).reshape(ab_rows, rows_dev)
 
     coded = pl.pallas_call(
         functools.partial(ab_kernel, ny, y_rows),

time: 130 us -> 124 us (0.954)
  starting transfers between devices: 64.1 us -> 53.4 us
  blocking collectives: 10.2 us -> 17.9 us
  Pallas kernels: 19.8 us -> 18.5 us
    ppermute x7 -> x6, starting transfers between devices: 38.5 us -> 30.4 us  [send(): return lax.ppermute(block, axis, pairs)]
    all_gather x1, blocking collectives: 10.2 us -> 17.9 us  [local(): all_cd = lax.all_gather(own, ('x', 'core'), axis=0, tiled=True)]
    all_to_all x1, waiting for transfers between devices: 10.1 us -> 4.71 us  [local(): ladder_cd = jnp.sum(lax.all_to_all(total, 'zl', 0, 0), axis=0)]
    ppermute x7 -> x6, waiting for transfers between devices: 8.4 us -> 11.9 us  [send(): return lax.ppermute(block, axis, pairs)]
    all_to_all x1, starting transfers between devices: 6.07 us -> 3.41 us  [local(): ladder_cd = jnp.sum(lax.all_to_all(total, 'zl', 0, 0), axis=0)]
    all_to_all x2, waiting for transfers between devices: 0.04 us -> 1.54 us  [the longest x1 1.32 us: local(): own = lax.all_to_all(own, 'zl', 0, 0).reshape(nzl * 8, cols_dev)]
  transfers between devices with their start and end apart: 11 -> 10, of which waited for: 6 -> 7; matrix products, arithmetic and copies ran while one was open for 4% -> 4% of each run, Pallas kernels for 15% -> 15%
where the time goes in v6:
time: 124 us; the launch traced here: 123 us
  starting transfers between devices  53.4 us (43%)
  waiting for transfers between devices  26.3 us (21%)
  Pallas kernels  18.5 us (15%)
  blocking collectives  17.9 us (14%)
  local copies, waits for them, and re-layouts  4.16 us (3%)
  other arithmetic  2.29 us (2%)
    ppermute x6, starting transfers between devices, send(): return lax.ppermute(block, axis, pairs)  30.4 us
    all_gather x1, blocking collectives, local(): all_cd = lax.all_gather(own, ('x', 'core'), axis=0, tiled=True)  17.9 us
    ppermute x6, waiting for transfers between devices, send(): return lax.ppermute(block, axis, pairs)  11.9 us
    all_to_all x1, waiting for transfers between devices, local(): coded = lax.all_to_all(coded.reshape(ny, y_pad, rows_dev), 'y', 0, 0)  8.16 us
    pallas_call x1, Pallas kernels, local(): pl.pallas_call(functools.partial(ab_kernel, ny, y_rows), grid=(rows_dev /...  7.27 us
    all_to_all x1, starting transfers between devices, local(): all_ab = lax.all_to_all(both, 'y', 0, 0).reshape(ab_rows, rows_dev)  6.82 us
    all_to_all x1, starting transfers between devices, local(): coded = lax.all_to_all(coded.reshape(ny, y_pad, rows_dev), 'y', 0, 0)  6.71 us
    all_to_all x1, starting transfers between devices, local(): own = lax.all_to_all(own, 'zl', 0, 0).reshape(nzl * 8, cols_dev)  6.1 us
  transfers between devices with their start and end apart: 10, of which 7 were waited for; matrix products, arithmetic and copies ran while one was open for 4% of the time, Pallas kernels for 15%

profile of v6, /device:TPU:1, one launch (start us, length us, event | category | flops | bytes accessed | tf_op | source)
XLA Modules:
  0.0 123.5 jit_solution(17593887506170588175)
XLA Ops:
  0.6 15.7 %collective-permute-start = (bf16[18,1536]{1,0:T(8,128)(2,1)}, bf16[18,1536]{1,0:T(8,128)(2,1)S(1)}, u32[]{:S(2)}, u32[]{:S(2)}) collective-permute-start(bf16[18,1536]{1,0:T(8,128)(2,1)} %param.14), channel_id=1, source_target_pairs={{0,1},{1,0},{2,3},{3,2},{4,5},{5,4},{6,7},{7,6},{8,9},{9,8},{10,11... | collective-permute-start | bytes 165896 | tf_op jit(solution)/shard_map/ppermute | solution.py:22
  16.3 0.7 broadcast_in_dim.6
  17.1 0.7 pad.8
  17.7 6.1 %all-to-all-start = ((bf16[6,8,1280]{2,1,0:T(8,128)(2,1)}), bf16[6,8,1280]{2,1,0:T(8,128)(2,1)S(1)}, u32[]{:S(2)}, u32[]{:S(2)}) async-start(bf16[6,8,1280]{2,1,0:T(8,128)(2,1)} %pad.8), calls=%async_computation | async-start | bytes 245760 | tf_op jit(solution)/shard_map/all_to_all | solution.py:180
  23.8 0.1 fusion.17
  23.9 0.1 fusion.choose
  24.1 0.1 fusion.1.choose
  24.2 0.6 stack.27.place
  24.9 0.0 copy-start.2
  24.9 5.4 %masked.1 = (bf16[1536,1280]{1,0:T(8,128)(2,1)}, f32[18,1536]{1,0:T(8,128)}, f32[6,1280]{1,0:T(8,128)}) custom-call(s32[6]{0:T(128)} %stack.27.place, s32[6,5]{1,0:T(8,128)} %tile_mask.1, s32[1000]{0:T(1024)} %irrep.1, f32[1000]{0:T(1024)} %energy.1, s32[2,288]{1,0:T(2,128)} %pairs.1, f32[100]{0:T(128)} %occ.1, s32[1,1000]{1,0:T(1,128)} %bitcast.15, ...), custom_call_target="tpu_custom_call" | custom-call | flops 7864320 | bytes 7864320 | tf_op jit(solution)/shard_map/masked/pallas_call | solution.py:189
  30.3 0.0 collective-permute-done
  30.3 0.0 copy-done.2
  30.4 1.3 %all-to-all-done = bf16[6,8,1280]{2,1,0:T(8,128)(2,1)S(1)} async-done(((bf16[6,8,1280]{2,1,0:T(8,128)(2,1)}), bf16[6,8,1280]{2,1,0:T(8,128)(2,1)S(1)}, u32[]{:S(2)}, u32[]{:S(2)}) %all-to-all-start) | async-done | bytes 122912 | tf_op jit(solution)/shard_map/all_to_all | solution.py:180
  31.7 1.0 broadcast_in_dim.7
  32.7 6.8 %all-to-all-start.1 = ((bf16[8,40,1536]{2,1,0:T(8,128)(2,1)}), bf16[8,40,1536]{2,1,0:T(8,128)(2,1)S(1)}, u32[]{:S(2)}, u32[]{:S(2)}) async-start(bf16[8,40,1536]{2,1,0:T(8,128)(2,1)} %broadcast_in_dim.7), calls=%async_computation.1 | async-start | bytes 1966080 | tf_op jit(solution)/shard_map/all_to_all | solution.py:223
  39.6 17.9 %all_gather.3.amps = bf16[384,1280]{1,0:T(8,128)(2,1)} all-gather(bf16[48,1280]{1,0:T(8,128)(2,1)S(1)} %bitcast.14), channel_id=1, replica_groups=mesh['zl'=6,'x'=4,'core'=2,'y'=8,'zh'=2] {'x','core'}, dimensions={0}, use_global_device_ids=true | all-gather | bytes 1105920 | tf_op jit(solution)/shard_map/all_gather | solution.py:222
  57.5 7.3 %ab_product.1 = s16[320,1536]{1,0:T(8,128)(2,1)} custom-call(bf16[320,384]{1,0:T(8,128)(2,1)S(1)} %fusion.choose, bf16[384,1280]{1,0:T(8,128)(2,1)} %all_gather.3.amps, bf16[1536,1280]{1,0:T(8,128)(2,1)} %get-tuple-element.20.masked), custom_call_target="tpu_custom_call" | custom-call | flops 1572864000 | bytes 3932160 | tf_op jit(solution)/shard_map/ab_product/pallas_call | solution.py:225
  64.8 0.2 all-to-all-done.1
  65.0 0.0 copy-start
  65.0 6.7 %all-to-all-start.2 = ((s16[8,40,1536]{2,1,0:T(8,128)(2,1)}), s16[8,40,1536]{2,1,0:T(8,128)(2,1)S(1)}, u32[]{:S(2)}, u32[]{:S(2)}) async-start(s16[8,40,1536]{2,1,0:T(8,128)(2,1)} %bitcast.10), calls=%async_computation.2 | async-start | bytes 1966080 | tf_op jit(solution)/shard_map/all_to_all | solution.py:262
  71.7 0.0 copy-done
  71.7 5.8 %cd_product.1 = (f32[160,1280]{1,0:T(8,128)S(1)}, f32[160,1280]{1,0:T(8,128)S(1)}) custom-call(bf16[320,320]{1,0:T(8,128)(2,1)S(1)} %fusion.1.choose, bf16[320,1536]{1,0:T(8,128)(2,1)} %bitcast.13, bf16[1536,1280]{1,0:T(8,128)(2,1)} %get-tuple-element.20.masked), custom_call_target="tpu_custom_call" | custom-call | flops 1572864000 | bytes 3932160 | tf_op jit(solution)/shard_map/cd_product/pallas_call | solution.py:244
  77.5 2.4 %collective-permute-start.1 = (f32[160,1280]{1,0:T(8,128)S(1)}, f32[160,1280]{1,0:T(8,128)S(1)}, u32[]{:S(2)}, u32[]{:S(2)}) collective-permute-start(f32[160,1280]{1,0:T(8,128)S(1)} %get-tuple-element.25), channel_id=1, source_target_pairs={{0,16},{16,0},{1,17},{17,1},{2,18},{18,2},{3,19},{19,3},{4,20},{20... | collective-permute-start | bytes 2457608 | tf_op jit(solution)/shard_map/ppermute | solution.py:22
  79.8 1.9 %collective-permute-done.1 = f32[160,1280]{1,0:T(8,128)S(1)} collective-permute-done((f32[160,1280]{1,0:T(8,128)S(1)}, f32[160,1280]{1,0:T(8,128)S(1)}, u32[]{:S(2)}, u32[]{:S(2)}) %collective-permute-start.1) | collective-permute-done | bytes 819232 | tf_op jit(solution)/shard_map/ppermute | solution.py:22
  81.8 0.1 add.282
  81.9 0.1 fusion.40
  81.9 2.8 %collective-permute-start.2 = (f32[40,1280]{1,0:T(8,128)S(1)}, f32[40,1280]{1,0:T(8,128)S(1)}, u32[]{:S(2)}, u32[]{:S(2)}) collective-permute-start(f32[40,1280]{1,0:T(8,128)S(1)} %get-tuple-element.33), channel_id=1, source_target_pairs={{0,32},{32,64},{64,96},{96,0},{1,33},{33,65},{65,97},{97,1},{2,34}... | collective-permute-start | bytes 614408 | tf_op jit(solution)/shard_map/ppermute | solution.py:22
  84.7 3.7 %collective-permute-start.5 = (f32[40,1280]{1,0:T(8,128)S(1)}, f32[40,1280]{1,0:T(8,128)S(1)}, u32[]{:S(2)}, u32[]{:S(2)}) collective-permute-start(f32[40,1280]{1,0:T(8,128)S(1)} %get-tuple-element.31), channel_id=1, source_target_pairs={{0,96},{32,0},{64,32},{96,64},{1,97},{33,1},{65,33},{97,65},{2,98}... | collective-permute-start | bytes 614408 | tf_op jit(solution)/shard_map/ppermute | solution.py:22
  88.4 2.8 %collective-permute-start.4 = (f32[40,1280]{1,0:T(8,128)S(1)}, f32[40,1280]{1,0:T(8,128)S(1)}, u32[]{:S(2)}, u32[]{:S(2)}) collective-permute-start(f32[40,1280]{1,0:T(8,128)S(1)} %get-tuple-element.32), channel_id=1, source_target_pairs={{0,64},{32,96},{64,0},{96,32},{1,65},{33,97},{65,1},{97,33},{2,66}... | collective-permute-start | bytes 614408 | tf_op jit(solution)/shard_map/ppermute | solution.py:22
  91.2 0.1 collective-permute-done.2
  91.3 8.2 %all-to-all-done.2 = s16[8,40,1536]{2,1,0:T(8,128)(2,1)S(1)} async-done(((s16[8,40,1536]{2,1,0:T(8,128)(2,1)}), s16[8,40,1536]{2,1,0:T(8,128)(2,1)S(1)}, u32[]{:S(2)}, u32[]{:S(2)}) %all-to-all-start.2) | async-done | bytes 983072 | tf_op jit(solution)/shard_map/all_to_all | solution.py:262
  99.5 0.3 copy.11
  99.8 0.0 copy-start.1
  99.8 0.0 copy-start.3
  99.8 0.4 multiply_reduce_fusion
  100.3 3.1 %collective-permute-start.3 = (f32[18,1536]{1,0:T(8,128)S(1)}, f32[18,1536]{1,0:T(8,128)S(1)}, u32[]{:S(2)}, u32[]{:S(2)}) collective-permute-start(f32[18,1536]{1,0:T(8,128)S(1)} %slice.43), channel_id=1, source_target_pairs={{0,1},{1,0},{2,3},{3,2},{4,5},{5,4},{6,7},{7,6},{8,9},{9,8},{10,11... | collective-permute-start | bytes 331784 | tf_op jit(solution)/shard_map/ppermute | solution.py:22
  103.3 0.0 collective-permute-done.5
  103.3 0.0 collective-permute-done.4
  103.4 0.1 fusion.4
  103.4 0.7 reshape.194
  104.1 3.4 %all-to-all-start.3 = ((f32[6,6,1280]{2,1,0:T(8,128)}), f32[6,6,1280]{2,1,0:T(8,128)S(1)}, u32[]{:S(2)}, u32[]{:S(2)}) async-start(f32[6,6,1280]{2,1,0:T(8,128)} %reshape.194), calls=%async_computation.3 | async-start | bytes 491520 | tf_op jit(solution)/shard_map/all_to_all | solution.py:272
  107.5 9.8 %collective-permute-done.3 = f32[18,1536]{1,0:T(8,128)S(1)} collective-permute-done((f32[18,1536]{1,0:T(8,128)S(1)}, f32[18,1536]{1,0:T(8,128)S(1)}, u32[]{:S(2)}, u32[]{:S(2)}) %collective-permute-start.3) | collective-permute-done | bytes 110624 | tf_op jit(solution)/shard_map/ppermute | solution.py:22
  117.4 0.0 copy-done.1
  117.4 0.7 fusion.5
  118.1 4.7 %all-to-all-done.3 = f32[6,6,1280]{2,1,0:T(8,128)S(1)} async-done(((f32[6,6,1280]{2,1,0:T(8,128)}), f32[6,6,1280]{2,1,0:T(8,128)S(1)}, u32[]{:S(2)}, u32[]{:S(2)}) %all-to-all-start.3) | async-done | bytes 184352 | tf_op jit(solution)/shard_map/all_to_all | solution.py:272
  122.8 0.0 copy-done.3
  122.8 0.6 div.93
  (6 shorter events, 0.2 us)
Async XLA Ops:
  0.6 29.7 %collective-permute-start = (bf16[18,1536]{1,0:T(8,128)(2,1)}, bf16[18,1536]{1,0:T(8,128)(2,1)S(1)}, u32[]{:S(2)}, u32[]{:S(2)}) collective-permute-start(bf16[18,1536]{1,0:T(8,128)(2,1)} %param.14), channel_id=1, source_target_pairs={{0,1},{1,0},{2,3},{3,2},{4,5},{5,4},{6,7},{7,6},{8,9},{9,8},{10,11... | collective-permute-start | bytes 165896 | tf_op jit(solution)/shard_map/ppermute | solution.py:22
  17.7 14.0 %all-to-all-start = ((bf16[6,8,1280]{2,1,0:T(8,128)(2,1)}), bf16[6,8,1280]{2,1,0:T(8,128)(2,1)S(1)}, u32[]{:S(2)}, u32[]{:S(2)}) async-start(bf16[6,8,1280]{2,1,0:T(8,128)(2,1)} %pad.8), calls=%async_computation | async-start | bytes 245760 | tf_op jit(solution)/shard_map/all_to_all | solution.py:180
  24.9 5.4 %copy-start.2 = (bf16[18,1536]{1,0:T(8,128)(2,1)S(1)}, bf16[18,1536]{1,0:T(8,128)(2,1)}, u32[]{:S(2)}) copy-start(bf16[18,1536]{1,0:T(8,128)(2,1)} %param.14) | copy-start | bytes 165892
  32.7 32.2 %all-to-all-start.1 = ((bf16[8,40,1536]{2,1,0:T(8,128)(2,1)}), bf16[8,40,1536]{2,1,0:T(8,128)(2,1)S(1)}, u32[]{:S(2)}, u32[]{:S(2)}) async-start(bf16[8,40,1536]{2,1,0:T(8,128)(2,1)} %broadcast_in_dim.7), calls=%async_computation.1 | async-start | bytes 1966080 | tf_op jit(solution)/shard_map/all_to_all | solution.py:223
  65.0 6.7 %copy-start = (bf16[8,40,1536]{2,1,0:T(8,128)(2,1)}, bf16[8,40,1536]{2,1,0:T(8,128)(2,1)S(1)}, u32[]{:S(2)}) copy-start(bf16[8,40,1536]{2,1,0:T(8,128)(2,1)S(1)} %all-to-all-done.1) | copy-start | bytes 2949124
  65.0 34.5 %all-to-all-start.2 = ((s16[8,40,1536]{2,1,0:T(8,128)(2,1)}), s16[8,40,1536]{2,1,0:T(8,128)(2,1)S(1)}, u32[]{:S(2)}, u32[]{:S(2)}) async-start(s16[8,40,1536]{2,1,0:T(8,128)(2,1)} %bitcast.10), calls=%async_computation.2 | async-start | bytes 1966080 | tf_op jit(solution)/shard_map/all_to_all | solution.py:262
  77.5 4.3 %collective-permute-start.1 = (f32[160,1280]{1,0:T(8,128)S(1)}, f32[160,1280]{1,0:T(8,128)S(1)}, u32[]{:S(2)}, u32[]{:S(2)}) collective-permute-start(f32[160,1280]{1,0:T(8,128)S(1)} %get-tuple-element.25), channel_id=1, source_target_pairs={{0,16},{16,0},{1,17},{17,1},{2,18},{18,2},{3,19},{19,3},{4,20},{20... | collective-permute-start | bytes 2457608 | tf_op jit(solution)/shard_map/ppermute | solution.py:22
  81.9 9.4 %collective-permute-start.2 = (f32[40,1280]{1,0:T(8,128)S(1)}, f32[40,1280]{1,0:T(8,128)S(1)}, u32[]{:S(2)}, u32[]{:S(2)}) collective-permute-start(f32[40,1280]{1,0:T(8,128)S(1)} %get-tuple-element.33), channel_id=1, source_target_pairs={{0,32},{32,64},{64,96},{96,0},{1,33},{33,65},{65,97},{97,1},{2,34}... | collective-permute-start | bytes 614408 | tf_op jit(solution)/shard_map/ppermute | solution.py:22
  84.7 18.6 %collective-permute-start.5 = (f32[40,1280]{1,0:T(8,128)S(1)}, f32[40,1280]{1,0:T(8,128)S(1)}, u32[]{:S(2)}, u32[]{:S(2)}) collective-permute-start(f32[40,1280]{1,0:T(8,128)S(1)} %get-tuple-element.31), channel_id=1, source_target_pairs={{0,96},{32,0},{64,32},{96,64},{1,97},{33,1},{65,33},{97,65},{2,98}... | collective-permute-start | bytes 614408 | tf_op jit(solution)/shard_map/ppermute | solution.py:22
  88.4 14.9 %collective-permute-start.4 = (f32[40,1280]{1,0:T(8,128)S(1)}, f32[40,1280]{1,0:T(8,128)S(1)}, u32[]{:S(2)}, u32[]{:S(2)}) collective-permute-start(f32[40,1280]{1,0:T(8,128)S(1)} %get-tuple-element.32), channel_id=1, source_target_pairs={{0,64},{32,96},{64,0},{96,32},{1,65},{33,97},{65,1},{97,33},{2,66}... | collective-permute-start | bytes 614408 | tf_op jit(solution)/shard_map/ppermute | solution.py:22
  99.8 17.6 %copy-start.1 = (f32[18,1536]{1,0:T(8,128)S(1)}, f32[18,1536]{1,0:T(8,128)}, u32[]{:S(2)}) copy-start(f32[18,1536]{1,0:T(8,128)} %get-tuple-element.27) | copy-start | bytes 331780
  99.8 23.0 %copy-start.3 = (f32[6,1280]{1,0:T(8,128)S(1)}, f32[6,1280]{1,0:T(8,128)}, u32[]{:S(2)}) copy-start(f32[6,1280]{1,0:T(8,128)} %get-tuple-element.29) | copy-start | bytes 92164
  100.3 17.1 %collective-permute-start.3 = (f32[18,1536]{1,0:T(8,128)S(1)}, f32[18,1536]{1,0:T(8,128)S(1)}, u32[]{:S(2)}, u32[]{:S(2)}) collective-permute-start(f32[18,1536]{1,0:T(8,128)S(1)} %slice.43), channel_id=1, source_target_pairs={{0,1},{1,0},{2,3},{3,2},{4,5},{5,4},{6,7},{7,6},{8,9},{9,8},{10,11... | collective-permute-start | bytes 331784 | tf_op jit(solution)/shard_map/ppermute | solution.py:22
  104.1 18.7 %all-to-all-start.3 = ((f32[6,6,1280]{2,1,0:T(8,128)}), f32[6,6,1280]{2,1,0:T(8,128)S(1)}, u32[]{:S(2)}, u32[]{:S(2)}) async-start(f32[6,6,1280]{2,1,0:T(8,128)} %reshape.194), calls=%async_computation.3 | async-start | bytes 491520 | tf_op jit(solution)/shard_map/all_to_all | solution.py:272

commit v7 on v6

--- a/solution.py
+++ b/solution.py
@@ -14,7 +14,7 @@
 TABLE = 2048
 AB = ("zl", "x", "core")
 CD = ("y", "zh")
-VMEM_LIMIT = 52 * 1024 * 1024
+VMEM_LIMIT = 50 * 1024 * 1024
 MASK_LIMIT = 60 * 1024 * 1024
 
 
@@ -95,32 +95,40 @@
         part.wait()
 
 
-def ab_kernel(groups, used, choose, amps, masked, coded, chosen):
+def pick(choose, amps, chosen):
+    for c in range(0, amps.shape[1], TILE):
+        part = jnp.dot(choose[...], amps[:, c : c + TILE], preferred_element_type=jnp.float32)
+        chosen[:, c : c + TILE] = part.astype(chosen.dtype)
+
+
+def ab_kernel(groups, used, choose, amps, masked, coded, chosen, held, arrived):
+    parts = copies(masked, held, arrived, 0)
+    pick(choose, amps, chosen)
+    for j, part in enumerate(parts):
+        part.wait()
+        span = slice(j * TILE, (j + 1) * TILE)
+        sums = lax.dot_general(
+            chosen[...], held[span, :], (((1,), (1,)), ((), ())), preferred_element_type=jnp.float32
+        )
+        rows, columns = sums.shape
+        sums = sums.reshape(groups, rows // groups, columns)
+        largest = jnp.max(jnp.abs(sums), axis=1, keepdims=True)
+        scale = jnp.ceil(jnp.log2(jnp.maximum(largest, 2.0**-120)) * 256.0)
+        whole = jnp.floor(sums * jnp.exp2(scale * (-1.0 / 256.0)) * 32767.0 + 0.5)
+        place = lax.broadcasted_iota(jnp.int32, sums.shape, 1)
+        whole = jnp.clip(jnp.where(place == used, scale, whole), -32767.0, 32767.0)
+        coded[:, span] = whole.reshape(rows, columns).astype(jnp.int32).astype(jnp.int16)
+
+
+def cd_kernel(choose, amps, masked, keep, give, chosen):
+    rows, side = chosen.shape[0], amps.shape[1]
+
     @pl.when(pl.program_id(0) == 0)
     def _():
-        for c in range(0, amps.shape[1], TILE):
+        for c in range(0, side, TILE):
             part = jnp.dot(choose[...], amps[:, c : c + TILE], preferred_element_type=jnp.float32)
-            chosen[:, c : c + TILE] = part.astype(chosen.dtype)
-
-    sums = lax.dot_general(
-        chosen[...], masked[...], (((1,), (1,)), ((), ())), preferred_element_type=jnp.float32
-    )
-    rows, columns = sums.shape
-    sums = sums.reshape(groups, rows // groups, columns)
-    largest = jnp.max(jnp.abs(sums), axis=1, keepdims=True)
-    scale = jnp.ceil(jnp.log2(jnp.maximum(largest, 2.0**-120)) * 256.0)
-    parts = jnp.floor(sums * jnp.exp2(scale * (-1.0 / 256.0)) * 32767.0 + 0.5)
-    place = lax.broadcasted_iota(jnp.int32, sums.shape, 1)
-    parts = jnp.clip(jnp.where(place == used, scale, parts), -32767.0, 32767.0)
-    coded[...] = parts.reshape(rows, columns).astype(jnp.int32).astype(jnp.int16)
-
-
-def cd_kernel(choose, amps, masked, keep, give, chosen):
-    @pl.when(pl.program_id(0) == 0)
-    def _():
-        for c in range(0, amps.shape[1], TILE):
-            part = jnp.dot(choose[...], amps[:, c : c + TILE], preferred_element_type=jnp.float32)
-            chosen[:, c : c + TILE] = part.astype(chosen.dtype)
+            chosen[:, c : c + TILE] = part[:rows].astype(chosen.dtype)
+            chosen[:, side + c : side + c + TILE] = part[rows:].astype(chosen.dtype)
 
     sums = jnp.dot(chosen[...], masked[...], preferred_element_type=jnp.float32)
     half = keep.shape[0]
@@ -169,12 +177,16 @@
         to_x = (x + out // x_pad) % nx
         to_core = (core + out // (x_pad * nx)) % ncore
         k = ((r // cd_count * nx + to_x) * ncore + to_core) * cd_count + r % cd_count
-        return chooser(jnp.where(r < x_rows, k // y_rows * y_pad + k % y_rows, -1), ab_rows)
+        source = k // y_rows * 2 * y_rows + k % y_rows
+        source = jnp.concatenate([jnp.where(r < x_rows, source + part, -1) for part in (0, y_rows)])
+        return chooser(source, 2 * ny * y_rows)
 
     other = send(amp_ab, "zh", shift(nzh, 1))
     first = jnp.where(zh == 0, amp_ab, other)
     second = jnp.where(zh == 0, other, amp_ab)
-    both = copied(pad_rows(jnp.concatenate([first, second], axis=0), y_pad), ny)
+    side = rows_dev // 2
+    both = jnp.concatenate([first[:, :side], second[:, :side], first[:, side:], second[:, side:]], axis=0)
+    both = copied(both, ny)
 
     own = jnp.pad(copied(amp_cd, nzl), ((0, 0), (0, 8 - cd_count), (0, 0)))
     own = lax.all_to_all(own, "zl", 0, 0).reshape(nzl * 8, cols_dev)
@@ -220,19 +232,18 @@
     choose_ab, choose_cd = ab_chooser(), cd_chooser()
     own, masked, both, choose_ab, choose_cd = lax.optimization_barrier((own, masked, both, choose_ab, choose_cd))
     all_cd = lax.all_gather(own, ("x", "core"), axis=0, tiled=True)
-    all_ab = lax.all_to_all(both, "y", 0, 0).reshape(ab_rows, rows_dev)
+    all_ab = lax.all_to_all(both, "y", 0, 0).reshape(2 * ny * y_rows, side)
 
     coded = pl.pallas_call(
         functools.partial(ab_kernel, ny, y_rows),
-        grid=(rows_dev // TILE,),
-        in_specs=[
-            pl.BlockSpec((ab_rows, count), lambda i: (0, 0)),
-            pl.BlockSpec((count, cols_dev), lambda i: (0, 0)),
-            pl.BlockSpec((TILE, cols_dev), lambda i: (i, 0)),
-        ],
-        out_specs=pl.BlockSpec((ab_rows, TILE), lambda i: (0, i)),
+        in_specs=[vmem, vmem, pl.BlockSpec(memory_space=pl.ANY)],
+        out_specs=vmem,
         out_shape=jax.ShapeDtypeStruct((ab_rows, rows_dev), jnp.int16),
-        scratch_shapes=[pltpu.VMEM((ab_rows, cols_dev), jnp.bfloat16)],
+        scratch_shapes=[
+            pltpu.VMEM((ab_rows, cols_dev), jnp.bfloat16),
+            pltpu.VMEM((rows_dev, cols_dev), jnp.bfloat16),
+            pltpu.SemaphoreType.DMA((rows_dev // TILE,)),
+        ],
         compiler_params=params,
         cost_estimate=pl.CostEstimate(
             flops=2 * ab_rows * cols_dev * (rows_dev + count), bytes_accessed=2 * rows_dev * cols_dev, transcendentals=0
@@ -245,8 +256,8 @@
         cd_kernel,
         grid=(cols_dev // TILE,),
         in_specs=[
-            pl.BlockSpec((cd_rows, ab_rows), lambda i: (0, 0)),
-            pl.BlockSpec((ab_rows, rows_dev), lambda i: (0, 0)),
+            pl.BlockSpec((2 * cd_rows, 2 * ny * y_rows), lambda i: (0, 0)),
+            pl.BlockSpec((2 * ny * y_rows, side), lambda i: (0, 0)),
             pl.BlockSpec((rows_dev, TILE), lambda i: (0, i)),
         ],
         out_specs=[pl.BlockSpec((half, TILE), lambda i: (0, i))] * 2,

time: 124 us -> 123 us (level)
  transfers between devices with their start and end apart: 10 -> 10, of which waited for: 7 -> 6; matrix products, arithmetic and copies ran while one was open for 4% -> 4% of each run, Pallas kernels for 15% -> 14%
where the time goes in v7:
time: 123 us; the launch traced here: 122 us
  starting transfers between devices  53.4 us (43%)
  waiting for transfers between devices  26.7 us (22%)
  Pallas kernels  17.6 us (14%)
  blocking collectives  17 us (14%)
  local copies, waits for them, and re-layouts  4.11 us (3%)
  other arithmetic  2.47 us (2%)
    ppermute x6, starting transfers between devices, send(): return lax.ppermute(block, axis, pairs)  30.1 us
    all_gather x1, blocking collectives, local(): all_cd = lax.all_gather(own, ('x', 'core'), axis=0, tiled=True)  17 us
    ppermute x6, waiting for transfers between devices, send(): return lax.ppermute(block, axis, pairs)  11.9 us
    all_to_all x1, waiting for transfers between devices, local(): coded = lax.all_to_all(coded.reshape(ny, y_pad, rows_dev), 'y', 0, 0)  8.27 us
    all_to_all x1, starting transfers between devices, local(): coded = lax.all_to_all(coded.reshape(ny, y_pad, rows_dev), 'y', 0, 0)  6.94 us
    all_to_all x1, starting transfers between devices, local(): all_ab = lax.all_to_all(both, 'y', 0, 0).reshape(2 * ny * y_rows, side)  6.82 us
    pallas_call x1, Pallas kernels, local(): pl.pallas_call(functools.partial(ab_kernel, ny, y_rows), in_specs=[vmem,...  6.45 us
    all_to_all x1, starting transfers between devices, local(): own = lax.all_to_all(own, 'zl', 0, 0).reshape(nzl * 8, cols_dev)  6.1 us
  transfers between devices with their start and end apart: 10, of which 6 were waited for; matrix products, arithmetic and copies ran while one was open for 4% of the time, Pallas kernels for 14%

profile of v7, /device:TPU:1, one launch (start us, length us, event | category | flops | bytes accessed | tf_op | source)
XLA Modules:
  0.0 122.1 jit_solution(10515738886081584872)
XLA Ops:
  0.6 15.7 %collective-permute-start = (bf16[18,1536]{1,0:T(8,128)(2,1)}, bf16[18,1536]{1,0:T(8,128)(2,1)S(1)}, u32[]{:S(2)}, u32[]{:S(2)}) collective-permute-start(bf16[18,1536]{1,0:T(8,128)(2,1)} %param.14), channel_id=1, source_target_pairs={{0,1},{1,0},{2,3},{3,2},{4,5},{5,4},{6,7},{7,6},{8,9},{9,8},{10,11... | collective-permute-start | bytes 165896 | tf_op jit(solution)/shard_map/ppermute | solution.py:22
  16.3 0.7 broadcast_in_dim.7
  17.1 0.7 pad.4
  17.7 6.1 %all-to-all-start = ((bf16[6,8,1280]{2,1,0:T(8,128)(2,1)}), bf16[6,8,1280]{2,1,0:T(8,128)(2,1)S(1)}, u32[]{:S(2)}, u32[]{:S(2)}) async-start(bf16[6,8,1280]{2,1,0:T(8,128)(2,1)} %pad.4), calls=%async_computation | async-start | bytes 245760 | tf_op jit(solution)/shard_map/all_to_all | solution.py:192
  23.8 0.1 fusion.14
  23.9 0.1 pad_add_fusion
  24.0 0.2 fusion.choose
  24.2 0.1 fusion.1.choose
  24.4 0.6 stack.27.place
  25.0 0.0 copy-start.1
  25.0 5.4 %masked.1 = (bf16[1536,1280]{1,0:T(8,128)(2,1)}, f32[18,1536]{1,0:T(8,128)}, f32[6,1280]{1,0:T(8,128)}) custom-call(s32[6]{0:T(128)} %stack.27.place, s32[6,5]{1,0:T(8,128)} %tile_mask.1, s32[1000]{0:T(1024)} %irrep.1, f32[1000]{0:T(1024)} %energy.1, s32[2,288]{1,0:T(2,128)} %pairs.1, f32[100]{0:T(128)} %occ.1, s32[1,1000]{1,0:T(1,128)} %bitcast.15, ...), custom_call_target="tpu_custom_call" | custom-call | flops 7864320 | bytes 7864320 | tf_op jit(solution)/shard_map/masked/pallas_call | solution.py:201
  30.4 0.0 collective-permute-done
  30.4 0.0 copy-done.1
  30.6 1.1 all-to-all-done
  31.7 1.0 broadcast_in_dim.8
  32.7 6.8 %all-to-all-start.1 = ((bf16[8,72,768]{2,1,0:T(8,128)(2,1)}), bf16[8,72,768]{2,1,0:T(8,128)(2,1)S(1)}, u32[]{:S(2)}, u32[]{:S(2)}) async-start(bf16[8,72,768]{2,1,0:T(8,128)(2,1)} %broadcast_in_dim.8), calls=%async_computation.1 | async-start | bytes 1769472 | tf_op jit(solution)/shard_map/all_to_all | solution.py:235
  39.5 17.0 %all_gather.3.amps = bf16[384,1280]{1,0:T(8,128)(2,1)S(1)} all-gather(bf16[48,1280]{1,0:T(8,128)(2,1)S(1)} %bitcast.14), channel_id=1, replica_groups=mesh['zl'=6,'x'=4,'core'=2,'y'=8,'zh'=2] {'x','core'}, dimensions={0}, use_global_device_ids=true | all-gather | bytes 1105920 | tf_op jit(solution)/shard_map/all_gather | solution.py:234
  56.5 6.5 %ab_product.1 = s16[320,1536]{1,0:T(8,128)(2,1)} custom-call(bf16[320,384]{1,0:T(8,128)(2,1)S(1)} %fusion.1.choose, bf16[384,1280]{1,0:T(8,128)(2,1)S(1)} %all_gather.3.amps, bf16[1536,1280]{1,0:T(8,128)(2,1)} %get-tuple-element.20.masked), custom_call_target="tpu_custom_call" | custom-call | flops 1572864000 | bytes 3932160 | tf_op jit(solution)/shard_map/ab_product/pallas_call | solution.py:237
  63.0 0.0 all-to-all-done.1
  63.0 6.9 %all-to-all-start.2 = ((s16[8,40,1536]{2,1,0:T(8,128)(2,1)}), s16[8,40,1536]{2,1,0:T(8,128)(2,1)S(1)}, u32[]{:S(2)}, u32[]{:S(2)}) async-start(s16[8,40,1536]{2,1,0:T(8,128)(2,1)} %bitcast.10), calls=%async_computation.2 | async-start | bytes 1966080 | tf_op jit(solution)/shard_map/all_to_all | solution.py:273
  69.9 5.7 %cd_product.1 = (f32[160,1280]{1,0:T(8,128)S(1)}, f32[160,1280]{1,0:T(8,128)S(1)}) custom-call(bf16[640,576]{1,0:T(8,128)(2,1)S(1)} %fusion.choose, bf16[576,768]{1,0:T(8,128)(2,1)S(1)} %bitcast.13, bf16[1536,1280]{1,0:T(8,128)(2,1)} %get-tuple-element.20.masked), custom_call_target="tpu_custom_call" | custom-call | flops 1572864000 | bytes 3932160 | tf_op jit(solution)/shard_map/cd_product/pallas_call | solution.py:255
  75.6 2.3 %collective-permute-start.1 = (f32[160,1280]{1,0:T(8,128)S(1)}, f32[160,1280]{1,0:T(8,128)S(1)}, u32[]{:S(2)}, u32[]{:S(2)}) collective-permute-start(f32[160,1280]{1,0:T(8,128)S(1)} %get-tuple-element.25), channel_id=1, source_target_pairs={{0,16},{16,0},{1,17},{17,1},{2,18},{18,2},{3,19},{19,3},{4,20},{20... | collective-permute-start | bytes 2457608 | tf_op jit(solution)/shard_map/ppermute | solution.py:22
  78.0 1.9 %collective-permute-done.1 = f32[160,1280]{1,0:T(8,128)S(1)} collective-permute-done((f32[160,1280]{1,0:T(8,128)S(1)}, f32[160,1280]{1,0:T(8,128)S(1)}, u32[]{:S(2)}, u32[]{:S(2)}) %collective-permute-start.1) | collective-permute-done | bytes 819232 | tf_op jit(solution)/shard_map/ppermute | solution.py:22
  79.9 0.1 add.228
  80.0 0.1 fusion.36
  80.1 2.8 %collective-permute-start.2 = (f32[40,1280]{1,0:T(8,128)S(1)}, f32[40,1280]{1,0:T(8,128)S(1)}, u32[]{:S(2)}, u32[]{:S(2)}) collective-permute-start(f32[40,1280]{1,0:T(8,128)S(1)} %get-tuple-element.33), channel_id=1, source_target_pairs={{0,32},{32,64},{64,96},{96,0},{1,33},{33,65},{65,97},{97,1},{2,34}... | collective-permute-start | bytes 614408 | tf_op jit(solution)/shard_map/ppermute | solution.py:22
  82.9 3.7 %collective-permute-start.5 = (f32[40,1280]{1,0:T(8,128)S(1)}, f32[40,1280]{1,0:T(8,128)S(1)}, u32[]{:S(2)}, u32[]{:S(2)}) collective-permute-start(f32[40,1280]{1,0:T(8,128)S(1)} %get-tuple-element.31), channel_id=1, source_target_pairs={{0,96},{32,0},{64,32},{96,64},{1,97},{33,1},{65,33},{97,65},{2,98}... | collective-permute-start | bytes 614408 | tf_op jit(solution)/shard_map/ppermute | solution.py:22
  86.6 2.6 %collective-permute-start.4 = (f32[40,1280]{1,0:T(8,128)S(1)}, f32[40,1280]{1,0:T(8,128)S(1)}, u32[]{:S(2)}, u32[]{:S(2)}) collective-permute-start(f32[40,1280]{1,0:T(8,128)S(1)} %get-tuple-element.32), channel_id=1, source_target_pairs={{0,64},{32,96},{64,0},{96,32},{1,65},{33,97},{65,1},{97,33},{2,66}... | collective-permute-start | bytes 614408 | tf_op jit(solution)/shard_map/ppermute | solution.py:22
  89.1 0.3 collective-permute-done.2
  89.5 8.3 %all-to-all-done.2 = s16[8,40,1536]{2,1,0:T(8,128)(2,1)S(1)} async-done(((s16[8,40,1536]{2,1,0:T(8,128)(2,1)}), s16[8,40,1536]{2,1,0:T(8,128)(2,1)S(1)}, u32[]{:S(2)}, u32[]{:S(2)}) %all-to-all-start.2) | async-done | bytes 983072 | tf_op jit(solution)/shard_map/all_to_all | solution.py:273
  97.7 0.3 copy.11
  98.0 0.0 copy-start
  98.1 0.0 copy-start.2
  98.1 0.4 multiply_reduce_fusion
  98.5 3.0 %collective-permute-start.3 = (f32[18,1536]{1,0:T(8,128)S(1)}, f32[18,1536]{1,0:T(8,128)S(1)}, u32[]{:S(2)}, u32[]{:S(2)}) collective-permute-start(f32[18,1536]{1,0:T(8,128)S(1)} %slice.63), channel_id=1, source_target_pairs={{0,1},{1,0},{2,3},{3,2},{4,5},{5,4},{6,7},{7,6},{8,9},{9,8},{10,11... | collective-permute-start | bytes 331784 | tf_op jit(solution)/shard_map/ppermute | solution.py:22
  101.6 0.0 collective-permute-done.5
  101.6 0.0 collective-permute-done.4
  101.6 0.1 fusion.2
  101.6 0.7 reshape.128
  102.4 3.4 %all-to-all-start.3 = ((f32[6,6,1280]{2,1,0:T(8,128)}), f32[6,6,1280]{2,1,0:T(8,128)S(1)}, u32[]{:S(2)}, u32[]{:S(2)}) async-start(f32[6,6,1280]{2,1,0:T(8,128)} %reshape.128), calls=%async_computation.3 | async-start | bytes 491520 | tf_op jit(solution)/shard_map/all_to_all | solution.py:283
  105.8 9.6 %collective-permute-done.3 = f32[18,1536]{1,0:T(8,128)S(1)} collective-permute-done((f32[18,1536]{1,0:T(8,128)S(1)}, f32[18,1536]{1,0:T(8,128)S(1)}, u32[]{:S(2)}, u32[]{:S(2)}) %collective-permute-start.3) | collective-permute-done | bytes 110624 | tf_op jit(solution)/shard_map/ppermute | solution.py:22
  115.4 0.0 copy-done
  115.4 0.7 fusion.3
  116.1 5.3 %all-to-all-done.3 = f32[6,6,1280]{2,1,0:T(8,128)S(1)} async-done(((f32[6,6,1280]{2,1,0:T(8,128)}), f32[6,6,1280]{2,1,0:T(8,128)S(1)}, u32[]{:S(2)}, u32[]{:S(2)}) %all-to-all-start.3) | async-done | bytes 184352 | tf_op jit(solution)/shard_map/all_to_all | solution.py:283
  121.5 0.0 copy-done.2
  121.5 0.6 div.78
  (7 shorter events, 0.2 us)
Async XLA Ops:
  0.6 29.8 %collective-permute-start = (bf16[18,1536]{1,0:T(8,128)(2,1)}, bf16[18,1536]{1,0:T(8,128)(2,1)S(1)}, u32[]{:S(2)}, u32[]{:S(2)}) collective-permute-start(bf16[18,1536]{1,0:T(8,128)(2,1)} %param.14), channel_id=1, source_target_pairs={{0,1},{1,0},{2,3},{3,2},{4,5},{5,4},{6,7},{7,6},{8,9},{9,8},{10,11... | collective-permute-start | bytes 165896 | tf_op jit(solution)/shard_map/ppermute | solution.py:22
  17.7 14.0 %all-to-all-start = ((bf16[6,8,1280]{2,1,0:T(8,128)(2,1)}), bf16[6,8,1280]{2,1,0:T(8,128)(2,1)S(1)}, u32[]{:S(2)}, u32[]{:S(2)}) async-start(bf16[6,8,1280]{2,1,0:T(8,128)(2,1)} %pad.4), calls=%async_computation | async-start | bytes 245760 | tf_op jit(solution)/shard_map/all_to_all | solution.py:192
  25.0 5.4 %copy-start.1 = (bf16[18,1536]{1,0:T(8,128)(2,1)S(1)}, bf16[18,1536]{1,0:T(8,128)(2,1)}, u32[]{:S(2)}) copy-start(bf16[18,1536]{1,0:T(8,128)(2,1)} %param.14) | copy-start | bytes 165892
  32.7 30.3 %all-to-all-start.1 = ((bf16[8,72,768]{2,1,0:T(8,128)(2,1)}), bf16[8,72,768]{2,1,0:T(8,128)(2,1)S(1)}, u32[]{:S(2)}, u32[]{:S(2)}) async-start(bf16[8,72,768]{2,1,0:T(8,128)(2,1)} %broadcast_in_dim.8), calls=%async_computation.1 | async-start | bytes 1769472 | tf_op jit(solution)/shard_map/all_to_all | solution.py:235
  63.0 34.7 %all-to-all-start.2 = ((s16[8,40,1536]{2,1,0:T(8,128)(2,1)}), s16[8,40,1536]{2,1,0:T(8,128)(2,1)S(1)}, u32[]{:S(2)}, u32[]{:S(2)}) async-start(s16[8,40,1536]{2,1,0:T(8,128)(2,1)} %bitcast.10), calls=%async_computation.2 | async-start | bytes 1966080 | tf_op jit(solution)/shard_map/all_to_all | solution.py:273
  75.6 4.3 %collective-permute-start.1 = (f32[160,1280]{1,0:T(8,128)S(1)}, f32[160,1280]{1,0:T(8,128)S(1)}, u32[]{:S(2)}, u32[]{:S(2)}) collective-permute-start(f32[160,1280]{1,0:T(8,128)S(1)} %get-tuple-element.25), channel_id=1, source_target_pairs={{0,16},{16,0},{1,17},{17,1},{2,18},{18,2},{3,19},{19,3},{4,20},{20... | collective-permute-start | bytes 2457608 | tf_op jit(solution)/shard_map/ppermute | solution.py:22
  80.1 9.4 %collective-permute-start.2 = (f32[40,1280]{1,0:T(8,128)S(1)}, f32[40,1280]{1,0:T(8,128)S(1)}, u32[]{:S(2)}, u32[]{:S(2)}) collective-permute-start(f32[40,1280]{1,0:T(8,128)S(1)} %get-tuple-element.33), channel_id=1, source_target_pairs={{0,32},{32,64},{64,96},{96,0},{1,33},{33,65},{65,97},{97,1},{2,34}... | collective-permute-start | bytes 614408 | tf_op jit(solution)/shard_map/ppermute | solution.py:22
  82.9 18.7 %collective-permute-start.5 = (f32[40,1280]{1,0:T(8,128)S(1)}, f32[40,1280]{1,0:T(8,128)S(1)}, u32[]{:S(2)}, u32[]{:S(2)}) collective-permute-start(f32[40,1280]{1,0:T(8,128)S(1)} %get-tuple-element.31), channel_id=1, source_target_pairs={{0,96},{32,0},{64,32},{96,64},{1,97},{33,1},{65,33},{97,65},{2,98}... | collective-permute-start | bytes 614408 | tf_op jit(solution)/shard_map/ppermute | solution.py:22
  86.6 15.0 %collective-permute-start.4 = (f32[40,1280]{1,0:T(8,128)S(1)}, f32[40,1280]{1,0:T(8,128)S(1)}, u32[]{:S(2)}, u32[]{:S(2)}) collective-permute-start(f32[40,1280]{1,0:T(8,128)S(1)} %get-tuple-element.32), channel_id=1, source_target_pairs={{0,64},{32,96},{64,0},{96,32},{1,65},{33,97},{65,1},{97,33},{2,66}... | collective-permute-start | bytes 614408 | tf_op jit(solution)/shard_map/ppermute | solution.py:22
  98.0 17.4 %copy-start = (f32[18,1536]{1,0:T(8,128)S(1)}, f32[18,1536]{1,0:T(8,128)}, u32[]{:S(2)}) copy-start(f32[18,1536]{1,0:T(8,128)} %get-tuple-element.27) | copy-start | bytes 331780
  98.1 23.4 %copy-start.2 = (f32[6,1280]{1,0:T(8,128)S(1)}, f32[6,1280]{1,0:T(8,128)}, u32[]{:S(2)}) copy-start(f32[6,1280]{1,0:T(8,128)} %get-tuple-element.29) | copy-start | bytes 92164
  98.5 16.9 %collective-permute-start.3 = (f32[18,1536]{1,0:T(8,128)S(1)}, f32[18,1536]{1,0:T(8,128)S(1)}, u32[]{:S(2)}, u32[]{:S(2)}) collective-permute-start(f32[18,1536]{1,0:T(8,128)S(1)} %slice.63), channel_id=1, source_target_pairs={{0,1},{1,0},{2,3},{3,2},{4,5},{5,4},{6,7},{7,6},{8,9},{9,8},{10,11... | collective-permute-start | bytes 331784 | tf_op jit(solution)/shard_map/ppermute | solution.py:22
  102.4 19.1 %all-to-all-start.3 = ((f32[6,6,1280]{2,1,0:T(8,128)}), f32[6,6,1280]{2,1,0:T(8,128)S(1)}, u32[]{:S(2)}, u32[]{:S(2)}) async-start(f32[6,6,1280]{2,1,0:T(8,128)} %reshape.128), calls=%async_computation.3 | async-start | bytes 491520 | tf_op jit(solution)/shard_map/all_to_all | solution.py:283

commit v8 on v7

--- a/solution.py
+++ b/solution.py
@@ -230,7 +230,7 @@
     )
 
     choose_ab, choose_cd = ab_chooser(), cd_chooser()
-    own, masked, both, choose_ab, choose_cd = lax.optimization_barrier((own, masked, both, choose_ab, choose_cd))
+    own, masked, both, choose_ab = lax.optimization_barrier((own, masked, both, choose_ab))
     all_cd = lax.all_gather(own, ("x", "core"), axis=0, tiled=True)
     all_ab = lax.all_to_all(both, "y", 0, 0).reshape(2 * ny * y_rows, side)
 

time: 123 us -> 123 us (level)
    ppermute x6, waiting for transfers between devices: 11.9 us -> 9.28 us  [send(): return lax.ppermute(block, axis, pairs)]
    all_to_all x1, waiting for transfers between devices: 5.35 us -> 7.48 us  [local(): ladder_cd = jnp.sum(lax.all_to_all(total, 'zl', 0, 0), axis=0)]
where the time goes in v8:
time: 123 us
  starting transfers between devices  54.2 us (44%)
  waiting for transfers between devices  26.3 us (21%)
  Pallas kernels  17.6 us (14%)
  blocking collectives  17 us (14%)
  local copies, waits for them, and re-layouts  4.11 us (3%)
  other arithmetic  2.47 us (2%)
    ppermute x6, starting transfers between devices, send(): return lax.ppermute(block, axis, pairs)  30.1 us
    all_gather x1, blocking collectives, local(): all_cd = lax.all_gather(own, ('x', 'core'), axis=0, tiled=True)  17 us
    ppermute x6, waiting for transfers between devices, send(): return lax.ppermute(block, axis, pairs)  9.28 us
    all_to_all x1, waiting for transfers between devices, local(): coded = lax.all_to_all(coded.reshape(ny, y_pad, rows_dev), 'y', 0, 0)  8.04 us
    all_to_all x1, waiting for transfers between devices, local(): ladder_cd = jnp.sum(lax.all_to_all(total, 'zl', 0, 0), axis=0)  7.48 us
    all_to_all x1, starting transfers between devices, local(): coded = lax.all_to_all(coded.reshape(ny, y_pad, rows_dev), 'y', 0, 0)  6.94 us
    all_to_all x1, starting transfers between devices, local(): all_ab = lax.all_to_all(both, 'y', 0, 0).reshape(2 * ny * y_rows, side)  6.82 us
    pallas_call x1, Pallas kernels, local(): pl.pallas_call(functools.partial(ab_kernel, ny, y_rows), in_specs=[vmem,...  6.45 us
  transfers between devices with their start and end apart: 10, of which 6 were waited for; matrix products, arithmetic and copies ran while one was open for 4% of the time, Pallas kernels for 14%

profile of v8, /device:TPU:1, one launch (start us, length us, event | category | flops | bytes accessed | tf_op | source)
XLA Modules:
  0.0 122.5 jit_solution(11798839811649295768)
XLA Ops:
  0.6 15.7 %collective-permute-start = (bf16[18,1536]{1,0:T(8,128)(2,1)}, bf16[18,1536]{1,0:T(8,128)(2,1)S(1)}, u32[]{:S(2)}, u32[]{:S(2)}) collective-permute-start(bf16[18,1536]{1,0:T(8,128)(2,1)} %param.14), channel_id=1, source_target_pairs={{0,1},{1,0},{2,3},{3,2},{4,5},{5,4},{6,7},{7,6},{8,9},{9,8},{10,11... | collective-permute-start | bytes 165896 | tf_op jit(solution)/shard_map/ppermute | solution.py:22
  16.3 0.7 broadcast_in_dim.7
  17.1 0.7 pad.4
  17.7 6.1 %all-to-all-start = ((bf16[6,8,1280]{2,1,0:T(8,128)(2,1)}), bf16[6,8,1280]{2,1,0:T(8,128)(2,1)S(1)}, u32[]{:S(2)}, u32[]{:S(2)}) async-start(bf16[6,8,1280]{2,1,0:T(8,128)(2,1)} %pad.4), calls=%async_computation | async-start | bytes 245760 | tf_op jit(solution)/shard_map/all_to_all | solution.py:192
  23.8 0.1 fusion.14
  23.9 0.1 fusion.1.choose
  24.1 0.6 stack.27.place
  24.7 0.0 copy-start.1
  24.7 5.4 %masked.1 = (bf16[1536,1280]{1,0:T(8,128)(2,1)}, f32[18,1536]{1,0:T(8,128)}, f32[6,1280]{1,0:T(8,128)}) custom-call(s32[6]{0:T(128)} %stack.27.place, s32[6,5]{1,0:T(8,128)} %tile_mask.1, s32[1000]{0:T(1024)} %irrep.1, f32[1000]{0:T(1024)} %energy.1, s32[2,288]{1,0:T(2,128)} %pairs.1, f32[100]{0:T(128)} %occ.1, s32[1,1000]{1,0:T(1,128)} %bitcast.15, ...), custom_call_target="tpu_custom_call" | custom-call | flops 7864320 | bytes 7864320 | tf_op jit(solution)/shard_map/masked/pallas_call | solution.py:201
  30.1 0.0 collective-permute-done
  30.1 0.0 copy-done.1
  30.2 1.5 %all-to-all-done = bf16[6,8,1280]{2,1,0:T(8,128)(2,1)S(1)} async-done(((bf16[6,8,1280]{2,1,0:T(8,128)(2,1)}), bf16[6,8,1280]{2,1,0:T(8,128)(2,1)S(1)}, u32[]{:S(2)}, u32[]{:S(2)}) %all-to-all-start) | async-done | bytes 122912 | tf_op jit(solution)/shard_map/all_to_all | solution.py:192
  31.7 1.0 broadcast_in_dim.8
  32.7 6.8 %all-to-all-start.1 = ((bf16[8,72,768]{2,1,0:T(8,128)(2,1)}), bf16[8,72,768]{2,1,0:T(8,128)(2,1)S(1)}, u32[]{:S(2)}, u32[]{:S(2)}) async-start(bf16[8,72,768]{2,1,0:T(8,128)(2,1)} %broadcast_in_dim.8), calls=%async_computation.1 | async-start | bytes 1769472 | tf_op jit(solution)/shard_map/all_to_all | solution.py:235
  39.6 0.1 pad_add_fusion
  39.7 17.0 %all_gather.3.amps = bf16[384,1280]{1,0:T(8,128)(2,1)S(1)} all-gather(bf16[48,1280]{1,0:T(8,128)(2,1)S(1)} %bitcast.14), channel_id=1, replica_groups=mesh['zl'=6,'x'=4,'core'=2,'y'=8,'zh'=2] {'x','core'}, dimensions={0}, use_global_device_ids=true | all-gather | bytes 1105920 | tf_op jit(solution)/shard_map/all_gather | solution.py:234
  56.6 6.4 %ab_product.1 = s16[320,1536]{1,0:T(8,128)(2,1)} custom-call(bf16[320,384]{1,0:T(8,128)(2,1)S(1)} %fusion.1.choose, bf16[384,1280]{1,0:T(8,128)(2,1)S(1)} %all_gather.3.amps, bf16[1536,1280]{1,0:T(8,128)(2,1)} %get-tuple-element.19.masked), custom_call_target="tpu_custom_call" | custom-call | flops 1572864000 | bytes 3932160 | tf_op jit(solution)/shard_map/ab_product/pallas_call | solution.py:237
  63.1 0.0 all-to-all-done.1
  63.1 6.9 %all-to-all-start.2 = ((s16[8,40,1536]{2,1,0:T(8,128)(2,1)}), s16[8,40,1536]{2,1,0:T(8,128)(2,1)S(1)}, u32[]{:S(2)}, u32[]{:S(2)}) async-start(s16[8,40,1536]{2,1,0:T(8,128)(2,1)} %bitcast.10), calls=%async_computation.2 | async-start | bytes 1966080 | tf_op jit(solution)/shard_map/all_to_all | solution.py:273
  70.0 0.2 fusion.choose
  70.3 5.7 %cd_product.1 = (f32[160,1280]{1,0:T(8,128)S(1)}, f32[160,1280]{1,0:T(8,128)S(1)}) custom-call(bf16[640,576]{1,0:T(8,128)(2,1)S(1)} %fusion.choose, bf16[576,768]{1,0:T(8,128)(2,1)S(1)} %bitcast.13, bf16[1536,1280]{1,0:T(8,128)(2,1)} %get-tuple-element.19.masked), custom_call_target="tpu_custom_call" | custom-call | flops 1572864000 | bytes 3932160 | tf_op jit(solution)/shard_map/cd_product/pallas_call | solution.py:255
  76.0 2.4 %collective-permute-start.1 = (f32[160,1280]{1,0:T(8,128)S(1)}, f32[160,1280]{1,0:T(8,128)S(1)}, u32[]{:S(2)}, u32[]{:S(2)}) collective-permute-start(f32[160,1280]{1,0:T(8,128)S(1)} %get-tuple-element.23), channel_id=1, source_target_pairs={{0,16},{16,0},{1,17},{17,1},{2,18},{18,2},{3,19},{19,3},{4,20},{20... | collective-permute-start | bytes 2457608 | tf_op jit(solution)/shard_map/ppermute | solution.py:22
  78.3 1.9 %collective-permute-done.1 = f32[160,1280]{1,0:T(8,128)S(1)} collective-permute-done((f32[160,1280]{1,0:T(8,128)S(1)}, f32[160,1280]{1,0:T(8,128)S(1)}, u32[]{:S(2)}, u32[]{:S(2)}) %collective-permute-start.1) | collective-permute-done | bytes 819232 | tf_op jit(solution)/shard_map/ppermute | solution.py:22
  80.3 0.1 add.228
  80.3 0.1 fusion.36
  80.4 2.8 %collective-permute-start.2 = (f32[40,1280]{1,0:T(8,128)S(1)}, f32[40,1280]{1,0:T(8,128)S(1)}, u32[]{:S(2)}, u32[]{:S(2)}) collective-permute-start(f32[40,1280]{1,0:T(8,128)S(1)} %get-tuple-element.31), channel_id=1, source_target_pairs={{0,32},{32,64},{64,96},{96,0},{1,33},{33,65},{65,97},{97,1},{2,34}... | collective-permute-start | bytes 614408 | tf_op jit(solution)/shard_map/ppermute | solution.py:22
  83.2 3.7 %collective-permute-start.5 = (f32[40,1280]{1,0:T(8,128)S(1)}, f32[40,1280]{1,0:T(8,128)S(1)}, u32[]{:S(2)}, u32[]{:S(2)}) collective-permute-start(f32[40,1280]{1,0:T(8,128)S(1)} %get-tuple-element.29), channel_id=1, source_target_pairs={{0,96},{32,0},{64,32},{96,64},{1,97},{33,1},{65,33},{97,65},{2,98}... | collective-permute-start | bytes 614408 | tf_op jit(solution)/shard_map/ppermute | solution.py:22
  86.9 2.6 %collective-permute-start.4 = (f32[40,1280]{1,0:T(8,128)S(1)}, f32[40,1280]{1,0:T(8,128)S(1)}, u32[]{:S(2)}, u32[]{:S(2)}) collective-permute-start(f32[40,1280]{1,0:T(8,128)S(1)} %get-tuple-element.30), channel_id=1, source_target_pairs={{0,64},{32,96},{64,0},{96,32},{1,65},{33,97},{65,1},{97,33},{2,66}... | collective-permute-start | bytes 614408 | tf_op jit(solution)/shard_map/ppermute | solution.py:22
  89.5 0.3 collective-permute-done.2
  89.8 8.0 %all-to-all-done.2 = s16[8,40,1536]{2,1,0:T(8,128)(2,1)S(1)} async-done(((s16[8,40,1536]{2,1,0:T(8,128)(2,1)}), s16[8,40,1536]{2,1,0:T(8,128)(2,1)S(1)}, u32[]{:S(2)}, u32[]{:S(2)}) %all-to-all-start.2) | async-done | bytes 983072 | tf_op jit(solution)/shard_map/all_to_all | solution.py:273
  97.8 0.3 copy.11
  98.1 0.0 copy-start
  98.2 0.0 copy-start.2
  98.2 0.4 multiply_reduce_fusion
  98.6 3.1 %collective-permute-start.3 = (f32[18,1536]{1,0:T(8,128)S(1)}, f32[18,1536]{1,0:T(8,128)S(1)}, u32[]{:S(2)}, u32[]{:S(2)}) collective-permute-start(f32[18,1536]{1,0:T(8,128)S(1)} %slice.63), channel_id=1, source_target_pairs={{0,1},{1,0},{2,3},{3,2},{4,5},{5,4},{6,7},{7,6},{8,9},{9,8},{10,11... | collective-permute-start | bytes 331784 | tf_op jit(solution)/shard_map/ppermute | solution.py:22
  101.7 0.0 collective-permute-done.5
  101.7 0.0 collective-permute-done.4
  101.7 0.1 fusion.2
  101.8 0.7 reshape.128
  102.5 4.2 %all-to-all-start.3 = ((f32[6,6,1280]{2,1,0:T(8,128)}), f32[6,6,1280]{2,1,0:T(8,128)S(1)}, u32[]{:S(2)}, u32[]{:S(2)}) async-start(f32[6,6,1280]{2,1,0:T(8,128)} %reshape.128), calls=%async_computation.3 | async-start | bytes 491520 | tf_op jit(solution)/shard_map/all_to_all | solution.py:283
  106.7 7.0 %collective-permute-done.3 = f32[18,1536]{1,0:T(8,128)S(1)} collective-permute-done((f32[18,1536]{1,0:T(8,128)S(1)}, f32[18,1536]{1,0:T(8,128)S(1)}, u32[]{:S(2)}, u32[]{:S(2)}) %collective-permute-start.3) | collective-permute-done | bytes 110624 | tf_op jit(solution)/shard_map/ppermute | solution.py:22
  113.7 0.0 copy-done
  113.7 0.7 fusion.3
  114.4 7.5 %all-to-all-done.3 = f32[6,6,1280]{2,1,0:T(8,128)S(1)} async-done(((f32[6,6,1280]{2,1,0:T(8,128)}), f32[6,6,1280]{2,1,0:T(8,128)S(1)}, u32[]{:S(2)}, u32[]{:S(2)}) %all-to-all-start.3) | async-done | bytes 184352 | tf_op jit(solution)/shard_map/all_to_all | solution.py:283
  121.9 0.0 copy-done.2
  121.9 0.6 div.78
  (7 shorter events, 0.2 us)
Async XLA Ops:
  0.6 29.5 %collective-permute-start = (bf16[18,1536]{1,0:T(8,128)(2,1)}, bf16[18,1536]{1,0:T(8,128)(2,1)S(1)}, u32[]{:S(2)}, u32[]{:S(2)}) collective-permute-start(bf16[18,1536]{1,0:T(8,128)(2,1)} %param.14), channel_id=1, source_target_pairs={{0,1},{1,0},{2,3},{3,2},{4,5},{5,4},{6,7},{7,6},{8,9},{9,8},{10,11... | collective-permute-start | bytes 165896 | tf_op jit(solution)/shard_map/ppermute | solution.py:22
  17.7 14.0 %all-to-all-start = ((bf16[6,8,1280]{2,1,0:T(8,128)(2,1)}), bf16[6,8,1280]{2,1,0:T(8,128)(2,1)S(1)}, u32[]{:S(2)}, u32[]{:S(2)}) async-start(bf16[6,8,1280]{2,1,0:T(8,128)(2,1)} %pad.4), calls=%async_computation | async-start | bytes 245760 | tf_op jit(solution)/shard_map/all_to_all | solution.py:192
  24.7 5.4 %copy-start.1 = (bf16[18,1536]{1,0:T(8,128)(2,1)S(1)}, bf16[18,1536]{1,0:T(8,128)(2,1)}, u32[]{:S(2)}) copy-start(bf16[18,1536]{1,0:T(8,128)(2,1)} %param.14) | copy-start | bytes 165892
  32.7 30.4 %all-to-all-start.1 = ((bf16[8,72,768]{2,1,0:T(8,128)(2,1)}), bf16[8,72,768]{2,1,0:T(8,128)(2,1)S(1)}, u32[]{:S(2)}, u32[]{:S(2)}) async-start(bf16[8,72,768]{2,1,0:T(8,128)(2,1)} %broadcast_in_dim.8), calls=%async_computation.1 | async-start | bytes 1769472 | tf_op jit(solution)/shard_map/all_to_all | solution.py:235
  63.1 34.7 %all-to-all-start.2 = ((s16[8,40,1536]{2,1,0:T(8,128)(2,1)}), s16[8,40,1536]{2,1,0:T(8,128)(2,1)S(1)}, u32[]{:S(2)}, u32[]{:S(2)}) async-start(s16[8,40,1536]{2,1,0:T(8,128)(2,1)} %bitcast.10), calls=%async_computation.2 | async-start | bytes 1966080 | tf_op jit(solution)/shard_map/all_to_all | solution.py:273
  76.0 4.3 %collective-permute-start.1 = (f32[160,1280]{1,0:T(8,128)S(1)}, f32[160,1280]{1,0:T(8,128)S(1)}, u32[]{:S(2)}, u32[]{:S(2)}) collective-permute-start(f32[160,1280]{1,0:T(8,128)S(1)} %get-tuple-element.23), channel_id=1, source_target_pairs={{0,16},{16,0},{1,17},{17,1},{2,18},{18,2},{3,19},{19,3},{4,20},{20... | collective-permute-start | bytes 2457608 | tf_op jit(solution)/shard_map/ppermute | solution.py:22
  80.4 9.4 %collective-permute-start.2 = (f32[40,1280]{1,0:T(8,128)S(1)}, f32[40,1280]{1,0:T(8,128)S(1)}, u32[]{:S(2)}, u32[]{:S(2)}) collective-permute-start(f32[40,1280]{1,0:T(8,128)S(1)} %get-tuple-element.31), channel_id=1, source_target_pairs={{0,32},{32,64},{64,96},{96,0},{1,33},{33,65},{65,97},{97,1},{2,34}... | collective-permute-start | bytes 614408 | tf_op jit(solution)/shard_map/ppermute | solution.py:22
  83.2 18.5 %collective-permute-start.5 = (f32[40,1280]{1,0:T(8,128)S(1)}, f32[40,1280]{1,0:T(8,128)S(1)}, u32[]{:S(2)}, u32[]{:S(2)}) collective-permute-start(f32[40,1280]{1,0:T(8,128)S(1)} %get-tuple-element.29), channel_id=1, source_target_pairs={{0,96},{32,0},{64,32},{96,64},{1,97},{33,1},{65,33},{97,65},{2,98}... | collective-permute-start | bytes 614408 | tf_op jit(solution)/shard_map/ppermute | solution.py:22
  86.9 14.8 %collective-permute-start.4 = (f32[40,1280]{1,0:T(8,128)S(1)}, f32[40,1280]{1,0:T(8,128)S(1)}, u32[]{:S(2)}, u32[]{:S(2)}) collective-permute-start(f32[40,1280]{1,0:T(8,128)S(1)} %get-tuple-element.30), channel_id=1, source_target_pairs={{0,64},{32,96},{64,0},{96,32},{1,65},{33,97},{65,1},{97,33},{2,66}... | collective-permute-start | bytes 614408 | tf_op jit(solution)/shard_map/ppermute | solution.py:22
  98.1 15.5 %copy-start = (f32[18,1536]{1,0:T(8,128)S(1)}, f32[18,1536]{1,0:T(8,128)}, u32[]{:S(2)}) copy-start(f32[18,1536]{1,0:T(8,128)} %get-tuple-element.25) | copy-start | bytes 331780
  98.2 23.7 %copy-start.2 = (f32[6,1280]{1,0:T(8,128)S(1)}, f32[6,1280]{1,0:T(8,128)}, u32[]{:S(2)}) copy-start(f32[6,1280]{1,0:T(8,128)} %get-tuple-element.27) | copy-start | bytes 92164
  98.6 15.0 %collective-permute-start.3 = (f32[18,1536]{1,0:T(8,128)S(1)}, f32[18,1536]{1,0:T(8,128)S(1)}, u32[]{:S(2)}, u32[]{:S(2)}) collective-permute-start(f32[18,1536]{1,0:T(8,128)S(1)} %slice.63), channel_id=1, source_target_pairs={{0,1},{1,0},{2,3},{3,2},{4,5},{5,4},{6,7},{7,6},{8,9},{9,8},{10,11... | collective-permute-start | bytes 331784 | tf_op jit(solution)/shard_map/ppermute | solution.py:22
  102.5 19.4 %all-to-all-start.3 = ((f32[6,6,1280]{2,1,0:T(8,128)}), f32[6,6,1280]{2,1,0:T(8,128)S(1)}, u32[]{:S(2)}, u32[]{:S(2)}) async-start(f32[6,6,1280]{2,1,0:T(8,128)} %reshape.128), calls=%async_computation.3 | async-start | bytes 491520 | tf_op jit(solution)/shard_map/all_to_all | solution.py:283
